TPU v7x, 32 devices: a whole 2x2x4 slice. The times are simulated.
32 devices in a mesh: rep: 4 (over y, x), shard: 8 (over z, core).
Axes of the slice: x: 2, y: 2, z: 4, core: 2. Of those that a mesh axis runs over, the one named last changes fastest.
Arguments:
- tokens: bfloat16 [8192, 2048], P(('rep', 'shard')), may hold values from -6 to 6
- document_ends: int32 [32, 4], P(('rep', 'shard')), may hold values from 0 to 256, as said below
- projector: bfloat16 [2048, 6144], P('shard'), may hold values from -0.125 to 0.125
- projbias: bfloat16 [6144], P('shard'), may hold values from -3 to 3
- combiner: bfloat16 [2048, 2048], P('shard'), may hold values from -0.5 to 0.5
- combbias: bfloat16 [2048], P('shard'), may hold values from -2 to 2
- expander: bfloat16 [2048, 8192], P('shard'), may hold values from -0.125 to 0.125
- expbias: bfloat16 [8192], P('shard'), may hold values from -3 to 3
- contractor: bfloat16 [8192, 2048], P('shard'), may hold values from -0.0625 to 0.0625
- contbias: bfloat16 [2048], P('shard'), may hold values from -2 to 2
- attendgain: bfloat16 [2048], P('shard'), may hold values from 0.099609375 to 1.8984375
- attendshift: bfloat16 [2048], P('shard'), may hold values from -2 to 2
- feedgain: bfloat16 [2048], P('shard'), may hold values from 0.099609375 to 1.8984375
- feedshift: bfloat16 [2048], P('shard'), may hold values from -2 to 2
- cotangent: bfloat16 [8192, 2048], P(('rep', 'shard')), may hold values from -6 to 6
Outputs:
- block_output: bfloat16 [8192, 2048], P(('rep', 'shard'))
- input_gradient: bfloat16 [8192, 2048], P(('rep', 'shard'))
- projector_gradient: float32 [2048, 6144], P('shard')
- projbias_gradient: float32 [6144], P('shard')
- combiner_gradient: float32 [2048, 2048], P('shard')
- combbias_gradient: float32 [2048], P('shard')
- expander_gradient: float32 [2048, 8192], P('shard')
- expbias_gradient: float32 [8192], P('shard')
- contractor_gradient: float32 [8192, 2048], P('shard')
- contbias_gradient: float32 [2048], P('shard')
- attendgain_gradient: float32 [2048], P('shard')
- attendshift_gradient: float32 [2048], P('shard')
- feedgain_gradient: float32 [2048], P('shard')
- feedshift_gradient: float32 [2048], P('shard')
Inputs may be any that keep to these rules, and one draw needn't show every extreme that they name: `document_ends`: each row never falls; a device's documents run from slot 0 to its last entry one after another, and slots from the last entry on are padding. The last entry is 128 or more, and 256 on some device.
All inputs are finite; a program needn't handle non-finite values.
Results may differ from a plain program's by a relative error of at most 0.015.
Values may be sent and summed in bfloat16 or wider, within the bound.
A program may use at most 512 MiB of HBM per device.

v0:
```python
from functools import partial
import math

import jax
import jax.numpy as jnp
from jax import lax
from jax.sharding import PartitionSpec as P

H = 8
ROT = 64


epsilon = 1e-05
masked_value = -1e30


def normalize(values):
    centre = jnp.mean(values, axis=1, keepdims=True)
    centred = values - centre
    spread = jnp.mean(centred * centred, axis=1, keepdims=True)
    inverse = lax.rsqrt(spread + epsilon)
    return (centred * inverse, inverse)


def layout(ends, count):
    index = jnp.arange(count, dtype=jnp.int32)
    passed = index[:, None] >= ends[None, :]
    document = jnp.sum(passed.astype(jnp.int32), axis=1)
    begin = jnp.max(jnp.where(passed, ends[None, :], 0), axis=1)
    position = (index - begin).astype(jnp.float32)
    allowed = (document[:, None] == document[None, :]) & (index[None, :] <= index[:, None])
    return (position, allowed, index < ends[-1])


def rotary_tables(position, rotary):
    half = rotary // 2
    freqs = jnp.exp(-jnp.arange(half, dtype=jnp.float32) * (2.0 / rotary) * math.log(10000.0))
    angles = position[:, None] * freqs[None, :]
    angles = jnp.concatenate([angles, angles], axis=1)
    return (jnp.cos(angles)[:, None, :], jnp.sin(angles)[:, None, :])


def rotate(values, cosine, sine, rotary):
    half = rotary // 2
    front = values[..., :rotary]
    turned = jnp.concatenate([-front[..., half:], front[..., :half]], axis=-1)
    return jnp.concatenate([front * cosine + turned * sine, values[..., rotary:]], axis=-1)


def unrotate(grads, cosine, sine, rotary):
    half = rotary // 2
    front = grads[..., :rotary]
    scaled = front * sine
    backward = jnp.concatenate([scaled[..., half:], -scaled[..., :half]], axis=-1)
    return jnp.concatenate([front * cosine + backward, grads[..., rotary:]], axis=-1)


def masked_scores(query_low, keys_low, allowed, factor):
    scores = (
        jnp.einsum("qhd,khd->hqk", query_low, keys_low, preferred_element_type=jnp.float32) * factor
    )
    return jnp.where(allowed[None], scores, masked_value)


def right_trans(left, right):
    return lax.dot_general(
        left, right, (((1,), (1,)), ((), ())), preferred_element_type=jnp.float32
    )


def left_trans(left, right):
    return lax.dot_general(
        left, right, (((0,), (0,)), ((), ())), preferred_element_type=jnp.float32
    )


def weight_sums(left, right):
    piece = lax.slice_in_dim(
        left, 0, left.shape[1] // lax.axis_size("shard") * lax.axis_size("shard"), axis=1
    )
    return lax.psum_scatter(
        left_trans(piece, right).astype(jnp.bfloat16), "shard", scatter_dimension=0, tiled=True
    ).astype(jnp.float32)


def local(
    tokens,
    document_ends,
    projector,
    projbias,
    combiner,
    combbias,
    expander,
    expbias,
    contractor,
    contbias,
    attendgain,
    attendshift,
    feedgain,
    feedshift,
    cotangent,
):
    count, width = tokens.shape
    headsize = width // H
    factor = 1.0 / math.sqrt(headsize)
    position, allowed, live = layout(document_ends[0], count)
    cosine, sine = rotary_tables(position, ROT)
    (
        full_projector,
        full_combiner,
        full_projbias,
        full_combbias,
        gain_attend,
        shift_attend,
        gain_feed,
        shift_feed,
    ) = (
        lax.all_gather(projector, "shard", axis=0, tiled=True),
        lax.all_gather(combiner, "shard", axis=0, tiled=True),
        lax.all_gather(projbias, "shard", axis=0, tiled=True),
        lax.all_gather(combbias, "shard", axis=0, tiled=True),
        lax.all_gather(attendgain, "shard", axis=0, tiled=True),
        lax.all_gather(attendshift, "shard", axis=0, tiled=True),
        lax.all_gather(feedgain, "shard", axis=0, tiled=True),
        lax.all_gather(feedshift, "shard", axis=0, tiled=True),
    )
    floated = tokens.astype(jnp.float32)
    normed, inverse = normalize(floated)
    first_input = (normed * gain_attend + shift_attend).astype(jnp.bfloat16)
    second_input = (normed * gain_feed + shift_feed).astype(jnp.bfloat16)
    mixed = jnp.dot(first_input, full_projector, preferred_element_type=jnp.float32) + full_projbias
    query_low = rotate(mixed[:, :width].reshape(count, H, headsize), cosine, sine, ROT).astype(
        jnp.bfloat16
    )
    keys_low = rotate(
        mixed[:, width : 2 * width].reshape(count, H, headsize), cosine, sine, ROT
    ).astype(jnp.bfloat16)
    values_low = mixed[:, 2 * width :].reshape(count, H, headsize).astype(jnp.bfloat16)
    scores = masked_scores(query_low, keys_low, allowed, factor)
    peak = jnp.max(scores, axis=2, keepdims=True)
    raised = jnp.exp(scores - peak)
    total = jnp.sum(raised, axis=2, keepdims=True)
    probs_low = (raised / total).astype(jnp.bfloat16)
    logsum = peak + jnp.log(total)
    context = jnp.einsum("hqk,khd->qhd", probs_low, values_low, preferred_element_type=jnp.float32)
    context = context.reshape(count, width).astype(jnp.bfloat16)
    attended = jnp.dot(context, full_combiner, preferred_element_type=jnp.float32) + full_combbias
    full_expander, full_contractor, full_expbias, full_contbias = (
        lax.all_gather(expander, "shard", axis=0, tiled=True),
        lax.all_gather(contractor, "shard", axis=0, tiled=True),
        lax.all_gather(expbias, "shard", axis=0, tiled=True),
        lax.all_gather(contbias, "shard", axis=0, tiled=True),
    )
    hidden = jnp.dot(second_input, full_expander, preferred_element_type=jnp.float32) + full_expbias
    activated, gelu_back = jax.vjp(partial(jax.nn.gelu, approximate=False), hidden)
    active_low = activated.astype(jnp.bfloat16)
    feedout = (
        jnp.dot(active_low, full_contractor, preferred_element_type=jnp.float32) + full_contbias
    )
    block_output = (floated + jnp.where(live[:, None], attended + feedout, 0.0)).astype(
        jnp.bfloat16
    )
    (
        back_projector,
        back_combiner,
        back_expander,
        back_contractor,
        back_gain_attend,
        back_gain_feed,
    ) = (
        lax.all_gather(projector, "shard", axis=0, tiled=True),
        lax.all_gather(combiner, "shard", axis=0, tiled=True),
        lax.all_gather(expander, "shard", axis=0, tiled=True),
        lax.all_gather(contractor, "shard", axis=0, tiled=True),
        lax.all_gather(attendgain, "shard", axis=0, tiled=True),
        lax.all_gather(feedgain, "shard", axis=0, tiled=True),
    )
    upstream = jnp.where(live[:, None], cotangent, jnp.zeros_like(cotangent))
    contractor_part = weight_sums(active_low, upstream)
    combiner_part = weight_sums(context, upstream)
    output_bias = jnp.sum(upstream, axis=0, dtype=jnp.float32)
    d_active = right_trans(upstream, back_contractor)
    d_hidden = gelu_back(d_active)[0].astype(jnp.bfloat16)
    expander_part = weight_sums(second_input, d_hidden)
    hidden_bias = jnp.sum(d_hidden, axis=0, dtype=jnp.float32)
    d_second = right_trans(d_hidden, back_expander)
    d_context = (
        right_trans(upstream, back_combiner).reshape(count, H, headsize).astype(jnp.bfloat16)
    )
    scores_again = masked_scores(query_low, keys_low, allowed, factor)
    probs = jnp.exp(scores_again - logsum)
    d_probs = jnp.einsum("qhd,khd->hqk", d_context, values_low, preferred_element_type=jnp.float32)
    d_values = jnp.einsum("hqk,qhd->khd", probs_low, d_context, preferred_element_type=jnp.float32)
    d_scores = (probs * (d_probs - jnp.sum(d_probs * probs, axis=2, keepdims=True))).astype(
        jnp.bfloat16
    )
    d_query = (
        jnp.einsum("hqk,khd->qhd", d_scores, keys_low, preferred_element_type=jnp.float32) * factor
    )
    d_keys = (
        jnp.einsum("hqk,qhd->khd", d_scores, query_low, preferred_element_type=jnp.float32) * factor
    )
    d_mixed = jnp.concatenate(
        [
            unrotate(d_query, cosine, sine, ROT).reshape(count, width),
            unrotate(d_keys, cosine, sine, ROT).reshape(count, width),
            d_values.reshape(count, width),
        ],
        axis=1,
    ).astype(jnp.bfloat16)
    projector_part = weight_sums(first_input, d_mixed)
    mixed_bias = jnp.sum(d_mixed, axis=0, dtype=jnp.float32)
    d_first = right_trans(d_mixed, back_projector)
    attend_scale = jnp.sum(d_first * normed, axis=0)
    attend_offset = jnp.sum(d_first, axis=0)
    feed_scale = jnp.sum(d_second * normed, axis=0)
    feed_offset = jnp.sum(d_second, axis=0)
    d_normed = d_first * back_gain_attend + d_second * back_gain_feed
    grad_float = cotangent.astype(jnp.float32) + inverse * (
        d_normed
        - jnp.mean(d_normed, axis=1, keepdims=True)
        - normed * jnp.mean(d_normed * normed, axis=1, keepdims=True)
    )
    input_gradient = grad_float.astype(jnp.bfloat16)
    mixed_bias, output_bias, hidden_bias, attend_scale, attend_offset, feed_scale, feed_offset = (
        lax.psum_scatter(
            mixed_bias.astype(jnp.bfloat16), "shard", scatter_dimension=0, tiled=True
        ).astype(jnp.float32),
        lax.psum_scatter(
            output_bias.astype(jnp.bfloat16), "shard", scatter_dimension=0, tiled=True
        ).astype(jnp.float32),
        lax.psum_scatter(
            hidden_bias.astype(jnp.bfloat16), "shard", scatter_dimension=0, tiled=True
        ).astype(jnp.float32),
        lax.psum_scatter(
            attend_scale.astype(jnp.bfloat16), "shard", scatter_dimension=0, tiled=True
        ).astype(jnp.float32),
        lax.psum_scatter(
            attend_offset.astype(jnp.bfloat16), "shard", scatter_dimension=0, tiled=True
        ).astype(jnp.float32),
        lax.psum_scatter(
            feed_scale.astype(jnp.bfloat16), "shard", scatter_dimension=0, tiled=True
        ).astype(jnp.float32),
        lax.psum_scatter(
            feed_offset.astype(jnp.bfloat16), "shard", scatter_dimension=0, tiled=True
        ).astype(jnp.float32),
    )
    (
        projector_part,
        mixed_bias,
        combiner_part,
        output_bias,
        expander_part,
        hidden_bias,
        contractor_part,
        attend_scale,
        attend_offset,
        feed_scale,
        feed_offset,
    ) = (
        lax.psum(projector_part.astype(jnp.bfloat16), "rep").astype(jnp.float32),
        lax.psum(mixed_bias.astype(jnp.bfloat16), "rep").astype(jnp.float32),
        lax.psum(combiner_part.astype(jnp.bfloat16), "rep").astype(jnp.float32),
        lax.psum(output_bias.astype(jnp.bfloat16), "rep").astype(jnp.float32),
        lax.psum(expander_part.astype(jnp.bfloat16), "rep").astype(jnp.float32),
        lax.psum(hidden_bias.astype(jnp.bfloat16), "rep").astype(jnp.float32),
        lax.psum(contractor_part.astype(jnp.bfloat16), "rep").astype(jnp.float32),
        lax.psum(attend_scale.astype(jnp.bfloat16), "rep").astype(jnp.float32),
        lax.psum(attend_offset.astype(jnp.bfloat16), "rep").astype(jnp.float32),
        lax.psum(feed_scale.astype(jnp.bfloat16), "rep").astype(jnp.float32),
        lax.psum(feed_offset.astype(jnp.bfloat16), "rep").astype(jnp.float32),
    )
    return (
        block_output,
        input_gradient,
        projector_part,
        mixed_bias,
        combiner_part,
        output_bias,
        expander_part,
        hidden_bias,
        contractor_part,
        output_bias,
        attend_scale,
        attend_offset,
        feed_scale,
        feed_offset,
    )


def solution(mesh):
    placed = (
        P(("rep", "shard"), None),
        P(("rep", "shard"), None),
        P("shard", None),
        P("shard"),
        P("shard", None),
        P("shard"),
        P("shard", None),
        P("shard"),
        P("shard", None),
        P("shard"),
        P("shard"),
        P("shard"),
        P("shard"),
        P("shard"),
        P(("rep", "shard"), None),
    )
    return jax.shard_map(
        local,
        mesh=mesh,
        in_specs=placed,
        out_specs=(
            P(("rep", "shard"), None),
            P(("rep", "shard"), None),
            P("shard", None),
            P("shard"),
            P("shard", None),
            P("shard"),
            P("shard", None),
            P("shard"),
            P("shard", None),
            P("shard"),
            P("shard"),
            P("shard"),
            P("shard"),
            P("shard"),
        ),
        check_vma=False,
    )
```

profile of v0, /device:TPU:10, one launch (start us, length us, event | category | flops | bytes accessed | tf_op | source)
XLA Modules:
  0.0 2147.7 jit_solution(16015139742509927921)
XLA Ops:
  10.7 9.1 all-gather.1
  19.8 11.9 all-gather
  31.7 13.4 all-gather.2
  47.3 180.9 %all-gather.12.cloned.1.call-done = bf16[2048,6144]{1,0:T(8,128)(2,1)} async-done(((bf16[256,6144]{1,0:T(8,128)(2,1)}), bf16[2048,6144]{1,0:T(8,128)(2,1)}) %all-gather.12.cloned.1.call-update) | async-done | bytes 25165840 | tf_op jit(solution)/shard_map/all_gather | solution.py:118
  228.2 12.0 convolution_add_fusion.1
  246.3 1.2 fusion.64
  248.5 1.0 copy-done.6
  249.5 5.6 convolution_convert_fusion.3
  255.2 55.1 %all-gather.14.cloned.1.call-done = bf16[2048,2048]{1,0:T(8,128)(2,1)} async-done(((bf16[256,2048]{1,0:T(8,128)(2,1)}), bf16[2048,2048]{1,0:T(8,128)(2,1)}) %all-gather.14.cloned.1.call-update) | async-done | bytes 8388624 | tf_op jit(solution)/shard_map/all_gather | solution.py:119
  310.3 7.1 convolution_convert_fusion.4
  317.4 2.7 copy.123
  320.1 2.4 multiply_reduce_fusion
  326.6 1.3 slice.118
  328.8 1.4 fusion.37
  330.2 1.5 pad_maximum_fusion.3
  331.7 2.3 copy.108
  334.0 2.8 pad_maximum_fusion.4
  336.8 2.3 copy.112
  339.1 2.0 convolution_convert_fusion.5
  342.0 15.0 convolution_convert_fusion.2
  357.6 19.5 all-gather.5
  377.2 9.2 all-gather.4
  386.5 34.8 %all_gather.51 = bf16[8192]{0:T(1024)(128)(2,1)S(1)} all-gather(bf16[1024]{0:T(1024)(128)(2,1)S(1)} %copy-done.24), channel_id=1, replica_groups=mesh['rep'=4,'shard'=8] {'shard'}, dimensions={0}, use_global_device_ids=true | all-gather | bytes 18432 | tf_op jit(solution)/shard_map/all_gather | solution.py:151
  421.3 177.8 %all-gather.16.cloned.1.call-done = bf16[2048,8192]{1,0:T(8,128)(2,1)} async-done(((bf16[256,8192]{1,0:T(8,128)(2,1)}), bf16[2048,8192]{1,0:T(8,128)(2,1)}) %all-gather.16.cloned.1.call-update) | async-done | bytes 33554448 | tf_op jit(solution)/shard_map/all_gather | solution.py:149
  599.1 33.2 %multiply_convert_fusion = (bf16[256,8192]{1,0:T(8,128)(2,1)}, f32[256,8192]{1,0:T(8,128)}, f32[256,8192]{1,0:T(8,128)}) fusion(f32[8192]{0:T(1024)S(1)} %convert_element_type.189, bf16[2048,8192]{1,0:T(8,128)(2,1)} %all-gather.16.cloned.1.call-done, bf16[256,2048]{1,0:T(8,128)(2,1)S(1)} %copy-done, f32[2048]{0:T(1024)S(1)} %bitcast.88, ...), kind=kOutput, calls=%fused_computation.7 | convolution fusion | flops 8731492352 | bytes 55625728 | tf_op jit(solution)/shard_map/dot_general | solution.py:154
  632.3 255.1 %all-gather.18.cloned.1.call-done = bf16[8192,2048]{1,0:T(8,128)(2,1)} async-done(((bf16[1024,2048]{1,0:T(8,128)(2,1)}), bf16[8192,2048]{1,0:T(8,128)(2,1)}) %all-gather.18.cloned.1.call-update) | async-done | bytes 33554448 | tf_op jit(solution)/shard_map/all_gather | solution.py:150
  887.4 21.9 %fusion.65 = (bf16[8192]{0:T(1024)(128)(2,1)S(1)}, bf16[256,8192]{1,0:T(8,128)(2,1)}) fusion(f32[256,8192]{1,0:T(8,128)} %get-tuple-element.42, f32[256,8192]{1,0:T(8,128)} %get-tuple-element.68, bf16[8192,2048]{1,0:T(8,128)(2,1)} %all-gather.18.cloned.1.call-done, bf16[256,2048]{1,0:T(8,128)(2,1)S(1)} %copy-done.2, pred[256]{0:T(512)(128)(4,1)S(1)} %iota_compare_fusion.2), kind=kOutput, calls=%fused_computation.131 | convolution fusion | flops 8621907968 | bytes 55591168 | tf_op jit(solution)/shard_map/dot_general | solution.py:66
  909.3 16.5 convolution_convert_fusion.1
  925.9 16.5 convolution_convert_fusion
  942.5 34.9 %reduce-scatter.7.cloned.1.call-done = bf16[256,2048]{1,0:T(8,128)(2,1)} async-done(((bf16[2048,2048]{1,0:T(8,128)(2,1)}), bf16[256,2048]{1,0:T(8,128)(2,1)}) %reduce-scatter.7.cloned.1.call-update) | async-done | bytes 1048592 | tf_op jit(solution)/shard_map/reduce_scatter | solution.py:81
  977.3 247.8 %reduce-scatter.5.cloned.1.call-done = bf16[256,6144]{1,0:T(8,128)(2,1)} async-done(((bf16[2048,6144]{1,0:T(8,128)(2,1)}), bf16[256,6144]{1,0:T(8,128)(2,1)}) %reduce-scatter.5.cloned.1.call-update) | async-done | bytes 3145744 | tf_op jit(solution)/shard_map/reduce_scatter | solution.py:81
  1225.1 326.3 %reduce-scatter.9.cloned.1.call-done = bf16[256,8192]{1,0:T(8,128)(2,1)} async-done(((bf16[2048,8192]{1,0:T(8,128)(2,1)}), bf16[256,8192]{1,0:T(8,128)(2,1)}) %reduce-scatter.9.cloned.1.call-update) | async-done | bytes 4194320 | tf_op jit(solution)/shard_map/reduce_scatter | solution.py:81
  1551.4 326.4 %reduce-scatter.11.cloned.1.call-done = bf16[1024,2048]{1,0:T(8,128)(2,1)} async-done(((bf16[8192,2048]{1,0:T(8,128)(2,1)}), bf16[1024,2048]{1,0:T(8,128)(2,1)}) %reduce-scatter.11.cloned.1.call-update) | async-done | bytes 4194320 | tf_op jit(solution)/shard_map/reduce_scatter | solution.py:81
  1881.0 11.9 all-gather.6
  1892.9 9.1 all-gather.3
  1902.4 2.2 fusion.51
  1904.6 7.2 convolution_add_fusion.3
  1911.9 14.0 fusion.52
  1925.9 19.3 fusion.55
  1945.2 24.4 %all-reduce.7 = (bf16[6144]{0:T(1024)(128)(2,1)S(1)}, bf16[2048]{0:T(1024)(128)(2,1)S(1)}, bf16[8192]{0:T(1024)(128)(2,1)S(1)}, bf16[2048]{0:T(1024)(128)(2,1)S(...) all-reduce(bf16[6144]{0:T(1024)(128)(2,1)S(1)} %fusion.51, ...), channel_id=3, replica_groups=mesh['rep'=4,'shard'=8] {'shard'}, use_global_device_ids=true, to_apply=%region_12.13.clone | all-reduce | flops 24576 | bytes 98304
  1970.1 8.9 all-reduce.8
  1982.5 3.5 fusion.25
  1986.0 17.8 fusion.8
  2003.7 121.2 %all-reduce.12.cloned.1.call-done = (bf16[256,6144]{1,0:T(8,128)(2,1)}, bf16[256,2048]{1,0:T(8,128)(2,1)}, bf16[256,8192]{1,0:T(8,128)(2,1)}, bf16[1024,2048]{1,0:T(8,128)(2,1)}) async-done(((bf16[256,6144]{1,0:T(8,128)(2,1)}, bf16[256,2048]{1,0:T(8,128)(2,1)}, bf16[256,8192]{1,0:T(8,128)(2,1)}, bf16[1024,2048]{1,0:T(8,128)(2,1)}), (bf16[256,6144]{1,0:T(8,128)(2,1)}, bf16[256,2048]{1,0:T(8,128)(2,1)}, ...) | async-done | bytes 12582928 | tf_op jit(solution)/shard_map/psum | solution.py:261
  2125.0 2.9 convert_element_type.203
  2127.9 3.4 convert_element_type.200
  2131.4 4.4 convert_element_type.206
  2135.7 4.4 convert_element_type.209
  (159 shorter events, 25.2 us)
Async XLA Ops:
  7.2 221.0 %all-gather.12.cloned.1.call-start = ((), (), s32[]{:S(2)}) async-start(), calls=%async_computation.4 | async-start | bytes 28311552 | tf_op jit(solution)/shard_map/all_gather | solution.py:118
  7.9 302.4 %all-gather.14.cloned.1.call-start = ((), (), s32[]{:S(2)}) async-start(), calls=%async_computation.5 | async-start | bytes 9437184 | tf_op jit(solution)/shard_map/all_gather | solution.py:119
  8.7 1.4 copy-start.27
  8.7 2.0 copy-start.28
  8.7 2.0 copy-start.29
  8.7 2.0 copy-start.25
  8.7 37.8 %copy-start = (bf16[256,2048]{1,0:T(8,128)(2,1)S(1)}, bf16[256,2048]{1,0:T(8,128)(2,1)}, u32[]{:S(2)}) copy-start(bf16[256,2048]{1,0:T(8,128)(2,1)} %param.15) | copy-start | bytes 3145732
  8.7 590.4 %all-gather.16.cloned.1.call-start = ((), (), s32[]{:S(2)}) async-start(), calls=%async_computation.6 | async-start | bytes 37748736 | tf_op jit(solution)/shard_map/all_gather | solution.py:149
  9.4 878.0 %all-gather.18.cloned.1.call-start = ((), (), s32[]{:S(2)}) async-start(), calls=%async_computation.7 | async-start | bytes 37748736 | tf_op jit(solution)/shard_map/all_gather | solution.py:150
  10.0 967.3 %reduce-scatter.7.cloned.1.call-start = ((), (), s32[]{:S(2)}) async-start(), calls=%async_computation.9 | async-start | bytes 9437184 | tf_op jit(solution)/shard_map/reduce_scatter | solution.py:81
  31.6 309.4 %copy-start.22 = (f32[8,1,256]{2,1,0:T(1,128)}, f32[8,1,256]{2,1,0:T(1,128)S(1)}, u32[]{:S(2)}) copy-start(f32[8,1,256]{2,1,0:T(1,128)S(1)} %convert_element_type.218) | copy-start | bytes 24580
  240.3 7.5 copy-start.12
  243.5 2.8 copy-start.13
  244.3 2.0 copy-start.15
  246.3 1.5 copy-start.18
  246.3 1.5 copy-start.20
  247.8 1.7 copy-start.1
  248.5 1.0 copy-start.6
  255.2 969.9 %reduce-scatter.5.cloned.1.call-start = ((), (), s32[]{:S(2)}) async-start(), calls=%async_computation.8 | async-start | bytes 28311552 | tf_op jit(solution)/shard_map/reduce_scatter | solution.py:81
  322.6 1.4 copy-start.14
  322.6 1.6 copy-start.21
  324.2 1.4 copy-start.16
  324.2 1.6 copy-start.19
  339.1 2.9 copy-start.3
  339.1 2.9 copy-start.5
  341.0 1.0 copy-start.11
  357.0 0.7 copy-start.30
  357.0 0.7 copy-start.31
  357.0 29.5 %copy-start.24 = (bf16[1024]{0:T(1024)(128)(2,1)S(1)}, bf16[1024]{0:T(1024)(128)(2,1)}, u32[]{:S(2)}) copy-start(bf16[1024]{0:T(1024)(128)(2,1)} %param.22) | copy-start | bytes 6148
  357.0 1194.4 %reduce-scatter.9.cloned.1.call-start = ((), (), s32[]{:S(2)}) async-start(), calls=%async_computation.10 | async-start | bytes 37748736 | tf_op jit(solution)/shard_map/reduce_scatter | solution.py:81
  599.1 288.3 %copy-start.2 = (bf16[256,2048]{1,0:T(8,128)(2,1)S(1)}, bf16[256,2048]{1,0:T(8,128)(2,1)}, u32[]{:S(2)}) copy-start(bf16[256,2048]{1,0:T(8,128)(2,1)} %param.29) | copy-start | bytes 3145732
  925.8 952.0 %reduce-scatter.11.cloned.1.call-start = ((), (), s32[]{:S(2)}) async-start(), calls=%async_computation.11 | async-start | bytes 37748736 | tf_op jit(solution)/shard_map/reduce_scatter | solution.py:81
  942.4 1182.6 %all-reduce.12.cloned.1.call-start = ((), (), s32[]{:S(2)}) async-start(), calls=%async_computation.12 | async-start | bytes 25165824 | tf_op jit(solution)/shard_map/psum | solution.py:261
  1877.8 0.7 copy-start.34
  1877.8 3.2 copy-start.32
  1877.8 3.2 copy-start.33
  1877.8 24.6 %copy-start.4 = (bf16[256,8,256]{0,2,1:T(8,128)(2,1)S(1)}, bf16[256,8,256]{0,2,1:T(8,128)(2,1)}, u32[]{:S(2)}) copy-start(bf16[256,8,256]{0,2,1:T(8,128)(2,1)} %copy.108) | copy-start | bytes 3145732
  1881.0 23.6 %copy-start.7 = (bf16[8,256,256]{2,1,0:T(8,128)(2,1)S(1)}, bf16[8,256,256]{2,1,0:T(8,128)(2,1)}, u32[]{:S(2)}) copy-start(bf16[8,256,256]{2,1,0:T(8,128)(2,1)} %copy-done.6) | copy-start | bytes 3145732
  1911.9 14.0 copy-start.23
  1979.0 7.0 copy-start.8
  1979.0 161.2 %copy-start.26 = (f32[256]{0:T(256)}, f32[256]{0:T(256)S(1)}, u32[]{:S(2)}) copy-start(f32[256]{0:T(256)S(1)} %convert_element_type.204) | copy-start | bytes 3076
  2125.0 2.9 copy-start.17
  2127.9 3.5 copy-start.10
  2131.4 4.4 copy-start.9
Sparse Core Ops, SparseCore 0:
  9.7 218.4 all-gather.11
  229.8 80.5 all-gather.13
  311.9 287.1 all-gather.15
  600.6 286.8 all-gather.17
  889.5 87.7 reduce-scatter.6
  979.5 245.5 reduce-scatter.4
  1227.5 323.8 reduce-scatter.8
  1553.9 323.8 reduce-scatter.10
  1881.7 243.2 all-reduce.11
where the time goes:
time: 2150 us
  waiting for transfers between devices  1730 us (80%)
  matrix products  194 us (9%)
  blocking collectives  152 us (7%)
  other arithmetic  35.6 us (2%)
    reduce_scatter x4, waiting for transfers between devices, weight_sums(): lax.psum_scatter(left_trans(piece, right).astype(jnp.bfloat16), 'shard',...  935 us
    all_gather x1, waiting for transfers between devices, local(): lax.all_gather(contractor, 'shard', axis=0, tiled=True)  255 us
    all_gather x1, waiting for transfers between devices, local(): lax.all_gather(projector, 'shard', axis=0, tiled=True)  181 us
    all_gather x1, waiting for transfers between devices, local(): lax.all_gather(expander, 'shard', axis=0, tiled=True)  178 us
    psum x1, waiting for transfers between devices, local(): lax.psum(projector_part.astype(jnp.bfloat16), 'rep').astype(jnp.float32)  121 us
    dot_general x4, matrix products, right_trans(): lax.dot_general(left, right, (((1,), (1,)), ((), ())), preferred_element_...  62.3 us
    all_gather x1, waiting for transfers between devices, local(): lax.all_gather(combiner, 'shard', axis=0, tiled=True)  55.1 us
    dot_general x4, matrix products, left_trans(): lax.dot_general(left, right, (((0,), (0,)), ((), ())), preferred_element_...  53.6 us
  transfers between devices with their start and end apart: 9, of which 9 were waited for; matrix products, arithmetic and copies ran while one was open for 11% of the time, Pallas kernels for 0%

commit v1 on v0

--- a/solution.py
+++ b/solution.py
@@ -8,10 +8,12 @@
 
 H = 8
 ROT = 64
-
+BLOCK = 256
 
 epsilon = 1e-05
 masked_value = -1e30
+f32 = jnp.float32
+bf16 = jnp.bfloat16
 
 
 def normalize(values):
@@ -27,17 +29,17 @@
     passed = index[:, None] >= ends[None, :]
     document = jnp.sum(passed.astype(jnp.int32), axis=1)
     begin = jnp.max(jnp.where(passed, ends[None, :], 0), axis=1)
-    position = (index - begin).astype(jnp.float32)
+    position = (index - begin).astype(f32)
     allowed = (document[:, None] == document[None, :]) & (index[None, :] <= index[:, None])
     return (position, allowed, index < ends[-1])
 
 
 def rotary_tables(position, rotary):
     half = rotary // 2
-    freqs = jnp.exp(-jnp.arange(half, dtype=jnp.float32) * (2.0 / rotary) * math.log(10000.0))
-    angles = position[:, None] * freqs[None, :]
-    angles = jnp.concatenate([angles, angles], axis=1)
-    return (jnp.cos(angles)[:, None, :], jnp.sin(angles)[:, None, :])
+    freqs = jnp.exp(-jnp.arange(half, dtype=f32) * (2.0 / rotary) * math.log(10000.0))
+    angles = position[..., None] * freqs
+    angles = jnp.concatenate([angles, angles], axis=-1)
+    return (jnp.cos(angles), jnp.sin(angles))
 
 
 def rotate(values, cosine, sine, rotary):
@@ -55,23 +57,150 @@
     return jnp.concatenate([front * cosine + backward, grads[..., rotary:]], axis=-1)
 
 
+def right_trans(left, right):
+    return lax.dot_general(left, right, (((1,), (1,)), ((), ())), preferred_element_type=f32)
+
+
+def left_trans(left, right):
+    return lax.dot_general(left, right, (((0,), (0,)), ((), ())), preferred_element_type=f32)
+
+
+def sharded_heads(
+    tokens, document_ends, projector, projbias, combiner, combbias, expander, expbias,
+    contractor, contbias, attendgain, attendshift, feedgain, feedshift, cotangent,
+):
+    count, width = tokens.shape
+    n = lax.axis_size("shard")
+    me = lax.axis_index("shard")
+    head = width // H
+    factor = 1.0 / math.sqrt(head)
+    rows = width // n
+    exp_cols = lax.all_to_all(expander, "shard", split_axis=1, concat_axis=0, tiled=True)
+    proj_cols = lax.all_to_all(
+        projector.reshape(rows, 3, n, head), "shard", split_axis=2, concat_axis=0, tiled=True
+    ).reshape(width, 3 * head)
+    vectors = jnp.concatenate(
+        [projbias, combbias, contbias, attendgain, attendshift, feedgain, feedshift]
+    )
+    vectors = lax.all_gather(vectors, "shard", axis=0, tiled=False).astype(f32)
+    wide = projbias.shape[0]
+    full_projbias = vectors[:, :wide].reshape(3, n, head)
+    my_projbias = lax.dynamic_index_in_dim(full_projbias, me, axis=1, keepdims=False).reshape(-1)
+    gains = vectors[:, wide:].reshape(n, 6, rows).transpose(1, 0, 2).reshape(6, width)
+    comb_b, cont_b, a_gain, a_shift, f_gain, f_shift = (gains[i] for i in range(6))
+    ends = lax.all_gather(document_ends, "shard", axis=0, tiled=True)
+    x = lax.all_gather(tokens, "shard", axis=0, tiled=True)
+    position, allowed, live = jax.vmap(lambda e: layout(e, count))(ends)
+    _, _, my_live = layout(document_ends[0], count)
+    upstream = lax.all_gather(
+        jnp.where(my_live[:, None], cotangent, jnp.zeros_like(cotangent)), "shard", axis=0, tiled=True
+    )
+    cosine, sine = rotary_tables(position, ROT)
+    floated = x.astype(f32)
+    normed, inverse = normalize(floated)
+    first = (normed * a_gain + a_shift).astype(bf16)
+    second = (normed * f_gain + f_shift).astype(bf16)
+    mixed = jnp.dot(first, proj_cols, preferred_element_type=f32) + my_projbias
+    mixed = mixed.reshape(n, count, 3, head)
+    q = rotate(mixed[:, :, 0], cosine, sine, ROT).astype(bf16)
+    k = rotate(mixed[:, :, 1], cosine, sine, ROT).astype(bf16)
+    v = mixed[:, :, 2].astype(bf16)
+    scores = jnp.einsum("bqd,bkd->bqk", q, k, preferred_element_type=f32) * factor
+    scores = jnp.where(allowed, scores, masked_value)
+    peak = jnp.max(scores, axis=2, keepdims=True)
+    raised = jnp.exp(scores - peak)
+    probs = raised / jnp.sum(raised, axis=2, keepdims=True)
+    probs_low = probs.astype(bf16)
+    context = jnp.einsum("bqk,bkd->bqd", probs_low, v, preferred_element_type=f32)
+    context = context.reshape(n * count, head).astype(bf16)
+    hidden = jnp.dot(second, exp_cols, preferred_element_type=f32) + expbias.astype(f32)
+    activated, gelu_back = jax.vjp(partial(jax.nn.gelu, approximate=False), hidden)
+    active = activated.astype(bf16)
+    part = jnp.dot(context, combiner, preferred_element_type=f32) + jnp.dot(
+        active, contractor, preferred_element_type=f32
+    )
+    summed = lax.psum_scatter(part.astype(bf16), "shard", scatter_dimension=0, tiled=True)
+    block_output = tokens.astype(f32) + jnp.where(
+        my_live[:, None], summed.astype(f32) + comb_b + cont_b, 0.0
+    )
+    block_output = block_output.astype(bf16)
+
+    d_active = right_trans(upstream, contractor)
+    d_hidden = gelu_back(d_active)[0].astype(bf16)
+    contractor_part = left_trans(active, upstream).astype(bf16)
+    combiner_part = left_trans(context, upstream).astype(bf16)
+    expander_part = left_trans(second, d_hidden).astype(bf16)
+    hidden_bias = jnp.sum(d_hidden, axis=0, dtype=f32)
+    d_context = right_trans(upstream, combiner).astype(bf16).reshape(n, count, head)
+    d_probs = jnp.einsum("bqd,bkd->bqk", d_context, v, preferred_element_type=f32)
+    d_v = jnp.einsum("bqk,bqd->bkd", probs_low, d_context, preferred_element_type=f32)
+    d_s = (probs * (d_probs - jnp.sum(d_probs * probs, axis=2, keepdims=True))).astype(bf16)
+    d_q = jnp.einsum("bqk,bkd->bqd", d_s, k, preferred_element_type=f32) * factor
+    d_k = jnp.einsum("bqk,bqd->bkd", d_s, q, preferred_element_type=f32) * factor
+    d_mixed = jnp.concatenate(
+        [unrotate(d_q, cosine, sine, ROT), unrotate(d_k, cosine, sine, ROT), d_v], axis=-1
+    ).astype(bf16).reshape(n * count, 3 * head)
+    projector_part = left_trans(first, d_mixed).astype(bf16)
+    mixed_bias = jnp.sum(d_mixed, axis=0, dtype=f32)
+    d_first = right_trans(d_mixed, proj_cols)
+    d_second = right_trans(d_hidden, exp_cols)
+    sums = jnp.stack(
+        [
+            jnp.sum(d_first * normed, axis=0),
+            jnp.sum(d_first, axis=0),
+            jnp.sum(d_second * normed, axis=0),
+            jnp.sum(d_second, axis=0),
+        ]
+    )
+    d_normed = lax.psum_scatter(
+        (d_first * a_gain + d_second * f_gain).astype(bf16),
+        "shard", scatter_dimension=0, tiled=True,
+    ).astype(f32)
+    own_normed, own_inverse = normalize(tokens.astype(f32))
+    grad = cotangent.astype(f32) + own_inverse * (
+        d_normed
+        - jnp.mean(d_normed, axis=1, keepdims=True)
+        - own_normed * jnp.mean(d_normed * own_normed, axis=1, keepdims=True)
+    )
+    input_gradient = grad.astype(bf16)
+
+    expander_part = lax.all_to_all(expander_part, "shard", split_axis=0, concat_axis=1, tiled=True)
+    projector_part = lax.all_to_all(
+        projector_part.reshape(width, 3, 1, head), "shard", split_axis=0, concat_axis=2, tiled=True
+    ).reshape(rows, 3 * width)
+    out_bias = jnp.sum(upstream, axis=0, dtype=f32)
+    mixed_full = jnp.zeros((3, n, head), f32)
+    mixed_full = lax.dynamic_update_slice(mixed_full, mixed_bias.reshape(3, 1, head), (0, me, 0))
+    vector = jnp.concatenate(
+        [
+            mixed_full.reshape(n, wide),
+            sums.reshape(4, n, rows).transpose(1, 0, 2).reshape(n, 4 * rows),
+        ],
+        axis=1,
+    )
+    vector = lax.psum_scatter(vector, "shard", scatter_dimension=0, tiled=True)[0]
+    own_out = lax.dynamic_slice(out_bias, (me * rows,), (rows,))
+    vector = lax.psum(jnp.concatenate([vector, own_out, hidden_bias]), "rep")
+    mixed_bias = vector[:wide]
+    a, b, c, d, out_bias = (vector[wide + i * rows : wide + (i + 1) * rows] for i in range(5))
+    hidden_bias = vector[wide + 5 * rows :]
+    projector_part, combiner_part, expander_part, contractor_part = (
+        item.astype(f32)
+        for item in lax.psum(
+            (projector_part, combiner_part, expander_part, contractor_part), "rep"
+        )
+    )
+    return (
+        block_output, input_gradient, projector_part, mixed_bias, combiner_part, out_bias,
+        expander_part, hidden_bias, contractor_part, out_bias, a, b, c, d,
+    )
+
+
 def masked_scores(query_low, keys_low, allowed, factor):
     scores = (
         jnp.einsum("qhd,khd->hqk", query_low, keys_low, preferred_element_type=jnp.float32) * factor
     )
     return jnp.where(allowed[None], scores, masked_value)
-
-
-def right_trans(left, right):
-    return lax.dot_general(
-        left, right, (((1,), (1,)), ((), ())), preferred_element_type=jnp.float32
-    )
-
-
-def left_trans(left, right):
-    return lax.dot_general(
-        left, right, (((0,), (0,)), ((), ())), preferred_element_type=jnp.float32
-    )
 
 
 def weight_sums(left, right):
@@ -105,6 +234,7 @@
     factor = 1.0 / math.sqrt(headsize)
     position, allowed, live = layout(document_ends[0], count)
     cosine, sine = rotary_tables(position, ROT)
+    cosine, sine = cosine[:, None, :], sine[:, None, :]
     (
         full_projector,
         full_combiner,
@@ -307,7 +437,7 @@
         P(("rep", "shard"), None),
     )
     return jax.shard_map(
-        local,
+        sharded_heads if mesh.shape["shard"] == H else local,
         mesh=mesh,
         in_specs=placed,
         out_specs=(

time: 2150 us -> 1160 us (0.54)
  waiting for transfers between devices: 1730 us -> 529 us
  local copies, waits for them, and re-layouts: 20.6 us -> 108 us
  blocking collectives: 152 us -> 214 us
  other arithmetic: 35.6 us -> 74.4 us
  starting transfers between devices: 0.36 us -> 30.3 us
    reduce_scatter x4 -> x2, waiting for transfers between devices: 935 us -> 0.02 us  [the longest x1 0.02 us: sharded_heads(): lax.psum_scatter(part.astype(bf16), 'shard', scatter_dimension=0, tiled=T...]
    all_gather x4 -> x2, waiting for transfers between devices: 669 us -> 0.01 us  [the longest x1 0.01 us: sharded_heads(): x = lax.all_gather(tokens, 'shard', axis=0, tiled=True)]
    all_to_all x0 -> x4, waiting for transfers between devices: none -> 344 us  [the longest x1 131 us: sharded_heads(): lax.all_to_all(projector_part.reshape(width, 3, 1, head), 'shard', split_...]
    psum x1, waiting for transfers between devices: 121 us -> 184 us  [sharded_heads(): lax.psum((projector_part, combiner_part, expander_part, contractor_part),...]
    all_gather x8 -> x2, blocking collectives: 119 us -> 172 us  [the longest x1 162 us: sharded_heads(): vectors = lax.all_gather(vectors, 'shard', axis=0, tiled=False).astype(f32)]
    all_to_all x0 -> x4, starting transfers between devices: none -> 30.2 us  [the longest x1 9.13 us: sharded_heads(): lax.all_to_all(expander_part, 'shard', split_axis=0, concat_axis=1, tiled...]
    reshape x0 -> x7, local copies, waits for them, and re-layouts: none -> 27.6 us  [the longest x1 10.9 us: sharded_heads(): mixed = mixed.reshape(n, count, 3, head)]
    dot_general x10 -> x9, matrix products: 78 us -> 54.4 us  [the longest x1 15.5 us: sharded_heads(): jnp.dot(active, contractor, preferred_element_type=f32)]
  transfers between devices with their start and end apart: 9 -> 9, of which waited for: 9 -> 4; matrix products, arithmetic and copies ran while one was open for 11% -> 20% of each run, Pallas kernels for 0% -> 0%
where the time goes in v1:
time: 1160 us; the launch traced here: 1150 us
  waiting for transfers between devices  529 us (46%)
  blocking collectives  214 us (18%)
  matrix products  180 us (16%)
  local copies, waits for them, and re-layouts  108 us (9%)
  other arithmetic  74.4 us (6%)
  starting transfers between devices  30.3 us (3%)
  between operations  14.7 us (1%)
    psum x1, waiting for transfers between devices, sharded_heads(): lax.psum((projector_part, combiner_part, expander_part, contractor_part),...  184 us
    all_gather x1, blocking collectives, sharded_heads(): vectors = lax.all_gather(vectors, 'shard', axis=0, tiled=False).astype(f32)  162 us
    all_to_all x1, waiting for transfers between devices, sharded_heads(): lax.all_to_all(projector_part.reshape(width, 3, 1, head), 'shard', split_...  131 us
    all_to_all x1, waiting for transfers between devices, sharded_heads(): lax.all_to_all(projector.reshape(rows, 3, n, head), 'shard', split_axis=2...  126 us
    all_to_all x1, waiting for transfers between devices, sharded_heads(): lax.all_to_all(expander_part, 'shard', split_axis=0, concat_axis=1, tiled...  86.8 us
    dot_general x4, matrix products, right_trans(): lax.dot_general(left, right, (((1,), (1,)), ((), ())), preferred_element_...  73.3 us
    dot_general x4, matrix products, left_trans(): lax.dot_general(left, right, (((0,), (0,)), ((), ())), preferred_element_...  47.6 us
    unnamed x1, blocking collectives  27.6 us
  transfers between devices with their start and end apart: 9, of which 4 were waited for; matrix products, arithmetic and copies ran while one was open for 20% of the time, Pallas kernels for 0%

profile of v1, /device:TPU:10, one launch (start us, length us, event | category | flops | bytes accessed | tf_op | source)
XLA Modules:
  0.0 1150.7 jit_solution(555882761586840402)
XLA Ops:
  7.9 4.6 copy.123
  12.6 3.9 copy.124
  16.4 5.3 all-to-all-start
  21.8 6.4 copy.131
  28.3 126.5 %all-to-all-done = bf16[256,3,8,256]{0,3,1,2:T(8,128)(2,1)} async-done(((bf16[256,3,8,256]{0,3,1,2:T(8,128)(2,1)}), bf16[256,3,8,256]{0,3,1,2:T(8,128)(2,1)}, u32[]{:S(2)}, u32[]{:S(2)}) %all-to-all-start) | async-done | bytes 3145760 | tf_op jit(solution)/shard_map/all_to_all | solution.py:79
  154.8 8.5 all-to-all-start.1
  167.6 162.0 %all-gather.2 = bf16[8,1,2304]{2,1,0:T(2,128)(2,1)S(1)} all-gather(bf16[1,1,2304]{2,1,0:T(2,128)(2,1)S(1)} %reshape.194), channel_id=2, replica_groups=mesh['rep'=4,'shard'=8] {'shard'}, dimensions={0}, use_global_device_ids=true | all-gather | bytes 41472 | tf_op jit(solution)/shard_map/all_gather | solution.py:85
  329.7 9.7 all-gather.1
  347.1 6.4 copy.132
  353.5 4.7 convert_reduce_fusion
  361.6 3.7 fusion.8
  368.7 8.6 broadcast_add_fusion
  377.3 10.9 reshape.199
  388.1 7.1 slice.170
  395.3 11.9 %fusion.56 = (f32[8,256,1,256]{3,2,1,0:T(1,128)}, f32[8,256,1,256]{3,2,1,0:T(1,128)}) fusion(f32[8,256,3,256]{3,2,1,0:T(4,128)} %reshape.199), kind=kLoop, calls=%fused_computation.139 | loop fusion | bytes 8388608 | tf_op jit(solution)/shard_map/slice | solution.py:105
  412.2 6.1 fusion.34
  418.3 4.4 fusion.60
  422.7 5.9 convolution_convert_fusion.4
  435.7 3.8 slice_multiply_fusion.2
  442.9 11.5 %fusion.53 = f32[2048,1024]{1,0:T(8,128)} fusion(bf16[2048,1024]{1,0:T(8,128)(2,1)S(1)} %bitcast.110, bf16[2048,2048]{1,0:T(8,128)(2,1)S(1)} %bitcast.99, f32[2048]{0:T(1024)S(1)} %bitcast.129, f32[2048]{0:T(1024)S(1)} %bitcast.131, f32[2048]{0:T(1024)S(1)} %add_rsqrt_fusion, f32[2048]{0:T(1024)S(1)} %broadcast_multiply_fusion.1), kind=kOutput, calls=%fused_computation.138 | convolution fusion | flops 8615100416 | bytes 21004288 | tf_op jit(solution)/shard_map/dot_general | solution.py:116
  454.4 33.1 %convert_reduce_fusion.2 = (f32[1024]{0:T(1024)}, bf16[2048,1024]{1,0:T(8,128)(2,1)}, f32[2048,1024]{1,0:T(8,128)}) fusion(f32[2048,1024]{1,0:T(8,128)} %fusion.53, f32[1024]{0:T(1024)S(1)} %convert_element_type.123, bf16[2048,2048]{1,0:T(8,128)(2,1)S(1)} %bitcast.101, bf16[1024,2048]{1,0:T(8,128)(2,1)} %param.23), kind=kOutput, calls=%fused_computation.21 | convolution fusion | flops 8747219968 | bytes 33562624 | tf_op jit(solution)/shard_map/dot_general | solution.py:61
  487.5 14.4 %fusion.62 = f32[2048,2048]{1,0:T(8,128)} fusion(bf16[2048,1024]{1,0:T(8,128)(2,1)} %get-tuple-element.29, bf16[2048,1024]{1,0:T(8,128)(2,1)S(1)} %bitcast.111), kind=kOutput, calls=%fused_computation.145 | convolution fusion | flops 8589934592 | bytes 25165824 | tf_op jit(solution)/shard_map/dot_general | solution.py:61
  501.9 5.0 fusion.36
  506.9 6.9 concatenate.61
  513.7 19.9 %fusion.11 = (f32[2048]{0:T(1024)S(1)}, f32[2048]{0:T(1024)S(1)}, f32[2048]{0:T(1024)S(1)}, f32[2048]{0:T(1024)S(1)}, bf16[2048,2048]{1,0:T(8,128)(2,1)}) fusion(bf16[2048,2048]{1,0:T(8,128)(2,1)} %all-gather.6.cloned.1.call-done, f32[2048]{0:T(1024)S(1)} %add_rsqrt_fusion, f32[2048]{0:T(1024)S(1)} %broadcast_multiply_fusion.1, f32[2048,2048]{1,0:T(8,128)} %fusion.62, ...), kind=kOutput, calls=%fused_computation.13 | convolution fusion | flops 6496968704 | bytes 39911424 | tf_op jit(solution)/shard_map/dot_general | solution.py:61
  537.1 10.8 multiply_convert_fusion
  547.9 15.5 %fusion.61 = f32[2048,2048]{1,0:T(8,128)} fusion(bf16[2048,1024]{1,0:T(8,128)(2,1)} %multiply_convert_fusion, bf16[1024,2048]{1,0:T(8,128)(2,1)} %param.23), kind=kOutput, calls=%fused_computation.144 | convolution fusion | flops 8589934592 | bytes 25165824 | tf_op jit(solution)/shard_map/dot_general | solution.py:119
  563.5 11.7 %add_convert_fusion.1 = bf16[2048,2048]{1,0:T(8,128)(2,1)} fusion(f32[2048,2048]{1,0:T(8,128)} %fusion.61, bf16[2048,256]{1,0:T(8,128)(2,1)S(1)} %bitcast.106, bf16[256,2048]{1,0:T(8,128)(2,1)S(1)} %copy-done), kind=kOutput, calls=%fused_computation.18 | convolution fusion | flops 2155872256 | bytes 27262976 | tf_op jit(solution)/shard_map/dot_general | solution.py:119
  575.2 12.2 %convolution_convert_fusion.2 = bf16[2048,768]{0,1:T(8,128)(2,1)} fusion(bf16[2048,2048]{1,0:T(8,128)(2,1)} %copy-done.3, bf16[2048,768]{1,0:T(8,128)(2,1)} %concatenate.61), kind=kOutput, calls=%fused_computation.40 | convolution fusion | flops 6444023808 | bytes 14680064 | tf_op jit(solution)/shard_map/dot_general | solution.py:65
  587.3 7.2 copy.140
  594.5 7.3 all-to-all-start.2
  601.8 15.3 %convolution_convert_fusion.1 = bf16[2048,1024]{1,0:T(8,128)(2,1)} fusion(bf16[2048,1024]{1,0:T(8,128)(2,1)} %get-tuple-element.29, bf16[2048,2048]{1,0:T(8,128)(2,1)} %all-gather.6.cloned.1.call-done, f32[2048]{0:T(1024)S(1)} %bitcast.130, f32[2048]{0:T(1024)S(1)} %bitcast.133, f32[2048]{0:T(1024)S(1)} %add_rsqrt_fusion, f32[2048]{0:T(1024)S(1)} %broadcast_multiply_fusion.1), kind=kOutput, calls=%fused_computation.39 | convolution fusion | flops 8617197568 | bytes 16809984 | tf_op jit(solution)/shard_map/dot_general | solution.py:65
  617.1 131.2 %all-to-all-done.2 = bf16[2048,3,1,256]{3,1,2,0:T(4,128)(2,1)} async-done(((bf16[2048,3,1,256]{3,1,2,0:T(4,128)(2,1)}), bf16[2048,3,1,256]{3,1,2,0:T(4,128)(2,1)}, u32[]{:S(2)}, u32[]{:S(2)}) %all-to-all-start.2) | async-done | bytes 3145760 | tf_op jit(solution)/shard_map/all_to_all | solution.py:168
  748.3 9.1 all-to-all-start.3
  757.4 6.9 convolution_convert_fusion.3
  764.4 13.2 %convolution_convert_fusion = bf16[1024,2048]{1,0:T(8,128)(2,1)} fusion(bf16[2048,1024]{1,0:T(8,128)(2,1)S(1)} %copy-done.10, bf16[2048,2048]{1,0:T(8,128)(2,1)} %all-gather.8.cloned.1.call-done), kind=kOutput, calls=%fused_computation.38 | convolution fusion | flops 8592031744 | bytes 16777216 | tf_op jit(solution)/shard_map/dot_general | solution.py:65
  777.6 7.2 copy.141
  784.8 5.7 reshape.186
  790.5 86.8 %all-to-all-done.3 = bf16[8,256,1024]{2,1,0:T(8,128)(2,1)} async-done(((bf16[8,256,1024]{2,1,0:T(8,128)(2,1)}), bf16[8,256,1024]{2,1,0:T(8,128)(2,1)}, u32[]{:S(2)}, u32[]{:S(2)}) %all-to-all-start.3) | async-done | bytes 4194336 | tf_op jit(solution)/shard_map/all_to_all | solution.py:167
  877.2 4.8 copy.156
  886.6 4.8 convert_reduce_fusion.1
  891.5 27.6 %all-reduce = f32[8,1792]{1,0:T(8,128)S(1)} all-reduce(f32[8,1792]{1,0:T(8,128)S(1)} %pad_maximum_fusion.11), channel_id=5, replica_groups=mesh['rep'=4,'shard'=8] {'shard'}, use_global_device_ids=true, to_apply=%region_19.20.clone | all-reduce | flops 14336 | bytes 114688
  919.9 14.7 %psum.36 = f32[3072]{0:T(1024)S(1)} all-reduce(f32[3072]{0:T(1024)S(1)} %pad_maximum_fusion.13), channel_id=1, replica_groups=mesh['rep'=4,'shard'=8] {'rep'}, use_global_device_ids=true, to_apply=%region_22.23 | all-reduce | flops 3072 | bytes 24576 | tf_op jit(solution)/shard_map/psum | solution.py:183
  938.4 4.0 fusion.26
  942.4 183.8 %all-reduce.4.cloned.1.call-done = (bf16[256,6144]{1,0:T(8,128)(2,1)}, bf16[256,2048]{1,0:T(8,128)(2,1)}, bf16[256,8192]{1,0:T(8,128)(2,1)}, bf16[1024,2048]{1,0:T(8,128)(2,1)}) async-done(((bf16[256,6144]{1,0:T(8,128)(2,1)}, bf16[256,2048]{1,0:T(8,128)(2,1)}, bf16[256,8192]{1,0:T(8,128)(2,1)}, bf16[1024,2048]{1,0:T(8,128)(2,1)}), (bf16[256,6144]{1,0:T(8,128)(2,1)}, bf16[256,2048]{1,0:T(8,128)(2,1)}, ...) | async-done | bytes 12582928 | tf_op jit(solution)/shard_map/psum | solution.py:189
  1129.1 5.3 convert_element_type.136
  1134.5 4.4 convert_element_type.143
  1138.8 4.4 convert_element_type.145
  (188 shorter events, 50.7 us)
Async XLA Ops:
  7.2 415.6 %copy-start = (bf16[256,2048]{1,0:T(8,128)(2,1)S(1)}, bf16[256,2048]{1,0:T(8,128)(2,1)}, u32[]{:S(2)}) copy-start(bf16[256,2048]{1,0:T(8,128)(2,1)} %param.19) | copy-start | bytes 3145732
  7.2 346.3 %all-gather.6.cloned.1.call-start = ((), (), s32[]{:S(2)}) async-start(), calls=%async_computation.6 | async-start | bytes 9437184 | tf_op jit(solution)/shard_map/all_gather | solution.py:92
  16.4 138.3 %all-to-all-start = ((bf16[256,3,8,256]{0,3,1,2:T(8,128)(2,1)}), bf16[256,3,8,256]{0,3,1,2:T(8,128)(2,1)}, u32[]{:S(2)}, u32[]{:S(2)}) async-start(bf16[256,3,8,256]{0,3,1,2:T(8,128)(2,1)} %copy.124), calls=%async_computation | async-start | bytes 6291456 | tf_op jit(solution)/shard_map/all_to_all | solution.py:79
  21.7 141.5 %copy-start.39 = (s32[1,4]{1,0:T(1,128)S(1)}, s32[1,4]{1,0:T(1,128)}, u32[]{:S(2)}) copy-start(s32[1,4]{1,0:T(1,128)} %param.16) | copy-start | bytes 52
  21.7 143.3 %copy-start.7 = (bf16[256,2048]{1,0:T(8,128)(2,1)S(1)}, bf16[256,2048]{1,0:T(8,128)(2,1)}, u32[]{:S(2)}) copy-start(bf16[256,2048]{1,0:T(8,128)(2,1)} %param.29) | copy-start | bytes 3145732
  21.7 144.5 %copy-start.33 = (bf16[768]{0:T(1024)(128)(2,1)S(1)}, bf16[768]{0:T(1024)(128)(2,1)}, u32[]{:S(2)}) copy-start(bf16[768]{0:T(1024)(128)(2,1)} %param.18) | copy-start | bytes 4612
  21.8 144.7 %copy-start.34 = (bf16[256]{0:T(256)(128)(2,1)S(1)}, bf16[256]{0:T(256)(128)(2,1)}, u32[]{:S(2)}) copy-start(bf16[256]{0:T(256)(128)(2,1)} %param.20) | copy-start | bytes 1540
  21.8 144.9 %copy-start.35 = (bf16[256]{0:T(256)(128)(2,1)S(1)}, bf16[256]{0:T(256)(128)(2,1)}, u32[]{:S(2)}) copy-start(bf16[256]{0:T(256)(128)(2,1)} %param.24) | copy-start | bytes 1540
  21.8 145.1 %copy-start.36 = (bf16[256]{0:T(256)(128)(2,1)S(1)}, bf16[256]{0:T(256)(128)(2,1)}, u32[]{:S(2)}) copy-start(bf16[256]{0:T(256)(128)(2,1)} %param.25) | copy-start | bytes 1540
  21.8 145.3 %copy-start.37 = (bf16[256]{0:T(256)(128)(2,1)S(1)}, bf16[256]{0:T(256)(128)(2,1)}, u32[]{:S(2)}) copy-start(bf16[256]{0:T(256)(128)(2,1)} %param.26) | copy-start | bytes 1540
  21.8 145.5 %copy-start.38 = (bf16[256]{0:T(256)(128)(2,1)S(1)}, bf16[256]{0:T(256)(128)(2,1)}, u32[]{:S(2)}) copy-start(bf16[256]{0:T(256)(128)(2,1)} %param.27) | copy-start | bytes 1540
  21.8 145.7 %copy-start.40 = (bf16[256]{0:T(256)(128)(2,1)S(1)}, bf16[256]{0:T(256)(128)(2,1)}, u32[]{:S(2)}) copy-start(bf16[256]{0:T(256)(128)(2,1)} %param.28) | copy-start | bytes 1540
  21.8 307.8 %copy-start.32 = (bf16[1024]{0:T(1024)(128)(2,1)S(1)}, bf16[1024]{0:T(1024)(128)(2,1)}, u32[]{:S(2)}) copy-start(bf16[1024]{0:T(1024)(128)(2,1)} %param.22) | copy-start | bytes 6148
  154.8 192.3 %all-to-all-start.1 = ((bf16[256,8,1024]{0,2,1:T(8,128)(2,1)}), bf16[256,8,1024]{0,2,1:T(8,128)(2,1)}, u32[]{:S(2)}, u32[]{:S(2)}) async-start(bf16[256,8,1024]{0,2,1:T(8,128)(2,1)} %bitcast.103), calls=%async_computation.1 | async-start | bytes 8388608 | tf_op jit(solution)/shard_map/all_to_all | solution.py:78
  163.2 259.5 %all-gather.8.cloned.1.call-start = ((), (), s32[]{:S(2)}) async-start(), calls=%async_computation.8 | async-start | bytes 9437184 | tf_op jit(solution)/shard_map/all_gather | solution.py:95
  166.1 770.2 %reduce-scatter.5.cloned.1.call-start = ((), (), s32[]{:S(2)}) async-start(), calls=%async_computation.9 | async-start | bytes 9437184 | tf_op jit(solution)/shard_map/reduce_scatter | solution.py:155
  340.1 102.7 %copy-start.26 = (f32[1,2,8,128]{3,1,2,0:T(2,128)}, f32[1,2,8,128]{3,1,2,0:T(2,128)S(1)}, u32[]{:S(2)}) copy-start(f32[1,2,8,128]{3,1,2,0:T(2,128)S(1)} %copy.161) | copy-start | bytes 24580
  340.2 21.4 %copy-start.20 = (f32[1,2,8,128]{3,1,2,0:T(2,128)}, f32[1,2,8,128]{3,1,2,0:T(2,128)S(1)}, u32[]{:S(2)}) copy-start(f32[1,2,8,128]{3,1,2,0:T(2,128)S(1)} %copy.157) | copy-start | bytes 24580
  353.5 5.8 copy-start.1
  361.6 7.1 copy-start.15
  365.3 3.4 copy-start.3
  422.7 8.8 copy-start.24
  422.7 5.9 copy-start.19
  428.7 1.9 copy-start.18
  430.6 1.7 copy-start.17
  430.6 2.6 copy-start.16
  434.3 8.6 slice-start
  434.3 8.6 copy-start.6
  439.5 3.4 slice-start.1
  441.2 13.2 %slice-start.2 = ((s8[8388608]{0:T(1024)(128)(4,1)}), s8[4194304]{0:T(1024)(128)(4,1)S(1)}, s32[]{:S(2)}) async-start(s8[8388608]{0:T(1024)(128)(4,1)} %bitcast.100), calls=%async_computation.13 | async-start | bytes 8388608
  442.9 11.5 %slice-start.3 = ((s8[8388608]{0:T(1024)(128)(4,1)}), s8[4194304]{0:T(1024)(128)(4,1)S(1)}, s32[]{:S(2)}) async-start(s8[8388608]{0:T(1024)(128)(4,1)} %bitcast.100), calls=%async_computation.14 | async-start | bytes 8388608
  487.5 14.4 %copy-start.11 = (f32[8,256,32]{2,1,0:T(8,128)S(1)}, f32[8,256,32]{2,1,0:T(8,128)}, u32[]{:S(2)}) copy-start(f32[8,256,32]{2,1,0:T(8,128)} %get-tuple-element.42) | copy-start | bytes 786436
  487.5 14.4 %copy-start.12 = (f32[8,256,32]{2,1,0:T(8,128)S(1)}, f32[8,256,32]{2,1,0:T(8,128)}, u32[]{:S(2)}) copy-start(f32[8,256,32]{2,1,0:T(8,128)} %get-tuple-element.43) | copy-start | bytes 786436
  487.5 14.4 %copy-start.13 = (f32[8,256,32]{2,1,0:T(8,128)S(1)}, f32[8,256,32]{2,1,0:T(8,128)}, u32[]{:S(2)}) copy-start(f32[8,256,32]{2,1,0:T(8,128)} %get-tuple-element.46) | copy-start | bytes 786436
  487.5 14.4 %copy-start.14 = (f32[8,256,32]{2,1,0:T(8,128)S(1)}, f32[8,256,32]{2,1,0:T(8,128)}, u32[]{:S(2)}) copy-start(f32[8,256,32]{2,1,0:T(8,128)} %get-tuple-element.47) | copy-start | bytes 786436
  501.9 11.9 %copy-start.21 = (f32[1,2,8,128]{3,1,2,0:T(2,128)S(1)}, f32[1,2,8,128]{3,1,2,0:T(2,128)}, u32[]{:S(2)}) copy-start(f32[1,2,8,128]{3,1,2,0:T(2,128)} %copy-done.20) | copy-start | bytes 24580
  533.7 404.7 %reduce-scatter.3.cloned.1.call-start = ((), (), s32[]{:S(2)}) async-start(), calls=%async_computation.7 | async-start | bytes 9437184 | tf_op jit(solution)/shard_map/reduce_scatter | solution.py:122
  587.3 14.4 %copy-start.27 = (f32[1,2,8,128]{3,1,2,0:T(2,128)S(1)}, f32[1,2,8,128]{3,1,2,0:T(2,128)}, u32[]{:S(2)}) copy-start(f32[1,2,8,128]{3,1,2,0:T(2,128)} %copy-done.26) | copy-start | bytes 24580
  594.5 153.8 %all-to-all-start.2 = ((bf16[2048,3,1,256]{3,1,2,0:T(4,128)(2,1)}), bf16[2048,3,1,256]{3,1,2,0:T(4,128)(2,1)}, u32[]{:S(2)}, u32[]{:S(2)}) async-start(bf16[2048,3,1,256]{3,1,2,0:T(4,128)(2,1)} %copy.140), calls=%async_computation.4 | async-start | bytes 8388608 | tf_op jit(solution)/shard_map/all_to_all | solution.py:168
  748.3 129.0 %all-to-all-start.3 = ((bf16[8,256,1024]{2,1,0:T(8,128)(2,1)}), bf16[8,256,1024]{2,1,0:T(8,128)(2,1)}, u32[]{:S(2)}, u32[]{:S(2)}) async-start(bf16[8,256,1024]{2,1,0:T(8,128)(2,1)} %bitcast.112), calls=%async_computation.5 | async-start | bytes 8388608 | tf_op jit(solution)/shard_map/all_to_all | solution.py:167
  757.4 368.8 %all-reduce.4.cloned.1.call-start = ((), (), s32[]{:S(2)}) async-start(), calls=%async_computation.10 | async-start | bytes 25165824 | tf_op jit(solution)/shard_map/psum | solution.py:189
  757.4 6.9 copy-start.10
  882.1 37.7 %copy-start.28 = (f32[1024]{0:T(1024)S(1)}, f32[1024]{0:T(1024)}, u32[]{:S(2)}) copy-start(f32[1024]{0:T(1024)} %get-tuple-element.28) | copy-start | bytes 12292
  882.1 56.3 %copy-start.8 = (bf16[256,2048]{1,0:T(8,128)(2,1)S(1)}, bf16[256,2048]{1,0:T(8,128)(2,1)}, u32[]{:S(2)}) copy-start(bf16[256,2048]{1,0:T(8,128)(2,1)} %param.29) | copy-start | bytes 3145732
  882.1 56.3 %copy-start.31 = (pred[256]{0:T(512)(128)(4,1)S(1)}, pred[256]{0:T(512)(128)(4,1)}, u32[]{:S(2)}) copy-start(pred[256]{0:T(512)(128)(4,1)} %copy-done.30) | copy-start | bytes 772
  936.4 206.9 %copy-start.29 = (f32[256]{0:T(256)}, f32[256]{0:T(256)S(1)}, u32[]{:S(2)}) copy-start(f32[256]{0:T(256)S(1)} %get-tuple-element.90) | copy-start | bytes 3076
  1126.2 8.3 copy-start.5
  1134.5 4.4 copy-start.4
  (7 other events, 6.4 us)
Sparse Core Ops, SparseCore 0:
  9.6 144.9 all-gather.5
  166.3 144.5 all-gather.7
  533.8 114.8 reduce-scatter.4
  651.5 213.6 reduce-scatter.2
  882.2 243.9 all-reduce.3

commit v2 on v0

--- a/solution.py
+++ b/solution.py
@@ -4,14 +4,20 @@
 import jax
 import jax.numpy as jnp
 from jax import lax
+from jax.experimental import pallas as pl
+from jax.experimental.pallas import tpu as pltpu
 from jax.sharding import PartitionSpec as P
 
 H = 8
 ROT = 64
-
+DOCS = 4
+LANES = 128
+VMEM_LIMIT = 60 * 1024 * 1024
 
 epsilon = 1e-05
 masked_value = -1e30
+f32 = jnp.float32
+bf16 = jnp.bfloat16
 
 
 def normalize(values):
@@ -27,17 +33,17 @@
     passed = index[:, None] >= ends[None, :]
     document = jnp.sum(passed.astype(jnp.int32), axis=1)
     begin = jnp.max(jnp.where(passed, ends[None, :], 0), axis=1)
-    position = (index - begin).astype(jnp.float32)
+    position = (index - begin).astype(f32)
     allowed = (document[:, None] == document[None, :]) & (index[None, :] <= index[:, None])
     return (position, allowed, index < ends[-1])
 
 
 def rotary_tables(position, rotary):
     half = rotary // 2
-    freqs = jnp.exp(-jnp.arange(half, dtype=jnp.float32) * (2.0 / rotary) * math.log(10000.0))
-    angles = position[:, None] * freqs[None, :]
-    angles = jnp.concatenate([angles, angles], axis=1)
-    return (jnp.cos(angles)[:, None, :], jnp.sin(angles)[:, None, :])
+    freqs = jnp.exp(-jnp.arange(half, dtype=f32) * (2.0 / rotary) * math.log(10000.0))
+    angles = position[..., None] * freqs
+    angles = jnp.concatenate([angles, angles], axis=-1)
+    return (jnp.cos(angles), jnp.sin(angles))
 
 
 def rotate(values, cosine, sine, rotary):
@@ -55,23 +61,19 @@
     return jnp.concatenate([front * cosine + backward, grads[..., rotary:]], axis=-1)
 
 
+def right_trans(left, right):
+    return lax.dot_general(left, right, (((1,), (1,)), ((), ())), preferred_element_type=f32)
+
+
+def left_trans(left, right):
+    return lax.dot_general(left, right, (((0,), (0,)), ((), ())), preferred_element_type=f32)
+
+
 def masked_scores(query_low, keys_low, allowed, factor):
     scores = (
         jnp.einsum("qhd,khd->hqk", query_low, keys_low, preferred_element_type=jnp.float32) * factor
     )
     return jnp.where(allowed[None], scores, masked_value)
-
-
-def right_trans(left, right):
-    return lax.dot_general(
-        left, right, (((1,), (1,)), ((), ())), preferred_element_type=jnp.float32
-    )
-
-
-def left_trans(left, right):
-    return lax.dot_general(
-        left, right, (((0,), (0,)), ((), ())), preferred_element_type=jnp.float32
-    )
 
 
 def weight_sums(left, right):
@@ -105,6 +107,7 @@
     factor = 1.0 / math.sqrt(headsize)
     position, allowed, live = layout(document_ends[0], count)
     cosine, sine = rotary_tables(position, ROT)
+    cosine, sine = cosine[:, None, :], sine[:, None, :]
     (
         full_projector,
         full_combiner,
@@ -288,6 +291,486 @@
     )
 
 
+def lane_half(shape):
+    return lax.broadcasted_iota(jnp.int32, shape, 1) < ROT // 2
+
+
+def turn(front, signed):
+    moved = jnp.where(
+        lane_half(front.shape),
+        pltpu.roll(front, LANES - ROT // 2, 1),
+        pltpu.roll(front, ROT // 2, 1),
+    )
+    return moved * signed
+
+
+def rotated(values, cosine, signed):
+    front = values[:, :LANES]
+    return jnp.concatenate([front * cosine + turn(front, signed), values[:, LANES:]], axis=1)
+
+
+def unrotated(grads, cosine, signed):
+    front = grads[:, :LANES]
+    return jnp.concatenate([front * cosine - turn(front, signed), grads[:, LANES:]], axis=1)
+
+
+def block_allowed(ends_ref, block, count):
+    row = lax.broadcasted_iota(jnp.int32, (count, 1), 0)
+    column = lax.broadcasted_iota(jnp.int32, (1, count), 1)
+    row_doc = jnp.zeros((count, 1), jnp.int32)
+    column_doc = jnp.zeros((1, count), jnp.int32)
+    for i in range(DOCS):
+        end = ends_ref[block, i]
+        row_doc += (row >= end).astype(jnp.int32)
+        column_doc += (column >= end).astype(jnp.int32)
+    return (row_doc == column_doc) & (column <= row)
+
+
+def dot(left, right):
+    return jnp.dot(left, right, preferred_element_type=f32)
+
+
+def softmax(q, k, allowed):
+    scores = right_trans(q, k) * (1.0 / math.sqrt(q.shape[1]))
+    scores = jnp.where(allowed, scores, masked_value)
+    raised = jnp.exp(scores - jnp.max(scores, axis=1, keepdims=True))
+    return raised / jnp.sum(raised, axis=1, keepdims=True)
+
+
+def forward_kernel(
+    ends_ref, x_ref, cos_ref, sin_ref, norms_ref, pbias_ref, ebias_ref,
+    proj_ref, exp_ref, comb_ref, cont_ref,
+    h1_ref, h2_ref, qkv_ref, ca_ref, slope_ref, part_ref,
+):
+    block = pl.program_id(0)
+    count, width = x_ref.shape
+    head = comb_ref.shape[0]
+    units = exp_ref.shape[1]
+    normed, _ = normalize(x_ref[...].astype(f32))
+    first = (normed * norms_ref[0:1, :] + norms_ref[1:2, :]).astype(bf16)
+    h1_ref[...] = first
+    second = (normed * norms_ref[2:3, :] + norms_ref[3:4, :]).astype(bf16)
+    h2_ref[...] = second
+    cosine, signed = cos_ref[...], sin_ref[...]
+    mixed = dot(first, proj_ref[...]) + pbias_ref[...]
+    q = rotated(mixed[:, :head], cosine, signed).astype(bf16)
+    k = rotated(mixed[:, head : 2 * head], cosine, signed).astype(bf16)
+    v = mixed[:, 2 * head :].astype(bf16)
+    qkv_ref[:, :head] = q
+    qkv_ref[:, head : 2 * head] = k
+    qkv_ref[:, 2 * head :] = v
+    probs = softmax(q, k, block_allowed(ends_ref, block, count)).astype(bf16)
+    ca_ref[:, :head] = dot(probs, v).astype(bf16)
+    tile = min(256, units)
+    for start in range(0, units, tile):
+        hidden = dot(second, exp_ref[:, start : start + tile]) + ebias_ref[:, start : start + tile]
+        below = 0.5 + 0.5 * lax.erf(hidden * math.sqrt(0.5))
+        ca_ref[:, head + start : head + start + tile] = (hidden * below).astype(bf16)
+        density = jnp.exp(hidden * hidden * -0.5) * (1.0 / math.sqrt(2.0 * math.pi))
+        slope_ref[:, start : start + tile] = (below + hidden * density).astype(bf16)
+    tile = min(512, width)
+    for start in range(0, width, tile):
+        cut = slice(start, start + tile)
+        part = dot(ca_ref[:, :head], comb_ref[:, cut]) + dot(ca_ref[:, head:], cont_ref[:, cut])
+        part_ref[:, cut] = part.astype(bf16)
+
+
+def backward_kernel(
+    ends_ref, x_ref, up_ref, cos_ref, sin_ref, norms_ref, qkv_ref, slope_ref,
+    proj_ref, exp_ref, comb_ref, cont_ref,
+    dh_ref, dm_ref, dn_ref, sums_ref, hbias_ref, mbias_ref,
+):
+    block = pl.program_id(0)
+    count, width = x_ref.shape
+    head = comb_ref.shape[0]
+    units = exp_ref.shape[1]
+    up = up_ref[...]
+
+    @pl.when(block == 0)
+    def _():
+        sums_ref[...] = jnp.zeros_like(sums_ref)
+        hbias_ref[...] = jnp.zeros_like(hbias_ref)
+        mbias_ref[...] = jnp.zeros_like(mbias_ref)
+
+    d_context = right_trans(up, comb_ref[...]).astype(bf16)
+    q, k, v = qkv_ref[:, :head], qkv_ref[:, head : 2 * head], qkv_ref[:, 2 * head :]
+    probs = softmax(q, k, block_allowed(ends_ref, block, count))
+    d_probs = right_trans(d_context, v)
+    d_v = left_trans(probs.astype(bf16), d_context)
+    d_s = probs * (d_probs - jnp.sum(d_probs * probs, axis=1, keepdims=True))
+    d_s = d_s.astype(bf16)
+    factor = 1.0 / math.sqrt(head)
+    cosine, signed = cos_ref[...], sin_ref[...]
+    d_q = unrotated(dot(d_s, k) * factor, cosine, signed).astype(bf16)
+    d_k = unrotated(left_trans(d_s, q) * factor, cosine, signed).astype(bf16)
+    dm_ref[:, :head] = d_q
+    dm_ref[:, head : 2 * head] = d_k
+    dm_ref[:, 2 * head :] = d_v.astype(bf16)
+    mbias_ref[...] += jnp.sum(dm_ref[...].astype(f32), axis=0, keepdims=True)
+    tile = min(256, units)
+    for start in range(0, units, tile):
+        cut = slice(start, start + tile)
+        d_hidden = (right_trans(up, cont_ref[cut, :]) * slope_ref[:, cut].astype(f32)).astype(bf16)
+        dh_ref[:, cut] = d_hidden
+        hbias_ref[:, cut] += jnp.sum(d_hidden.astype(f32), axis=0, keepdims=True)
+    x = x_ref[...].astype(f32)
+    centre = jnp.mean(x, axis=1, keepdims=True)
+    spread = jnp.mean((x - centre) * (x - centre), axis=1, keepdims=True)
+    inverse = lax.rsqrt(spread + epsilon)
+    tile = min(256, width)
+    for start in range(0, width, tile):
+        cut = slice(start, start + tile)
+        normed = (x_ref[:, cut].astype(f32) - centre) * inverse
+        d_first = right_trans(dm_ref[...], proj_ref[cut, :])
+        d_second = right_trans(dh_ref[...], exp_ref[cut, :])
+        dn_ref[:, cut] = (
+            d_first * norms_ref[0:1, cut] + d_second * norms_ref[2:3, cut]
+        ).astype(bf16)
+        sums_ref[0:1, cut] += jnp.sum(d_first * normed, axis=0, keepdims=True)
+        sums_ref[1:2, cut] += jnp.sum(d_first, axis=0, keepdims=True)
+        sums_ref[2:3, cut] += jnp.sum(d_second * normed, axis=0, keepdims=True)
+        sums_ref[3:4, cut] += jnp.sum(d_second, axis=0, keepdims=True)
+
+
+def rows_spec(count, columns):
+    return pl.BlockSpec((count, columns), lambda i, *_: (i, 0))
+
+
+def whole_spec(array):
+    return pl.BlockSpec(array.shape, lambda i, *_: (0, 0), pipeline_mode=pl.Buffered(1))
+
+
+def acc_spec(rows, columns):
+    return pl.BlockSpec((rows, columns), lambda i, *_: (0, 0))
+
+
+def forward_block(count, ends, x, cosine, signed, norms, pbias, ebias, proj, exp, comb, cont):
+    slots, width = x.shape
+    units, mix, head = exp.shape[1], proj.shape[1], comb.shape[0]
+    flops = 2 * slots * width * (mix + 2 * units + head)
+    wide = [width, width, mix, head + units, units, width]
+    return pl.pallas_call(
+        forward_kernel,
+        grid_spec=pltpu.PrefetchScalarGridSpec(
+            num_scalar_prefetch=1,
+            grid=(slots // count,),
+            in_specs=[
+                rows_spec(count, width), rows_spec(count, LANES), rows_spec(count, LANES),
+            ] + [whole_spec(a) for a in (norms, pbias, ebias, proj, exp, comb, cont)],
+            out_specs=[rows_spec(count, w) for w in wide],
+        ),
+        out_shape=[jax.ShapeDtypeStruct((slots, w), bf16) for w in wide],
+        compiler_params=pltpu.CompilerParams(vmem_limit_bytes=VMEM_LIMIT),
+        cost_estimate=pl.CostEstimate(
+            flops=flops, bytes_accessed=2 * slots * sum(wide), transcendentals=0
+        ),
+    )(ends, x, cosine, signed, norms, pbias, ebias, proj, exp, comb, cont)
+
+
+def backward_block(count, ends, x, up, cosine, signed, norms, qkv, slope, proj, exp, comb, cont):
+    slots, width = x.shape
+    units, mix, head = exp.shape[1], proj.shape[1], comb.shape[0]
+    flops = 2 * slots * width * (mix + 2 * units + head)
+    return pl.pallas_call(
+        backward_kernel,
+        grid_spec=pltpu.PrefetchScalarGridSpec(
+            num_scalar_prefetch=1,
+            grid=(slots // count,),
+            in_specs=[
+                rows_spec(count, width), rows_spec(count, width),
+                rows_spec(count, LANES), rows_spec(count, LANES), whole_spec(norms),
+                rows_spec(count, mix), rows_spec(count, units),
+            ] + [whole_spec(a) for a in (proj, exp, comb, cont)],
+            out_specs=[rows_spec(count, w) for w in (units, mix, width)]
+            + [acc_spec(4, width), acc_spec(1, units), acc_spec(1, mix)],
+        ),
+        out_shape=[jax.ShapeDtypeStruct((slots, w), bf16) for w in (units, mix, width)]
+        + [jax.ShapeDtypeStruct(s, f32) for s in ((4, width), (1, units), (1, mix))],
+        compiler_params=pltpu.CompilerParams(vmem_limit_bytes=VMEM_LIMIT),
+        cost_estimate=pl.CostEstimate(
+            flops=flops, bytes_accessed=2 * slots * (3 * width + 2 * units), transcendentals=0
+        ),
+    )(ends, x, up, cosine, signed, norms, qkv, slope, proj, exp, comb, cont)
+
+
+def links(move):
+    pairs = []
+    for y in range(2):
+        for x in range(2):
+            for z in range(4):
+                for c in range(2):
+                    ty, tx, tz, tc = move(y, x, z, c)
+                    pairs.append((((y * 2 + x) * 4 + z) * 2 + c, ((ty * 2 + tx) * 4 + tz % 4) * 2 + tc))
+    return pairs
+
+
+def send(value, move):
+    return lax.ppermute(value, ("rep", "shard"), links(move))
+
+
+def by_core(value):
+    return send(value, lambda y, x, z, c: (y, x, z, 1 - c))
+
+
+def by_x(value):
+    return send(value, lambda y, x, z, c: (y, 1 - x, z, c))
+
+
+def by_y(value):
+    return send(value, lambda y, x, z, c: (1 - y, x, z, c))
+
+
+def by_z(value, step):
+    return send(value, lambda y, x, z, c: (y, x, z + step, c))
+
+
+def pick(value, index, axis):
+    return lax.dynamic_index_in_dim(value, index, axis=axis, keepdims=False)
+
+
+def put(buffer, value, *index):
+    start = index + (0,) * (buffer.ndim - len(index))
+    return lax.dynamic_update_slice(
+        buffer, value.reshape((1,) * len(index) + buffer.shape[len(index):]).astype(buffer.dtype), start
+    )
+
+
+def added(a, b):
+    return (a.astype(f32) + b.astype(f32)).astype(bf16)
+
+
+def plane_sums(value, y, x):
+    a, b = value[:, :, 0], value[:, :, 1]
+    got = by_x(pick(a, 1 - x, 1))
+    a = added(pick(a, x, 1), got)
+    got = by_y(pick(b, 1 - y, 0))
+    b = added(pick(b, y, 0), got)
+    got = by_y(pick(a, 1 - y, 0))
+    a = added(pick(a, y, 0), got)
+    got = by_x(pick(b, 1 - x, 0))
+    b = added(pick(b, x, 0), got)
+    return a, b
+
+
+def plane_gather(a, b, y, x, place):
+    other_x, other_y = 1 - x, 1 - y
+    ay = by_y(a)
+    bx = by_x(b)
+    ax = by_x(jnp.stack([a, ay]))
+    by = by_y(jnp.stack([b, bx]))
+    place(y, x, 0, a)
+    place(y, x, 1, b)
+    place(other_y, x, 0, ay)
+    place(y, other_x, 1, bx)
+    place(y, other_x, 0, ax[0])
+    place(other_y, other_x, 0, ax[1])
+    place(other_y, x, 1, by[0])
+    place(other_y, other_x, 1, by[1])
+
+
+def sharded_heads(
+    tokens, document_ends, projector, projbias, combiner, combbias, expander, expbias,
+    contractor, contbias, attendgain, attendshift, feedgain, feedshift, cotangent,
+):
+    count, width = tokens.shape
+    n = lax.axis_size("shard")
+    rep = lax.axis_index("rep")
+    me = lax.axis_index("shard")
+    y, x, z, c = rep // 2, rep % 2, me // 2, me % 2
+    head = width // H
+    mix = 3 * head
+    rows = width // n
+    quarter = rows // 4
+    units = expbias.shape[0]
+    wide = projbias.shape[0]
+    both = units + mix
+
+    mine = lax.dynamic_slice_in_dim(expander, rep * quarter, quarter, 0).reshape(quarter, n, units)
+    mine_p = lax.dynamic_slice_in_dim(projector, rep * quarter, quarter, 0)
+    mine_p = mine_p.reshape(quarter, 3, n, head).transpose(0, 2, 1, 3).reshape(quarter, n, mix)
+    cols = jnp.concatenate([mine, mine_p], axis=2).transpose(1, 0, 2).reshape(4, 2, quarter, both)
+    far = [by_z(pick(cols, (z + step) % 4, 0), step) for step in (1, 2, 3)]
+    far = jnp.stack(far)
+    kept = pick(far, c, 1)
+    near = jnp.concatenate(
+        [
+            lax.dynamic_slice_in_dim(expander, (2 * z + 1 - c) * units, units, 1),
+            lax.dynamic_slice_in_dim(
+                projector.reshape(rows, 3, width), (2 * z + 1 - c) * head, head, 2
+            ).reshape(rows, mix),
+        ],
+        axis=1,
+    )
+    near = by_core(near)
+    passed = by_core(pick(far, 1 - c, 1))
+    exp_cols = jnp.zeros((4, 2, 2, 2, quarter, units), bf16)
+    proj_cols = jnp.zeros((4, 2, 2, 2, quarter, mix), bf16)
+    own = lax.dynamic_slice_in_dim(expander, me * units, units, 1)
+    own_p = lax.dynamic_slice_in_dim(projector.reshape(rows, 3, width), me * head, head, 2)
+    exp_cols = put(exp_cols, own, z, c)
+    exp_cols = put(exp_cols, near[:, :units], z, 1 - c)
+    proj_cols = put(proj_cols, own_p.reshape(rows, mix), z, c)
+    proj_cols = put(proj_cols, near[:, units:], z, 1 - c)
+
+    def place(py, px, half, value):
+        nonlocal exp_cols, proj_cols
+        core = c if half == 0 else 1 - c
+        for i, step in enumerate((1, 2, 3)):
+            source = (z - step) % 4
+            exp_cols = put(exp_cols, value[i, :, :units], source, core, py, px)
+            proj_cols = put(proj_cols, value[i, :, units:], source, core, py, px)
+
+    plane_gather(kept, passed, y, x, place)
+    exp_cols = exp_cols.reshape(width, units)
+    proj_cols = proj_cols.reshape(width, mix)
+
+    vectors = jnp.concatenate(
+        [projbias, combbias, contbias, attendgain, attendshift, feedgain, feedshift,
+         document_ends[0].astype(bf16)]
+    )
+    extra = 16
+    vectors = jnp.pad(vectors, (0, extra * width - vectors.shape[0])).reshape(extra, width)
+    chain = [jnp.concatenate([tokens, vectors], axis=0)]
+    for _ in range(3):
+        chain.append(by_z(chain[-1], 1))
+    mine = jnp.stack(chain)
+    others = by_core(mine)
+    slots = jnp.stack([mine, others], axis=1).reshape(n, count + extra, width)
+    x_all = slots[:, :count].reshape(n * count, width)
+    vectors = slots[:, count:].reshape(n, extra * width)
+    order = ((z - jnp.arange(4)) % 4)[:, None] * 2 + jnp.stack([c, 1 - c])[None, :]
+    order = order.reshape(-1)
+    ends = vectors[:, wide + 6 * rows : wide + 6 * rows + DOCS].astype(jnp.int32)
+    placed = jnp.zeros((n, wide + 6 * rows), bf16).at[order].set(vectors[:, : wide + 6 * rows])
+    full_projbias = placed[:, :wide].reshape(3, n, head)
+    my_projbias = pick(full_projbias, me, 1).reshape(1, mix).astype(f32)
+    gains = placed[:, wide:].reshape(n, 6, rows).transpose(1, 0, 2).reshape(6, width).astype(f32)
+    norms = gains[2:]
+
+    _, _, live = layout(document_ends[0], count)
+    upstream = jnp.where(live[:, None], cotangent, jnp.zeros_like(cotangent))
+    upstream, _ = lax.optimization_barrier((upstream, chain[-1]))
+    chain = [upstream]
+    for _ in range(3):
+        chain.append(by_z(chain[-1], 1))
+    mine = jnp.stack(chain)
+    others = by_core(mine)
+    up_all = jnp.stack([mine, others], axis=1).reshape(n * count, width)
+
+    position = jax.vmap(lambda e: layout(e, count)[0])(ends).reshape(-1)
+    half = ROT // 2
+    freqs = jnp.exp(-jnp.arange(half, dtype=f32) * (2.0 / ROT) * math.log(10000.0))
+    angles = position[:, None] * freqs[None, :]
+    sine, cosine = jnp.sin(angles), jnp.cos(angles)
+    still = jnp.ones((n * count, LANES - ROT), f32)
+    cosine = jnp.concatenate([cosine, cosine, still], axis=1)
+    signed = jnp.concatenate([-sine, sine, 0.0 * still], axis=1)
+
+    h1, h2, qkv, ca, slope, part = forward_block(
+        count, ends, x_all, cosine, signed, norms, my_projbias, expbias.astype(f32)[None],
+        proj_cols, exp_cols, combiner, contractor,
+    )
+
+    def group_sums(part):
+        part = part.reshape(4, 2, count, width)
+        acc = added(part[:, 0], by_core(part[:, 1]))
+        total = acc[3]
+        for slot in (2, 1, 0):
+            total = added(acc[slot], by_z(total, -1)) if slot else (
+                acc[0].astype(f32) + by_z(total, -1).astype(f32)
+            )
+        return total
+
+    summed = group_sums(part)
+    floated = tokens.astype(f32)
+    block_output = floated + jnp.where(
+        live[:, None], summed + (gains[0] + gains[1]), 0.0
+    )
+    block_output = block_output.astype(bf16)
+
+    low = left_trans(ca, up_all).astype(bf16)
+    low = low.reshape(2, 2, 2, (head + units) // 8, width)
+    low_a, low_b = plane_sums(low, y, x)
+    out_bias = jnp.sum(up_all, axis=0, dtype=f32)
+
+    dh, dm, dn, sums, hidden_bias, mixed_bias = backward_block(
+        count, ends, x_all, up_all, cosine, signed, norms, qkv, slope,
+        proj_cols, exp_cols, combiner, contractor,
+    )
+    high = jnp.concatenate(
+        [left_trans(h2, dh).astype(bf16), left_trans(h1, dm).astype(bf16)], axis=1
+    )
+    high = high.reshape(n, 2, 2, 2, quarter // 2, both).transpose(1, 2, 3, 0, 4, 5)
+    high_a, high_b = plane_sums(high, y, x)
+
+    low_out = jnp.zeros((2, 2, 2, (head + units) // 8, width), f32)
+
+    def place_low(py, px, half, value):
+        nonlocal low_out
+        low_out = put(low_out, value, py, px, half)
+
+    plane_gather(low_a, low_b, y, x, place_low)
+    low_out = low_out.reshape(head + units, width)
+
+    turned = jnp.stack([high_a, high_b], axis=1).reshape(4, 2, quarter, both)
+    far = [pick(turned, z, 0)] + [by_z(pick(turned, (z + step) % 4, 0), step) for step in (1, 2, 3)]
+    far = jnp.stack(far)
+    kept = pick(far, c, 1)
+    passed = by_core(pick(far, 1 - c, 1))
+    exp_rows = jnp.zeros((4, 2, quarter, units), bf16)
+    proj_rows = jnp.zeros((4, 2, quarter, mix), bf16)
+    for i in range(4):
+        source = (z - i) % 4
+        for core, value in ((c, kept[i]), (1 - c, passed[i])):
+            exp_rows = put(exp_rows, value[:, :units], source, core)
+            proj_rows = put(proj_rows, value[:, units:], source, core)
+    exp_rows = exp_rows.reshape(n, quarter, units).transpose(1, 0, 2).reshape(quarter, n * units)
+    proj_rows = (
+        proj_rows.reshape(n, quarter, 3, head).transpose(1, 2, 0, 3).reshape(quarter, 3 * width)
+    )
+    turned = jnp.concatenate([exp_rows, proj_rows], axis=1)
+    exp_out = jnp.zeros((2, 2, 2, quarter // 2, n * units), f32)
+    proj_out = jnp.zeros((2, 2, 2, quarter // 2, 3 * width), f32)
+
+    def place_high(py, px, half, value):
+        nonlocal exp_out, proj_out
+        exp_out = put(exp_out, value[:, : n * units], py, px, half)
+        proj_out = put(proj_out, value[:, n * units :], py, px, half)
+
+    plane_gather(turned[: quarter // 2], turned[quarter // 2 :], y, x, place_high)
+    exp_out = exp_out.reshape(rows, n * units)
+    proj_out = proj_out.reshape(rows, 3 * width)
+
+    d_normed = group_sums(dn)
+    own_normed, own_inverse = normalize(floated)
+    grad = cotangent.astype(f32) + own_inverse * (
+        d_normed
+        - jnp.mean(d_normed, axis=1, keepdims=True)
+        - own_normed * jnp.mean(d_normed * own_normed, axis=1, keepdims=True)
+    )
+    input_gradient = grad.astype(bf16)
+
+    mixed_full = jnp.zeros((3, n, head), f32)
+    mixed_full = lax.dynamic_update_slice(mixed_full, mixed_bias.reshape(3, 1, head), (0, me, 0))
+    vector = jnp.concatenate(
+        [
+            mixed_full.reshape(n, wide),
+            sums.reshape(4, n, rows).transpose(1, 0, 2).reshape(n, 4 * rows),
+        ],
+        axis=1,
+    )
+    vector = lax.psum_scatter(vector, "shard", scatter_dimension=0, tiled=True)[0]
+    own_out = lax.dynamic_slice(out_bias, (me * rows,), (rows,))
+    vector = lax.psum(jnp.concatenate([vector, own_out, hidden_bias[0]]), "rep")
+    mixed_bias = vector[:wide]
+    s0, s1, s2, s3, out_bias = (vector[wide + i * rows : wide + (i + 1) * rows] for i in range(5))
+    hidden_bias = vector[wide + 5 * rows :]
+    return (
+        block_output, input_gradient, proj_out, mixed_bias, low_out[:head], out_bias,
+        exp_out, hidden_bias, low_out[head:], out_bias, s0, s1, s2, s3,
+    )
+
+
 def solution(mesh):
     placed = (
         P(("rep", "shard"), None),
@@ -307,7 +790,7 @@
         P(("rep", "shard"), None),
     )
     return jax.shard_map(
-        local,
+        sharded_heads if dict(mesh.shape) == {"rep": 4, "shard": H} else local,
         mesh=mesh,
         in_specs=placed,
         out_specs=(

time: 2150 us -> 841 us (0.39)
  waiting for transfers between devices: 1730 us -> 376 us
  matrix products: 194 us -> 39 us
  local copies, waits for them, and re-layouts: 20.6 us -> 141 us
  blocking collectives: 152 us -> 39.4 us
  Pallas kernels: 0 us -> 95.7 us
  starting transfers between devices: 0.36 us -> 49.8 us
  other arithmetic: 35.6 us -> 83.9 us
    reduce_scatter x4 -> x0, waiting for transfers between devices: 935 us -> none  [weight_sums(): lax.psum_scatter(left_trans(piece, right).astype(jnp.bfloat16), 'shard',...]
    all_gather x4 -> x0, waiting for transfers between devices: 669 us -> none  [the longest x1 255 us: local(): lax.all_gather(contractor, 'shard', axis=0, tiled=True)]
    ppermute x0 -> x45, waiting for transfers between devices: none -> 376 us  [send(): return lax.ppermute(value, ('rep', 'shard'), links(move))]
    dot_general x14 -> x0, matrix products: 140 us -> none  [the longest x4 62.3 us: right_trans(): lax.dot_general(left, right, (((1,), (1,)), ((), ())), preferred_element_...]
    psum x1 -> x0, waiting for transfers between devices: 121 us -> none  [local(): lax.psum(projector_part.astype(jnp.bfloat16), 'rep').astype(jnp.float32)]
    all_gather x8 -> x0, blocking collectives: 119 us -> none  [the longest x1 34.8 us: local(): lax.all_gather(expbias, 'shard', axis=0, tiled=True)]
    pallas_call x0 -> x2, Pallas kernels: none -> 95.7 us  [the longest x1 49.2 us: backward_block(): pl.pallas_call(backward_kernel, grid_spec=pltpu.PrefetchScalarGridSpec(nu...]
    ppermute x0 -> x45, starting transfers between devices: none -> 49.8 us  [send(): return lax.ppermute(value, ('rep', 'shard'), links(move))]
  transfers between devices with their start and end apart: 9 -> 45, of which waited for: 9 -> 22; matrix products, arithmetic and copies ran while one was open for 11% -> 30% of each run, Pallas kernels for 0% -> 12%
where the time goes in v2:
time: 841 us; the launch traced here: 827 us
  waiting for transfers between devices  376 us (45%)
  local copies, waits for them, and re-layouts  141 us (17%)
  Pallas kernels  95.7 us (11%)
  other arithmetic  83.9 us (10%)
  starting transfers between devices  49.8 us (6%)
  blocking collectives  39.4 us (5%)
  matrix products  39 us (5%)
    ppermute x45, waiting for transfers between devices, send(): return lax.ppermute(value, ('rep', 'shard'), links(move))  376 us
    ppermute x45, starting transfers between devices, send(): return lax.ppermute(value, ('rep', 'shard'), links(move))  49.8 us
    pallas_call x1, Pallas kernels, backward_block(): pl.pallas_call(backward_kernel, grid_spec=pltpu.PrefetchScalarGridSpec(nu...  49.2 us
    pallas_call x1, Pallas kernels, forward_block(): pl.pallas_call(forward_kernel, grid_spec=pltpu.PrefetchScalarGridSpec(num...  46.5 us
    dot_general x3, matrix products, left_trans(): lax.dot_general(left, right, (((0,), (0,)), ((), ())), preferred_element_...  39 us
    dynamic_update_slice x72, local copies, waits for them, and re-layouts, put(): lax.dynamic_update_slice(buffer, value.reshape((1,) * len(index) + buffer...  36.7 us
    unnamed x1, blocking collectives  25.8 us
    unnamed x97, local copies, waits for them, and re-layouts  17 us
  transfers between devices with their start and end apart: 45, of which 22 were waited for; matrix products, arithmetic and copies ran while one was open for 30% of the time, Pallas kernels for 12%

profile of v2, /device:TPU:10, one launch (start us, length us, event | category | flops | bytes accessed | tf_op | source)
XLA Modules:
  0.0 827.4 jit_solution(13874697944813554672)
XLA Ops:
  10.2 4.6 copy.145
  37.6 10.3 %collective-permute-done.6 = bf16[2,64,1792]{2,1,0:T(8,128)(2,1)} collective-permute-done((bf16[2,64,1792]{2,1,0:T(8,128)(2,1)}, bf16[2,64,1792]{2,1,0:T(8,128)(2,1)}, u32[]{:S(2)}, u32[]{:S(2)}) %collective-permute-start.6) | collective-permute-done | bytes 458784 | tf_op jit(solution)/shard_map/ppermute | solution.py:508
  47.9 48.4 %collective-permute-done.7 = bf16[2,64,1792]{2,1,0:T(8,128)(2,1)} collective-permute-done((bf16[2,64,1792]{2,1,0:T(8,128)(2,1)}, bf16[2,64,1792]{2,1,0:T(8,128)(2,1)}, u32[]{:S(2)}, u32[]{:S(2)}) %collective-permute-start.7) | collective-permute-done | bytes 458784 | tf_op jit(solution)/shard_map/ppermute | solution.py:508
  107.1 8.7 %collective-permute-done.9 = bf16[3,64,1792]{2,1,0:T(8,128)(2,1)S(1)} collective-permute-done((bf16[3,64,1792]{2,1,0:T(8,128)(2,1)S(1)}, bf16[3,64,1792]{2,1,0:T(8,128)(2,1)S(1)}, u32[]{:S(2)}, u32[]{:S(2)}) %collective-permute-start.9) | collective-permute-done | bytes 688160 | tf_op jit(solution)/shard_map/ppermute | solution.py:508
  125.8 36.6 %collective-permute-done.10 = bf16[3,64,1792]{2,1,0:T(8,128)(2,1)S(1)} collective-permute-done((bf16[3,64,1792]{2,1,0:T(8,128)(2,1)S(1)}, bf16[3,64,1792]{2,1,0:T(8,128)(2,1)S(1)}, u32[]{:S(2)}, u32[]{:S(2)}) %collective-permute-start.10) | collective-permute-done | bytes 688160 | tf_op jit(solution)/shard_map/ppermute | solution.py:508
  173.4 19.7 %collective-permute-done.2 = bf16[272,2048]{1,0:T(8,128)(2,1)S(1)} collective-permute-done((bf16[272,2048]{1,0:T(8,128)(2,1)S(1)}, bf16[272,2048]{1,0:T(8,128)(2,1)S(1)}, u32[]{:S(2)}, u32[]{:S(2)}) %collective-permute-start.2) | collective-permute-done | bytes 1114144 | tf_op jit(solution)/shard_map/ppermute | solution.py:508
  193.0 3.5 fusion.103
  200.8 23.3 %collective-permute-done.17 = bf16[256,2048]{1,0:T(8,128)(2,1)S(1)} collective-permute-done((bf16[256,2048]{1,0:T(8,128)(2,1)S(1)}, bf16[256,2048]{1,0:T(8,128)(2,1)S(1)}, u32[]{:S(2)}, u32[]{:S(2)}) %collective-permute-start.17) | collective-permute-done | bytes 1048608 | tf_op jit(solution)/shard_map/ppermute | solution.py:508
  227.6 21.3 %collective-permute-done.18 = bf16[256,2048]{1,0:T(8,128)(2,1)S(1)} collective-permute-done((bf16[256,2048]{1,0:T(8,128)(2,1)S(1)}, bf16[256,2048]{1,0:T(8,128)(2,1)S(1)}, u32[]{:S(2)}, u32[]{:S(2)}) %collective-permute-start.18) | collective-permute-done | bytes 1048608 | tf_op jit(solution)/shard_map/ppermute | solution.py:508
  252.6 21.6 %collective-permute-done.19 = bf16[256,2048]{1,0:T(8,128)(2,1)S(1)} collective-permute-done((bf16[256,2048]{1,0:T(8,128)(2,1)S(1)}, bf16[256,2048]{1,0:T(8,128)(2,1)S(1)}, u32[]{:S(2)}, u32[]{:S(2)}) %collective-permute-start.19) | collective-permute-done | bytes 1048608 | tf_op jit(solution)/shard_map/ppermute | solution.py:508
  274.3 3.7 fusion.102
  280.1 7.9 pad_maximum_fusion
  290.1 8.4 %slice.581 = bf16[8,256,2048]{2,1,0:T(8,128)(2,1)} slice(bf16[8,272,2048]{2,1,0:T(8,128)(2,1)} %bitcast.638), slice={[0:8], [0:256], [0:2048]} | slice | bytes 16777216 | tf_op jit(solution)/shard_map/slice | solution.py:639
  300.0 3.7 fusion.30
  305.6 46.5 %shard_map.254 = (bf16[2048,2048]{1,0:T(8,128)(2,1)}, bf16[2048,2048]{1,0:T(8,128)(2,1)}, bf16[2048,768]{1,0:T(8,128)(2,1)}, bf16[2048,1280]{1,0:T(8,128)(2,1)},...) custom-call(s32[8,4]{1,0:T(8,128)} %copy-done.15, bf16[2048,2048]{1,0:T(8,128)(2,1)} %bitcast.650, ...), custom_call_target="tpu_custom_call" | custom-call | flops 25769803776 | bytes 37748736 | tf_op jit(solution)/shard_map/pallas_call | solution.py:452
  352.2 4.9 slice_bitcast_fusion.2
  358.2 6.4 pad_maximum_fusion.1
  364.5 3.7 convert_reduce_fusion
  368.2 8.3 %copy.151 = bf16[4,2,256,2048]{3,2,1,0:T(8,128)(2,1)} copy(bf16[4,2,256,2048]{3,2,0,1:T(8,128)(2,1)} %pad_maximum_fusion.1) | data formatting | bytes 16777216 | tf_op jit(solution)/shard_map/stack | solution.py:658
  376.5 49.2 %shard_map.255 = (bf16[2048,1024]{1,0:T(8,128)(2,1)}, bf16[2048,768]{1,0:T(8,128)(2,1)}, bf16[2048,2048]{1,0:T(8,128)(2,1)}, f32[4,2048]{1,0:T(4,128)}, f32[1,1024]{1,0:T(1,128)}, /*index=5*/f32[1,768]{1,0:T(1,128)}) custom-call(s32[8,4]{1,0:T(8,128)} %copy-done.15, bf16[2048,2048]{1,0:T(8,128)(2,1)} %bitcast.651, bf16[2048,2048]{1,0:T(8,128)(2,1)} %bitcast.652, ...), custom_call_target="tpu_custom_call" | custom-call | flops 25769803776 | bytes 33554432 | tf_op jit(solution)/shard_map/pallas_call | solution.py:474
  427.2 25.8 %all-reduce.1 = f32[8,1792]{1,0:T(8,128)S(1)} all-reduce(f32[8,1792]{1,0:T(8,128)S(1)} %pad_maximum_fusion.15), channel_id=2, replica_groups=mesh['rep'=4,'shard'=8] {'shard'}, use_global_device_ids=true, to_apply=%region_6.7.clone | all-reduce | flops 14336 | bytes 114688
  454.5 13.6 %psum.7 = f32[3072]{0:T(1024)S(1)} all-reduce(f32[3072]{0:T(1024)S(1)} %pad_maximum_fusion.16), channel_id=1, replica_groups=mesh['rep'=4,'shard'=8] {'rep'}, use_global_device_ids=true, to_apply=%region_8.9 | all-reduce | flops 3072 | bytes 24576 | tf_op jit(solution)/shard_map/psum | solution.py:764
  469.3 14.1 %convolution_convert_fusion.1 = bf16[2048,1024]{0,1:T(8,128)(2,1)} fusion(bf16[2048,2048]{1,0:T(8,128)(2,1)} %get-tuple-element.32, bf16[2048,1024]{1,0:T(8,128)(2,1)} %get-tuple-element.33), kind=kOutput, calls=%fused_computation.16 | convolution fusion | flops 8592031744 | bytes 16777216 | tf_op jit(solution)/shard_map/dot_general | solution.py:69
  483.4 9.2 %convolution_convert_fusion.2 = bf16[2048,768]{0,1:T(8,128)(2,1)S(1)} fusion(bf16[2048,2048]{1,0:T(8,128)(2,1)} %get-tuple-element.34, bf16[2048,768]{1,0:T(8,128)(2,1)S(1)} %copy-done.32), kind=kOutput, calls=%fused_computation.21 | convolution fusion | flops 6444023808 | bytes 14680064 | tf_op jit(solution)/shard_map/dot_general | solution.py:69
  492.6 6.4 pad_maximum_fusion.2
  499.0 10.1 %copy.154 = bf16[2048,1792]{1,0:T(8,128)(2,1)} copy(bf16[2048,1792]{0,1:T(8,128)(2,1)} %pad_maximum_fusion.2) | data formatting | bytes 14680064 | tf_op jit(solution)/shard_map/concatenate | solution.py:700
  509.1 3.6 fusion.106
  515.5 15.7 %convolution_convert_fusion = bf16[1280,2048]{1,0:T(8,128)(2,1)S(1)} fusion(bf16[2048,1280]{1,0:T(8,128)(2,1)} %get-tuple-element.39, bf16[2048,2048]{1,0:T(8,128)(2,1)} %bitcast.653), kind=kOutput, calls=%fused_computation.8 | convolution fusion | flops 10740039680 | bytes 18874368 | tf_op jit(solution)/shard_map/dot_general | solution.py:69
  538.7 25.0 %collective-permute-done.39 = bf16[2,160,2048]{2,1,0:T(8,128)(2,1)S(1)} collective-permute-done((bf16[2,160,2048]{2,1,0:T(8,128)(2,1)S(1)}, bf16[2,160,2048]{2,1,0:T(8,128)(2,1)S(1)}, u32[]{:S(2)}, u32[]{:S(2)}) %collective-permute-start.39) | collective-permute-done | bytes 1310752 | tf_op jit(solution)/shard_map/ppermute | solution.py:508
  565.1 16.4 %collective-permute-done.37 = bf16[2,160,2048]{2,1,0:T(8,128)(2,1)S(1)} collective-permute-done((bf16[2,160,2048]{2,1,0:T(8,128)(2,1)S(1)}, bf16[2,160,2048]{2,1,0:T(8,128)(2,1)S(1)}, u32[]{:S(2)}, u32[]{:S(2)}) %collective-permute-start.37) | collective-permute-done | bytes 1310752 | tf_op jit(solution)/shard_map/ppermute | solution.py:508
  585.7 5.4 fusion.1
  591.2 4.2 collective-permute-start.14
  597.4 5.6 collective-permute-done.27
  605.0 12.2 %collective-permute-done.38 = bf16[160,2048]{1,0:T(8,128)(2,1)} collective-permute-done((bf16[160,2048]{1,0:T(8,128)(2,1)S(1)}, bf16[160,2048]{1,0:T(8,128)(2,1)}, u32[]{:S(2)}, u32[]{:S(2)}) %collective-permute-start.38) | collective-permute-done | bytes 655392 | tf_op jit(solution)/shard_map/ppermute | solution.py:508
  625.3 8.8 %collective-permute-done.42 = bf16[160,2048]{1,0:T(8,128)(2,1)S(1)} collective-permute-done((bf16[160,2048]{1,0:T(8,128)(2,1)S(1)}, bf16[160,2048]{1,0:T(8,128)(2,1)S(1)}, u32[]{:S(2)}, u32[]{:S(2)}) %collective-permute-start.42) | collective-permute-done | bytes 655392 | tf_op jit(solution)/shard_map/ppermute | solution.py:508
  636.1 7.8 collective-permute-done.41
  645.2 3.7 collective-permute-start.29
  648.9 3.8 collective-permute-start.30
  654.8 31.0 %collective-permute-done.29 = bf16[2,64,1792]{2,1,0:T(8,128)(2,1)S(1)} collective-permute-done((bf16[2,64,1792]{2,1,0:T(8,128)(2,1)S(1)}, bf16[2,64,1792]{2,1,0:T(8,128)(2,1)S(1)}, u32[]{:S(2)}, u32[]{:S(2)}) %collective-permute-start.29) | collective-permute-done | bytes 458784 | tf_op jit(solution)/shard_map/ppermute | solution.py:508
  687.5 5.8 collective-permute-done.30
  697.9 23.9 %collective-permute-done.43 = bf16[2,160,2048]{2,1,0:T(8,128)(2,1)S(1)} collective-permute-done((bf16[2,160,2048]{2,1,0:T(8,128)(2,1)S(1)}, bf16[2,160,2048]{2,1,0:T(8,128)(2,1)S(1)}, u32[]{:S(2)}, u32[]{:S(2)}) %collective-permute-start.43) | collective-permute-done | bytes 1310752 | tf_op jit(solution)/shard_map/ppermute | solution.py:508
  722.4 4.0 slice.708
  743.8 3.4 broadcast_in_dim.91
  751.6 4.1 fusion
  767.2 10.7 %collective-permute-done.22 = bf16[256,2048]{1,0:T(8,128)(2,1)S(1)} collective-permute-done((bf16[256,2048]{1,0:T(8,128)(2,1)S(1)}, bf16[256,2048]{1,0:T(8,128)(2,1)S(1)}, u32[]{:S(2)}, u32[]{:S(2)}) %collective-permute-start.22) | collective-permute-done | bytes 1048608 | tf_op jit(solution)/shard_map/ppermute | solution.py:508
  781.9 19.0 %collective-permute-done.23 = bf16[256,2048]{1,0:T(8,128)(2,1)S(1)} collective-permute-done((bf16[256,2048]{1,0:T(8,128)(2,1)S(1)}, bf16[256,2048]{1,0:T(8,128)(2,1)S(1)}, u32[]{:S(2)}, u32[]{:S(2)}) %collective-permute-start.23) | collective-permute-done | bytes 1048608 | tf_op jit(solution)/shard_map/ppermute | solution.py:508
  807.7 14.4 %collective-permute-done.24 = bf16[256,2048]{1,0:T(8,128)(2,1)S(1)} collective-permute-done((bf16[256,2048]{1,0:T(8,128)(2,1)S(1)}, bf16[256,2048]{1,0:T(8,128)(2,1)S(1)}, u32[]{:S(2)}, u32[]{:S(2)}) %collective-permute-start.24) | collective-permute-done | bytes 1048608 | tf_op jit(solution)/shard_map/ppermute | solution.py:508
  822.9 3.7 fusion.14
  (382 shorter events, 173.0 us)
Async XLA Ops:
  5.6 32.1 %collective-permute-start.5 = (bf16[2,64,1792]{2,1,0:T(8,128)(2,1)}, bf16[2,64,1792]{2,1,0:T(8,128)(2,1)}, u32[]{:S(2)}, u32[]{:S(2)}) collective-permute-start(bf16[2,64,1792]{2,1,0:T(8,128)(2,1)} %get-tuple-element.76), channel_id=1, source_target_pairs={{0,2},{1,3},{2,4},{3,5},{4,6},{5,7},{6,0},{7,1},{8,10},{9,11},{10,... | collective-permute-start | bytes 1376264 | tf_op jit(solution)/shard_map/ppermute | solution.py:508
  7.1 40.8 %collective-permute-start.6 = (bf16[2,64,1792]{2,1,0:T(8,128)(2,1)}, bf16[2,64,1792]{2,1,0:T(8,128)(2,1)}, u32[]{:S(2)}, u32[]{:S(2)}) collective-permute-start(bf16[2,64,1792]{2,1,0:T(8,128)(2,1)} %get-tuple-element.78), channel_id=1, source_target_pairs={{0,4},{1,5},{2,6},{3,7},{4,0},{5,1},{6,2},{7,3},{8,12},{9,13},{10,... | collective-permute-start | bytes 1376264 | tf_op jit(solution)/shard_map/ppermute | solution.py:508
  8.4 87.9 %collective-permute-start.7 = (bf16[2,64,1792]{2,1,0:T(8,128)(2,1)}, bf16[2,64,1792]{2,1,0:T(8,128)(2,1)}, u32[]{:S(2)}, u32[]{:S(2)}) collective-permute-start(bf16[2,64,1792]{2,1,0:T(8,128)(2,1)} %get-tuple-element.77), channel_id=1, source_target_pairs={{0,6},{1,7},{2,0},{3,1},{4,2},{5,3},{6,4},{7,5},{8,14},{9,15},{10,... | collective-permute-start | bytes 1376264 | tf_op jit(solution)/shard_map/ppermute | solution.py:508
  19.4 80.2 %collective-permute-start.4 = (bf16[256,1792]{1,0:T(8,128)(2,1)}, bf16[256,1792]{1,0:T(8,128)(2,1)}, u32[]{:S(2)}, u32[]{:S(2)}) collective-permute-start(bf16[256,1792]{1,0:T(8,128)(2,1)} %pad_maximum_fusion.14), channel_id=1, source_target_pairs={{0,1},{1,0},{2,3},{3,2},{4,5},{5,4},{6,7},{7,6},{8,9},{9,8},{10,11... | collective-permute-start | bytes 2752520 | tf_op jit(solution)/shard_map/ppermute | solution.py:508
  21.3 85.8 %collective-permute-start = (bf16[272,2048]{1,0:T(8,128)(2,1)S(1)}, bf16[272,2048]{1,0:T(8,128)(2,1)}, u32[]{:S(2)}, u32[]{:S(2)}) collective-permute-start(bf16[272,2048]{1,0:T(8,128)(2,1)S(1)} %constant_dynamic-update-slice_fusion.8), channel_id=1, source_target_pairs={{0,2},{1,3},{2,4},{3,5},{4,6},{5,7},{6,0},{7,1},{8,10},{9,11},{10,... | collective-permute-start | bytes 3342344 | tf_op jit(solution)/shard_map/ppermute | solution.py:508
  97.9 18.7 %collective-permute-start.8 = (bf16[3,64,1792]{2,1,0:T(8,128)(2,1)S(1)}, bf16[3,64,1792]{2,1,0:T(8,128)(2,1)S(1)}, u32[]{:S(2)}, u32[]{:S(2)}) collective-permute-start(bf16[3,64,1792]{2,1,0:T(8,128)(2,1)S(1)} %get-tuple-element.84), channel_id=1, source_target_pairs={{0,1},{1,0},{2,3},{3,2},{4,5},{5,4},{6,7},{7,6},{8,9},{9,8},{10,11... | collective-permute-start | bytes 2064392 | tf_op jit(solution)/shard_map/ppermute | solution.py:508
  97.9 17.8 %collective-permute-start.9 = (bf16[3,64,1792]{2,1,0:T(8,128)(2,1)S(1)}, bf16[3,64,1792]{2,1,0:T(8,128)(2,1)S(1)}, u32[]{:S(2)}, u32[]{:S(2)}) collective-permute-start(bf16[3,64,1792]{2,1,0:T(8,128)(2,1)S(1)} %get-tuple-element.85), channel_id=1, source_target_pairs={{0,16},{1,17},{2,18},{3,19},{4,20},{5,21},{6,22},{7,23},{8,24},{9,... | collective-permute-start | bytes 2064392 | tf_op jit(solution)/shard_map/ppermute | solution.py:508
  107.1 61.0 %collective-permute-start.1 = (bf16[272,2048]{1,0:T(8,128)(2,1)}, bf16[272,2048]{1,0:T(8,128)(2,1)S(1)}, u32[]{:S(2)}, u32[]{:S(2)}) collective-permute-start(bf16[272,2048]{1,0:T(8,128)(2,1)} %collective-permute-done), channel_id=1, source_target_pairs={{0,2},{1,3},{2,4},{3,5},{4,6},{5,7},{6,0},{7,1},{8,10},{9,11},{10,... | collective-permute-start | bytes 3342344 | tf_op jit(solution)/shard_map/ppermute | solution.py:508
  115.9 52.2 %collective-permute-start.11 = (bf16[2,3,64,1792]{3,2,1,0:T(8,128)(2,1)S(1)}, bf16[2,3,64,1792]{3,2,1,0:T(8,128)(2,1)S(1)}, u32[]{:S(2)}, u32[]{:S(2)}) collective-permute-start(bf16[2,3,64,1792]{3,2,1,0:T(8,128)(2,1)S(1)} %pad_maximum_fusion.10), channel_id=1, source_target_pairs={{0,8},{1,9},{2,10},{3,11},{4,12},{5,13},{6,14},{7,15},{8,0},{9,1},... | collective-permute-start | bytes 4128776 | tf_op jit(solution)/shard_map/ppermute | solution.py:508
  116.5 46.0 %collective-permute-start.10 = (bf16[3,64,1792]{2,1,0:T(8,128)(2,1)S(1)}, bf16[3,64,1792]{2,1,0:T(8,128)(2,1)S(1)}, u32[]{:S(2)}, u32[]{:S(2)}) collective-permute-start(bf16[3,64,1792]{2,1,0:T(8,128)(2,1)S(1)} %collective-permute-done.8), channel_id=1, source_target_pairs={{0,8},{1,9},{2,10},{3,11},{4,12},{5,13},{6,14},{7,15},{8,0},{9,1},... | collective-permute-start | bytes 2064392 | tf_op jit(solution)/shard_map/ppermute | solution.py:508
  162.6 36.8 %collective-permute-start.12 = (bf16[2,3,64,1792]{3,2,1,0:T(8,128)(2,1)S(1)}, bf16[2,3,64,1792]{3,2,1,0:T(8,128)(2,1)S(1)}, u32[]{:S(2)}, u32[]{:S(2)}) collective-permute-start(bf16[2,3,64,1792]{3,2,1,0:T(8,128)(2,1)S(1)} %pad_maximum_fusion.11), channel_id=1, source_target_pairs={{0,16},{1,17},{2,18},{3,19},{4,20},{5,21},{6,22},{7,23},{8,24},{9,... | collective-permute-start | bytes 4128776 | tf_op jit(solution)/shard_map/ppermute | solution.py:508
  168.1 25.0 %collective-permute-start.2 = (bf16[272,2048]{1,0:T(8,128)(2,1)S(1)}, bf16[272,2048]{1,0:T(8,128)(2,1)S(1)}, u32[]{:S(2)}, u32[]{:S(2)}) collective-permute-start(bf16[272,2048]{1,0:T(8,128)(2,1)S(1)} %collective-permute-done.1), channel_id=1, source_target_pairs={{0,2},{1,3},{2,4},{3,5},{4,6},{5,7},{6,0},{7,1},{8,10},{9,11},{10,... | collective-permute-start | bytes 3342344 | tf_op jit(solution)/shard_map/ppermute | solution.py:508
  196.6 81.4 %collective-permute-start.3 = (bf16[4,272,2048]{2,1,0:T(8,128)(2,1)S(1)}, bf16[4,272,2048]{2,1,0:T(8,128)(2,1)S(1)}, u32[]{:S(2)}, u32[]{:S(2)}) collective-permute-start(bf16[4,272,2048]{2,1,0:T(8,128)(2,1)S(1)} %get-tuple-element.51), channel_id=1, source_target_pairs={{0,1},{1,0},{2,3},{3,2},{4,5},{5,4},{6,7},{7,6},{8,9},{9,8},{10,11... | collective-permute-start | bytes 13369352 | tf_op jit(solution)/shard_map/ppermute | solution.py:508
  198.5 25.6 %collective-permute-start.17 = (bf16[256,2048]{1,0:T(8,128)(2,1)S(1)}, bf16[256,2048]{1,0:T(8,128)(2,1)S(1)}, u32[]{:S(2)}, u32[]{:S(2)}) collective-permute-start(bf16[256,2048]{1,0:T(8,128)(2,1)S(1)} %broadcast_select_fusion), channel_id=1, source_target_pairs={{0,2},{1,3},{2,4},{3,5},{4,6},{5,7},{6,0},{7,1},{8,10},{9,11},{10,... | collective-permute-start | bytes 3145736 | tf_op jit(solution)/shard_map/ppermute | solution.py:508
  224.1 24.8 %collective-permute-start.18 = (bf16[256,2048]{1,0:T(8,128)(2,1)S(1)}, bf16[256,2048]{1,0:T(8,128)(2,1)S(1)}, u32[]{:S(2)}, u32[]{:S(2)}) collective-permute-start(bf16[256,2048]{1,0:T(8,128)(2,1)S(1)} %collective-permute-done.17), channel_id=1, source_target_pairs={{0,2},{1,3},{2,4},{3,5},{4,6},{5,7},{6,0},{7,1},{8,10},{9,11},{10,... | collective-permute-start | bytes 3145736 | tf_op jit(solution)/shard_map/ppermute | solution.py:508
  248.9 25.4 %collective-permute-start.19 = (bf16[256,2048]{1,0:T(8,128)(2,1)S(1)}, bf16[256,2048]{1,0:T(8,128)(2,1)S(1)}, u32[]{:S(2)}, u32[]{:S(2)}) collective-permute-start(bf16[256,2048]{1,0:T(8,128)(2,1)S(1)} %collective-permute-done.18), channel_id=1, source_target_pairs={{0,2},{1,3},{2,4},{3,5},{4,6},{5,7},{6,0},{7,1},{8,10},{9,11},{10,... | collective-permute-start | bytes 3145736 | tf_op jit(solution)/shard_map/ppermute | solution.py:508
  277.9 80.2 %collective-permute-start.20 = (bf16[4,256,2048]{2,1,0:T(8,128)(2,1)}, bf16[4,256,2048]{2,1,0:T(8,128)(2,1)}, u32[]{:S(2)}, u32[]{:S(2)}) collective-permute-start(bf16[4,256,2048]{2,1,0:T(8,128)(2,1)} %get-tuple-element.53), channel_id=1, source_target_pairs={{0,1},{1,0},{2,3},{3,2},{4,5},{5,4},{6,7},{7,6},{8,9},{9,8},{10,11... | collective-permute-start | bytes 12582920 | tf_op jit(solution)/shard_map/ppermute | solution.py:508
  357.1 227.1 %collective-permute-start.13 = (bf16[4,256,2048]{2,1,0:T(8,128)(2,1)}, bf16[4,256,2048]{2,1,0:T(8,128)(2,1)}, u32[]{:S(2)}, u32[]{:S(2)}) collective-permute-start(bf16[4,256,2048]{2,1,0:T(8,128)(2,1)} %slice_bitcast_fusion.2), channel_id=1, source_target_pairs={{0,1},{1,0},{2,3},{3,2},{4,5},{5,4},{6,7},{7,6},{8,9},{9,8},{10,11... | collective-permute-start | bytes 12582920 | tf_op jit(solution)/shard_map/ppermute | solution.py:508
  513.0 23.3 %slice-start = ((s8[8388608]{0:T(1024)(128)(4,1)}), s8[4194304]{0:T(1024)(128)(4,1)S(1)}, s32[]{:S(2)}) async-start(s8[8388608]{0:T(1024)(128)(4,1)} %bitcast.642), calls=%async_computation | async-start | bytes 8388608
  513.2 78.0 %collective-permute-start.25 = (bf16[2,8,32,1792]{3,2,1,0:T(8,128)(2,1)S(1)}, bf16[2,8,32,1792]{3,2,1,0:T(8,128)(2,1)}, u32[]{:S(2)}, u32[]{:S(2)}) collective-permute-start(bf16[2,8,32,1792]{3,2,1,0:T(8,128)(2,1)S(1)} %bitcast.679), channel_id=1, source_target_pairs={{0,8},{1,9},{2,10},{3,11},{4,12},{5,13},{6,14},{7,15},{8,0},{9,1},... | collective-permute-start | bytes 5505032 | tf_op jit(solution)/shard_map/ppermute | solution.py:508
  531.9 31.8 %collective-permute-start.39 = (bf16[2,160,2048]{2,1,0:T(8,128)(2,1)S(1)}, bf16[2,160,2048]{2,1,0:T(8,128)(2,1)S(1)}, u32[]{:S(2)}, u32[]{:S(2)}) collective-permute-start(bf16[2,160,2048]{2,1,0:T(8,128)(2,1)S(1)} %dynamic-slice_bitcast_fusion.1), channel_id=1, source_target_pairs={{0,16},{1,17},{2,18},{3,19},{4,20},{5,21},{6,22},{7,23},{8,24},{9,... | collective-permute-start | bytes 3932168 | tf_op jit(solution)/shard_map/ppermute | solution.py:508
  534.8 68.2 %collective-permute-start.27 = (bf16[2,8,32,1792]{3,2,0,1:T(8,128)(2,1)}, bf16[2,8,32,1792]{3,2,0,1:T(8,128)(2,1)S(1)}, u32[]{:S(2)}, u32[]{:S(2)}) collective-permute-start(bf16[2,8,32,1792]{3,2,0,1:T(8,128)(2,1)} %dynamic-slice_bitcast_fusion), channel_id=1, source_target_pairs={{0,16},{1,17},{2,18},{3,19},{4,20},{5,21},{6,22},{7,23},{8,24},{9,... | collective-permute-start | bytes 5505032 | tf_op jit(solution)/shard_map/ppermute | solution.py:508
  535.5 46.1 %collective-permute-start.37 = (bf16[2,160,2048]{2,1,0:T(8,128)(2,1)S(1)}, bf16[2,160,2048]{2,1,0:T(8,128)(2,1)S(1)}, u32[]{:S(2)}, u32[]{:S(2)}) collective-permute-start(bf16[2,160,2048]{2,1,0:T(8,128)(2,1)S(1)} %dynamic-slice_bitcast_fusion.2), channel_id=1, source_target_pairs={{0,8},{1,9},{2,10},{3,11},{4,12},{5,13},{6,14},{7,15},{8,0},{9,1},... | collective-permute-start | bytes 3932168 | tf_op jit(solution)/shard_map/ppermute | solution.py:508
  536.3 290.3 %copy-start.19 = (f32[256]{0:T(256)}, f32[256]{0:T(256)S(1)}, u32[]{:S(2)}) copy-start(f32[256]{0:T(256)S(1)} %get-tuple-element.129) | copy-start | bytes 3076
  563.7 186.7 %collective-permute-start.21 = (bf16[4,256,2048]{2,1,0:T(8,128)(2,1)}, bf16[4,256,2048]{2,1,0:T(8,128)(2,1)}, u32[]{:S(2)}, u32[]{:S(2)}) collective-permute-start(bf16[4,256,2048]{2,1,0:T(8,128)(2,1)} %slice_bitcast_fusion), channel_id=1, source_target_pairs={{0,1},{1,0},{2,3},{3,2},{4,5},{5,4},{6,7},{7,6},{8,9},{9,8},{10,11... | collective-permute-start | bytes 12582920 | tf_op jit(solution)/shard_map/ppermute | solution.py:508
  581.6 38.3 %collective-permute-start.40 = (bf16[160,2048]{1,0:T(8,128)(2,1)}, bf16[160,2048]{1,0:T(8,128)(2,1)}, u32[]{:S(2)}, u32[]{:S(2)}) collective-permute-start(bf16[160,2048]{1,0:T(8,128)(2,1)} %dynamic-slice_bitcast_fusion.7), channel_id=1, source_target_pairs={{0,8},{1,9},{2,10},{3,11},{4,12},{5,13},{6,14},{7,15},{8,0},{9,1},... | collective-permute-start | bytes 1966088 | tf_op jit(solution)/shard_map/ppermute | solution.py:508
  584.1 33.1 %collective-permute-start.38 = (bf16[160,2048]{1,0:T(8,128)(2,1)S(1)}, bf16[160,2048]{1,0:T(8,128)(2,1)}, u32[]{:S(2)}, u32[]{:S(2)}) collective-permute-start(bf16[160,2048]{1,0:T(8,128)(2,1)S(1)} %dynamic-slice_bitcast_fusion.8), channel_id=1, source_target_pairs={{0,16},{1,17},{2,18},{3,19},{4,20},{5,21},{6,22},{7,23},{8,24},{9,... | collective-permute-start | bytes 1966088 | tf_op jit(solution)/shard_map/ppermute | solution.py:508
  591.1 105.3 %copy-start.3 = (bf16[4,256,2048]{2,1,0:T(8,128)(2,1)}, bf16[4,256,2048]{2,1,0:T(8,128)(2,1)S(1)}, u32[]{:S(2)}) copy-start(bf16[4,256,2048]{2,1,0:T(8,128)(2,1)S(1)} %fusion.1) | copy-start | bytes 12582916
  591.2 32.3 %collective-permute-start.14 = (bf16[256,2048]{1,0:T(8,128)(2,1)S(1)}, bf16[256,2048]{1,0:T(8,128)(2,1)S(1)}, u32[]{:S(2)}, u32[]{:S(2)}) collective-permute-start(bf16[256,2048]{1,0:T(8,128)(2,1)S(1)} %slice_bitcast_fusion.8), channel_id=1, source_target_pairs={{0,6},{1,7},{2,0},{3,1},{4,2},{5,3},{6,4},{7,5},{8,14},{9,15},{10,... | collective-permute-start | bytes 3145736 | tf_op jit(solution)/shard_map/ppermute | solution.py:508
  603.1 41.1 %collective-permute-start.26 = (bf16[8,32,1792]{2,1,0:T(8,128)(2,1)S(1)}, bf16[8,32,1792]{2,1,0:T(8,128)(2,1)S(1)}, u32[]{:S(2)}, u32[]{:S(2)}) collective-permute-start(bf16[8,32,1792]{2,1,0:T(8,128)(2,1)S(1)} %dynamic-slice_bitcast_fusion.5), channel_id=1, source_target_pairs={{0,16},{1,17},{2,18},{3,19},{4,20},{5,21},{6,22},{7,23},{8,24},{9,... | collective-permute-start | bytes 2752520 | tf_op jit(solution)/shard_map/ppermute | solution.py:508
  621.2 12.9 %collective-permute-start.42 = (bf16[160,2048]{1,0:T(8,128)(2,1)S(1)}, bf16[160,2048]{1,0:T(8,128)(2,1)S(1)}, u32[]{:S(2)}, u32[]{:S(2)}) collective-permute-start(bf16[160,2048]{1,0:T(8,128)(2,1)S(1)} %get-tuple-element.43), channel_id=1, source_target_pairs={{0,8},{1,9},{2,10},{3,11},{4,12},{5,13},{6,14},{7,15},{8,0},{9,1},... | collective-permute-start | bytes 1966088 | tf_op jit(solution)/shard_map/ppermute | solution.py:508
  621.5 22.9 %collective-permute-start.28 = (bf16[8,32,1792]{2,1,0:T(8,128)(2,1)S(1)}, bf16[8,32,1792]{2,1,0:T(8,128)(2,1)S(1)}, u32[]{:S(2)}, u32[]{:S(2)}) collective-permute-start(bf16[8,32,1792]{2,1,0:T(8,128)(2,1)S(1)} %dynamic-slice_bitcast_fusion.4), channel_id=1, source_target_pairs={{0,8},{1,9},{2,10},{3,11},{4,12},{5,13},{6,14},{7,15},{8,0},{9,1},... | collective-permute-start | bytes 2752520 | tf_op jit(solution)/shard_map/ppermute | solution.py:508
  623.5 20.5 %collective-permute-start.41 = (bf16[160,2048]{1,0:T(8,128)(2,1)S(1)}, bf16[160,2048]{1,0:T(8,128)(2,1)S(1)}, u32[]{:S(2)}, u32[]{:S(2)}) collective-permute-start(bf16[160,2048]{1,0:T(8,128)(2,1)S(1)} %get-tuple-element.45), channel_id=1, source_target_pairs={{0,16},{1,17},{2,18},{3,19},{4,20},{5,21},{6,22},{7,23},{8,24},{9,... | collective-permute-start | bytes 1966088 | tf_op jit(solution)/shard_map/ppermute | solution.py:508
  634.1 62.2 %collective-permute-start.15 = (bf16[256,2048]{1,0:T(8,128)(2,1)S(1)}, bf16[256,2048]{1,0:T(8,128)(2,1)S(1)}, u32[]{:S(2)}, u32[]{:S(2)}) collective-permute-start(bf16[256,2048]{1,0:T(8,128)(2,1)S(1)} %fusion.19), channel_id=1, source_target_pairs={{0,6},{1,7},{2,0},{3,1},{4,2},{5,3},{6,4},{7,5},{8,14},{9,15},{10,... | collective-permute-start | bytes 3145736 | tf_op jit(solution)/shard_map/ppermute | solution.py:508
  645.2 40.6 %collective-permute-start.29 = (bf16[2,64,1792]{2,1,0:T(8,128)(2,1)S(1)}, bf16[2,64,1792]{2,1,0:T(8,128)(2,1)S(1)}, u32[]{:S(2)}, u32[]{:S(2)}) collective-permute-start(bf16[2,64,1792]{2,1,0:T(8,128)(2,1)S(1)} %get-tuple-element.75), channel_id=1, source_target_pairs={{0,2},{1,3},{2,4},{3,5},{4,6},{5,7},{6,0},{7,1},{8,10},{9,11},{10,... | collective-permute-start | bytes 1376264 | tf_op jit(solution)/shard_map/ppermute | solution.py:508
  648.9 44.4 %collective-permute-start.30 = (bf16[2,64,1792]{2,1,0:T(8,128)(2,1)S(1)}, bf16[2,64,1792]{2,1,0:T(8,128)(2,1)S(1)}, u32[]{:S(2)}, u32[]{:S(2)}) collective-permute-start(bf16[2,64,1792]{2,1,0:T(8,128)(2,1)S(1)} %get-tuple-element.74), channel_id=1, source_target_pairs={{0,4},{1,5},{2,6},{3,7},{4,0},{5,1},{6,2},{7,3},{8,12},{9,13},{10,... | collective-permute-start | bytes 1376264 | tf_op jit(solution)/shard_map/ppermute | solution.py:508
  652.7 41.4 %collective-permute-start.31 = (bf16[2,64,1792]{2,1,0:T(8,128)(2,1)S(1)}, bf16[2,64,1792]{2,1,0:T(8,128)(2,1)S(1)}, u32[]{:S(2)}, u32[]{:S(2)}) collective-permute-start(bf16[2,64,1792]{2,1,0:T(8,128)(2,1)S(1)} %get-tuple-element.73), channel_id=1, source_target_pairs={{0,6},{1,7},{2,0},{3,1},{4,2},{5,3},{6,4},{7,5},{8,14},{9,15},{10,... | collective-permute-start | bytes 1376264 | tf_op jit(solution)/shard_map/ppermute | solution.py:508
  685.8 36.2 %collective-permute-start.44 = (bf16[2,160,2048]{2,1,0:T(8,128)(2,1)S(1)}, bf16[2,160,2048]{2,1,0:T(8,128)(2,1)S(1)}, u32[]{:S(2)}, u32[]{:S(2)}) collective-permute-start(bf16[2,160,2048]{2,1,0:T(8,128)(2,1)S(1)} %pad_maximum_fusion.13), channel_id=1, source_target_pairs={{0,16},{1,17},{2,18},{3,19},{4,20},{5,21},{6,22},{7,23},{8,24},{9,... | collective-permute-start | bytes 3932168 | tf_op jit(solution)/shard_map/ppermute | solution.py:508
  693.3 28.4 %collective-permute-start.43 = (bf16[2,160,2048]{2,1,0:T(8,128)(2,1)S(1)}, bf16[2,160,2048]{2,1,0:T(8,128)(2,1)S(1)}, u32[]{:S(2)}, u32[]{:S(2)}) collective-permute-start(bf16[2,160,2048]{2,1,0:T(8,128)(2,1)S(1)} %pad_maximum_fusion.12), channel_id=1, source_target_pairs={{0,8},{1,9},{2,10},{3,11},{4,12},{5,13},{6,14},{7,15},{8,0},{9,1},... | collective-permute-start | bytes 3932168 | tf_op jit(solution)/shard_map/ppermute | solution.py:508
  695.3 32.5 %collective-permute-start.32 = (bf16[4,64,1792]{2,1,0:T(8,128)(2,1)}, bf16[4,64,1792]{2,1,0:T(8,128)(2,1)}, u32[]{:S(2)}, u32[]{:S(2)}) collective-permute-start(bf16[4,64,1792]{2,1,0:T(8,128)(2,1)} %dynamic-slice_bitcast_fusion.3), channel_id=1, source_target_pairs={{0,1},{1,0},{2,3},{3,2},{4,5},{5,4},{6,7},{7,6},{8,9},{9,8},{10,11... | collective-permute-start | bytes 2752520 | tf_op jit(solution)/shard_map/ppermute | solution.py:508
  697.7 125.2 %collective-permute-start.16 = (bf16[256,2048]{1,0:T(8,128)(2,1)}, bf16[256,2048]{1,0:T(8,128)(2,1)}, u32[]{:S(2)}, u32[]{:S(2)}) collective-permute-start(bf16[256,2048]{1,0:T(8,128)(2,1)} %fusion.20), channel_id=1, source_target_pairs={{0,6},{1,7},{2,0},{3,1},{4,2},{5,3},{6,4},{7,5},{8,14},{9,15},{10,... | collective-permute-start | bytes 3145736 | tf_op jit(solution)/shard_map/ppermute | solution.py:508
  739.1 19.5 %collective-permute-start.33 = (bf16[32,14336]{1,0:T(8,128)(2,1)}, bf16[32,14336]{1,0:T(8,128)(2,1)}, u32[]{:S(2)}, u32[]{:S(2)}) collective-permute-start(bf16[32,14336]{1,0:T(8,128)(2,1)} %get-tuple-element.65), channel_id=1, source_target_pairs={{0,16},{1,17},{2,18},{3,19},{4,20},{5,21},{6,22},{7,23},{8,24},{9,... | collective-permute-start | bytes 2752520 | tf_op jit(solution)/shard_map/ppermute | solution.py:508
  739.4 21.4 %collective-permute-start.34 = (bf16[32,14336]{1,0:T(8,128)(2,1)}, bf16[32,14336]{1,0:T(8,128)(2,1)}, u32[]{:S(2)}, u32[]{:S(2)}) collective-permute-start(bf16[32,14336]{1,0:T(8,128)(2,1)} %get-tuple-element.64), channel_id=1, source_target_pairs={{0,8},{1,9},{2,10},{3,11},{4,12},{5,13},{6,14},{7,15},{8,0},{9,1},... | collective-permute-start | bytes 2752520 | tf_op jit(solution)/shard_map/ppermute | solution.py:508
  755.8 22.2 %collective-permute-start.22 = (bf16[256,2048]{1,0:T(8,128)(2,1)S(1)}, bf16[256,2048]{1,0:T(8,128)(2,1)S(1)}, u32[]{:S(2)}, u32[]{:S(2)}) collective-permute-start(bf16[256,2048]{1,0:T(8,128)(2,1)S(1)} %slice_bitcast_fusion.4), channel_id=1, source_target_pairs={{0,6},{1,7},{2,0},{3,1},{4,2},{5,3},{6,4},{7,5},{8,14},{9,15},{10,... | collective-permute-start | bytes 3145736 | tf_op jit(solution)/shard_map/ppermute | solution.py:508
  760.0 43.4 %collective-permute-start.35 = (bf16[2,32,14336]{2,1,0:T(8,128)(2,1)S(1)}, bf16[2,32,14336]{2,1,0:T(8,128)(2,1)S(1)}, u32[]{:S(2)}, u32[]{:S(2)}) collective-permute-start(bf16[2,32,14336]{2,1,0:T(8,128)(2,1)S(1)} %pad_maximum_fusion.7), channel_id=1, source_target_pairs={{0,8},{1,9},{2,10},{3,11},{4,12},{5,13},{6,14},{7,15},{8,0},{9,1},... | collective-permute-start | bytes 5505032 | tf_op jit(solution)/shard_map/ppermute | solution.py:508
  762.2 43.3 %collective-permute-start.36 = (bf16[2,32,14336]{2,1,0:T(8,128)(2,1)S(1)}, bf16[2,32,14336]{2,1,0:T(8,128)(2,1)S(1)}, u32[]{:S(2)}, u32[]{:S(2)}) collective-permute-start(bf16[2,32,14336]{2,1,0:T(8,128)(2,1)S(1)} %pad_maximum_fusion.8), channel_id=1, source_target_pairs={{0,16},{1,17},{2,18},{3,19},{4,20},{5,21},{6,22},{7,23},{8,24},{9,... | collective-permute-start | bytes 5505032 | tf_op jit(solution)/shard_map/ppermute | solution.py:508
  778.4 22.6 %collective-permute-start.23 = (bf16[256,2048]{1,0:T(8,128)(2,1)S(1)}, bf16[256,2048]{1,0:T(8,128)(2,1)S(1)}, u32[]{:S(2)}, u32[]{:S(2)}) collective-permute-start(bf16[256,2048]{1,0:T(8,128)(2,1)S(1)} %fusion.17), channel_id=1, source_target_pairs={{0,6},{1,7},{2,0},{3,1},{4,2},{5,3},{6,4},{7,5},{8,14},{9,15},{10,... | collective-permute-start | bytes 3145736 | tf_op jit(solution)/shard_map/ppermute | solution.py:508
  801.3 20.8 %collective-permute-start.24 = (bf16[256,2048]{1,0:T(8,128)(2,1)S(1)}, bf16[256,2048]{1,0:T(8,128)(2,1)S(1)}, u32[]{:S(2)}, u32[]{:S(2)}) collective-permute-start(bf16[256,2048]{1,0:T(8,128)(2,1)S(1)} %fusion.18), channel_id=1, source_target_pairs={{0,6},{1,7},{2,0},{3,1},{4,2},{5,3},{6,4},{7,5},{8,14},{9,15},{10,... | collective-permute-start | bytes 3145736 | tf_op jit(solution)/shard_map/ppermute | solution.py:508
  (34 other events, 254.0 us)

commit v3 on v2

--- a/solution.py
+++ b/solution.py
@@ -491,81 +491,523 @@
             flops=flops, bytes_accessed=2 * slots * (3 * width + 2 * units), transcendentals=0
         ),
     )(ends, x, up, cosine, signed, norms, qkv, slope, proj, exp, comb, cont)
-
-
-def links(move):
-    pairs = []
-    for y in range(2):
-        for x in range(2):
-            for z in range(4):
-                for c in range(2):
-                    ty, tx, tz, tc = move(y, x, z, c)
-                    pairs.append((((y * 2 + x) * 4 + z) * 2 + c, ((ty * 2 + tx) * 4 + tz % 4) * 2 + tc))
-    return pairs
-
-
-def send(value, move):
-    return lax.ppermute(value, ("rep", "shard"), links(move))
-
-
-def by_core(value):
-    return send(value, lambda y, x, z, c: (y, x, z, 1 - c))
-
-
-def by_x(value):
-    return send(value, lambda y, x, z, c: (y, 1 - x, z, c))
-
-
-def by_y(value):
-    return send(value, lambda y, x, z, c: (1 - y, x, z, c))
-
-
-def by_z(value, step):
-    return send(value, lambda y, x, z, c: (y, x, z + step, c))
-
-
-def pick(value, index, axis):
-    return lax.dynamic_index_in_dim(value, index, axis=axis, keepdims=False)
-
-
-def put(buffer, value, *index):
-    start = index + (0,) * (buffer.ndim - len(index))
-    return lax.dynamic_update_slice(
-        buffer, value.reshape((1,) * len(index) + buffer.shape[len(index):]).astype(buffer.dtype), start
-    )
-
-
-def added(a, b):
-    return (a.astype(f32) + b.astype(f32)).astype(bf16)
-
-
-def plane_sums(value, y, x):
-    a, b = value[:, :, 0], value[:, :, 1]
-    got = by_x(pick(a, 1 - x, 1))
-    a = added(pick(a, x, 1), got)
-    got = by_y(pick(b, 1 - y, 0))
-    b = added(pick(b, y, 0), got)
-    got = by_y(pick(a, 1 - y, 0))
-    a = added(pick(a, y, 0), got)
-    got = by_x(pick(b, 1 - x, 0))
-    b = added(pick(b, x, 0), got)
-    return a, b
-
-
-def plane_gather(a, b, y, x, place):
-    other_x, other_y = 1 - x, 1 - y
-    ay = by_y(a)
-    bx = by_x(b)
-    ax = by_x(jnp.stack([a, ay]))
-    by = by_y(jnp.stack([b, bx]))
-    place(y, x, 0, a)
-    place(y, x, 1, b)
-    place(other_y, x, 0, ay)
-    place(y, other_x, 1, bx)
-    place(y, other_x, 0, ax[0])
-    place(other_y, other_x, 0, ax[1])
-    place(other_y, x, 1, by[0])
-    place(other_y, other_x, 1, by[1])
+MESH = pl.DeviceIdType.MESH
+
+
+def position_of():
+    rep, me = lax.axis_index("rep"), lax.axis_index("shard")
+    return rep, me, lax.div(rep, 2), lax.rem(rep, 2), lax.div(me, 2), lax.rem(me, 2)
+
+
+def meet(peers):
+    barrier = pltpu.get_barrier_semaphore()
+    for peer in peers:
+        pl.semaphore_signal(barrier, inc=1, device_id=peer, device_id_type=MESH)
+    pl.semaphore_wait(barrier, len(peers))
+
+
+def rows_at(start, size):
+    return pl.ds(pl.multiple_of(start, size), size)
+
+
+class Net:
+    def __init__(self, send_sem, recv_sem, local_sem):
+        self.send_sem, self.recv_sem, self.local_sem = send_sem, recv_sem, local_sem
+        self.sends, self.locals, self.started, self.sent = 0, 0, 0, []
+
+    def slots(self, count):
+        first = self.started
+        self.started += count
+        return first
+
+    def send(self, src, dst, peer, slot, when=None):
+        index = self.sends
+        self.sends += 1
+        copy = pltpu.make_async_remote_copy(
+            src_ref=src, dst_ref=dst, send_sem=self.send_sem.at[index],
+            recv_sem=self.recv_sem.at[slot], device_id=peer, device_id_type=MESH,
+        )
+        if when is None:
+            copy.start()
+        else:
+            pl.when(when)(lambda: copy.start())
+        self.sent.append((copy, when))
+
+    def arrived(self, dst, peer, slot):
+        pltpu.make_async_remote_copy(
+            src_ref=dst, dst_ref=dst, send_sem=self.send_sem.at[0],
+            recv_sem=self.recv_sem.at[slot], device_id=peer, device_id_type=MESH,
+        ).wait_recv()
+
+    def local(self, src, dst):
+        copy = pltpu.make_async_copy(src, dst, self.local_sem.at[self.locals])
+        self.locals += 1
+        copy.start()
+        return copy
+
+    def finish(self):
+        for copy, when in self.sent:
+            if when is None:
+                copy.wait_send()
+            else:
+                pl.when(when)(lambda copy=copy: copy.wait_send())
+
+
+def gather_kernel(
+    tok_ref, vec_ref, up_ref, exp_ref, proj_ref,
+    x_out, vec_out, up_out, exp_out, proj_out, send_sem, recv_sem, local_sem,
+):
+    rep, me, y, x, z, c = position_of()
+    count, width = tok_ref.shape
+    rows, quarter = exp_ref.shape[0], exp_ref.shape[0] // 4
+    units, mix = exp_out.shape[1], proj_out.shape[1]
+    head = mix // 3
+    sibling = (rep, me + 1 - 2 * c)
+    by_x, by_y = (rep + 1 - 2 * x, me), (rep + 2 - 4 * y, me)
+    ring = [(rep, lax.rem(me + k, 8)) for k in range(1, 8)]
+    meet(ring + [by_x, by_y])
+    net = Net(send_sem, recv_sem, local_sem)
+    waits = []
+
+    def weight_copies(go, first, size, source_rows, t):
+        source = rows_at(source_rows, size)
+        target = rows_at(first, size)
+        go(exp_ref.at[source, rows_at(t * units, units)], exp_out.at[target, :])
+        for j in range(3):
+            go(
+                proj_ref.at[source, rows_at(j * width + t * head, head)],
+                proj_out.at[target, pl.ds(j * head, head)],
+            )
+
+    remote = net.slots(24)
+    for step in (1, 2, 3):
+        tz = lax.rem(z + step, 4)
+        for core in (0, 1):
+            part = [0]
+
+            def go(src, dst):
+                net.send(
+                    src, dst, (rep, tz * 2 + core), remote + ((step - 1) * 2 + c) * 4 + part[0]
+                )
+                part[0] += 1
+
+            weight_copies(go, me * rows + rep * quarter, quarter, rep * quarter, tz * 2 + core)
+    near = net.slots(4)
+    part = [0]
+
+    def go_near(src, dst):
+        net.send(src, dst, sibling, near + part[0])
+        part[0] += 1
+
+    weight_copies(go_near, me * rows, rows, 0, sibling[1])
+    copies = []
+    weight_copies(lambda s, d: copies.append(net.local(s, d)), me * rows, rows, 0, me)
+
+    mine = rows_at(me * count, count)
+    small = net.slots(7)
+    for k, peer in enumerate(ring):
+        net.send(vec_ref, vec_out.at[me], peer, small + k)
+    copies.append(net.local(vec_ref, vec_out.at[me]))
+
+    def begin(source, out):
+        left, right, across = net.slots(3), net.slots(3), net.slots(7)
+        copies.append(net.local(source, out.at[mine]))
+        net.send(source, out.at[mine], (rep, me + 2), left, z < 3)
+        net.send(source, out.at[mine], (rep, me - 2), right, z > 0)
+        net.send(source, out.at[mine], sibling, across)
+        return out, left, right, across
+
+    def step_on(state, step):
+        out, left, right, across = state
+        for side, first, here, on in ((-1, left, z >= step, z < 3), (1, right, z + step <= 3, z > 0)):
+            block = out.at[rows_at((me + side * 2 * step) * count, count)]
+            pl.when(here)(lambda: net.arrived(block, sibling, first + step - 1))
+            if step < 3:
+                net.send(block, block, (rep, me - side * 2), first + step, here & on)
+            slot = across + step * 2 - (1 if side < 0 else 0)
+            net.send(block, block, sibling, slot, here)
+
+            def take(side=side, step=step, slot=slot, here=here):
+                block = out.at[rows_at((sibling[1] + side * 2 * step) * count, count)]
+                pl.when(here)(lambda: net.arrived(block, sibling, slot))
+
+            waits.append(take)
+
+    tokens = begin(tok_ref, x_out)
+
+    def shard_rows(step, core):
+        return (lax.rem(z + 4 - step, 4) * 2 + core) * rows
+
+    first_hop = net.slots(12)
+    for step in (1, 2, 3):
+        for core in (0, 1):
+            base = shard_rows(step, core)
+            at = rows_at(base + rep * quarter, quarter)
+            slot = remote + ((step - 1) * 2 + core) * 4
+            net.arrived(exp_out.at[at, :], sibling, slot)
+            for j in range(3):
+                net.arrived(proj_out.at[at, pl.ds(j * head, head)], sibling, slot + 1 + j)
+            peer = by_x if core == 0 else by_y
+            hop = first_hop + ((step - 1) * 2 + core) * 2
+            net.send(exp_out.at[at, :], exp_out.at[at, :], peer, hop)
+            net.send(proj_out.at[at, :], proj_out.at[at, :], peer, hop + 1)
+    step_on(tokens, 1)
+    cotangents = begin(up_ref, up_out)
+    second_hop = net.slots(18)
+    ends = []
+    for step in (1, 2, 3):
+        for core in (0, 1):
+            base = shard_rows(step, core)
+            hop = first_hop + ((step - 1) * 2 + core) * 2
+            if core == 0:
+                other = rows_at(base + (rep + 1 - 2 * x) * quarter, quarter)
+            else:
+                other = rows_at(base + (rep + 2 - 4 * y) * quarter, quarter)
+            net.arrived(exp_out.at[other, :], sibling, hop)
+            net.arrived(proj_out.at[other, :], sibling, hop + 1)
+            hop = second_hop + (step - 1) * 6
+            if core == 0:
+                pieces = [(rows_at(base + y * 2 * quarter, 2 * quarter), by_y, hop)]
+                gone = [(rows_at(base + (1 - y) * 2 * quarter, 2 * quarter), hop)]
+            else:
+                here = rows_at(base + rep * quarter, quarter)
+                pieces = [(here, by_x, hop + 2), (other, by_x, hop + 4)]
+                gone = [
+                    (rows_at(base + (rep + 1 - 2 * x) * quarter, quarter), hop + 2),
+                    (rows_at(base + (3 - rep) * quarter, quarter), hop + 4),
+                ]
+            for at, peer, slot in pieces:
+                net.send(exp_out.at[at, :], exp_out.at[at, :], peer, slot)
+                net.send(proj_out.at[at, :], proj_out.at[at, :], peer, slot + 1)
+            ends += gone
+    step_on(tokens, 2)
+    step_on(tokens, 3)
+    for step in (1, 2, 3):
+        step_on(cotangents, step)
+    for at, slot in ends:
+        net.arrived(exp_out.at[at, :], sibling, slot)
+        net.arrived(proj_out.at[at, :], sibling, slot + 1)
+    at = rows_at(sibling[1] * rows, rows)
+    net.arrived(exp_out.at[at, :], sibling, near)
+    for j in range(3):
+        net.arrived(proj_out.at[at, pl.ds(j * head, head)], sibling, near + 1 + j)
+    for k in range(1, 8):
+        net.arrived(vec_out.at[lax.rem(me + 8 - k, 8)], sibling, small + k - 1)
+    for out, _, _, across in (tokens, cotangents):
+        net.arrived(out.at[rows_at(sibling[1] * count, count)], sibling, across)
+    for take in waits:
+        take()
+    for copy in copies:
+        copy.wait()
+    net.finish()
+    assert net.sends <= GATHER_SEMS and net.started <= GATHER_SEMS and net.locals <= 16
+
+
+GATHER_SEMS = 128
+
+
+def gather(tokens, vectors, upstream, expander, projector):
+    count, width = tokens.shape
+    n = lax.axis_size("shard")
+    units, mix = expander.shape[1] // n, projector.shape[1] // n
+    shapes = [
+        (n * count, width), (n,) + vectors.shape, (n * count, width), (width, units), (width, mix)
+    ]
+    return pl.pallas_call(
+        gather_kernel,
+        out_shape=[jax.ShapeDtypeStruct(s, bf16) for s in shapes],
+        in_specs=[pl.BlockSpec(memory_space=pl.ANY)] * 5,
+        out_specs=[pl.BlockSpec(memory_space=pl.ANY)] * 5,
+        scratch_shapes=[
+            pltpu.SemaphoreType.DMA((GATHER_SEMS,)),
+            pltpu.SemaphoreType.DMA((GATHER_SEMS,)),
+            pltpu.SemaphoreType.DMA((16,)),
+        ],
+        compiler_params=pltpu.CompilerParams(
+            collective_id=0, has_side_effects=True, vmem_limit_bytes=VMEM_LIMIT
+        ),
+    )(tokens, vectors, upstream, expander, projector)
+
+
+def add_into(target, other):
+    rows = target.shape[-2]
+    step = min(32, rows)
+
+    @pl.loop(0, rows // step)
+    def _(i):
+        at = (Ellipsis, pl.ds(pl.multiple_of(i * step, step), step), slice(None))
+        lead = (slice(None),) * (len(target.shape) - 2)
+        at = lead + at[1:]
+        target[at] = (target[at].astype(f32) + other[at].astype(f32)).astype(target.dtype)
+
+
+def settle_kernel(
+    low_ref, he_ref, hp_ref, part_ref, dn_ref, vec_ref, own_ref,
+    low_out, exp_out, proj_out, osum_out, dsum_out, vec_out,
+    low_a, low_a1, low_a2, low_b, low_b1, low_b2,
+    he_a, he_a1, he_a2, he_b, he_b1, he_b2,
+    hp_a, hp_a1, hp_a2, hp_b, hp_b1, hp_b2,
+    o_in, o_sum, o_right, o_left, d_in, d_sum, d_right, d_left,
+    vec_in, vec_mix, vec_all, send_sem, recv_sem, local_sem,
+):
+    rep, me, y, x, z, c = position_of()
+    width = low_ref.shape[-1]
+    units, mix = he_ref.shape[-1], hp_ref.shape[-1]
+    head = mix // 3
+    sibling = (rep, me + 1 - 2 * c)
+    x_rep, y_rep, d_rep = rep + 1 - 2 * x, rep + 2 - 4 * y, 3 - rep
+    by_x, by_y, across = (x_rep, me), (y_rep, me), (d_rep, me)
+    ring = [(rep, lax.rem(me + k, 8)) for k in range(1, 8)]
+    meet(ring + [by_x, by_y, across])
+    net = Net(send_sem, recv_sem, local_sem)
+
+    class Sum:
+        def __init__(self, ref, at, a, a1, a2, b, b1, b2):
+            self.a, self.a1, self.a2, self.b, self.b1, self.b2 = a, a1, a2, b, b1, b2
+            self.loads = []
+            self.slot = net.slots(6)
+            for i in range(2):
+                net.send(at(ref, i * 2 + 1 - x, 0), a1.at[i], by_x, self.slot + i)
+                net.send(at(ref, (1 - y) * 2 + i, 1), b1.at[i], by_y, self.slot + 2 + i)
+                self.loads.append(net.local(at(ref, i * 2 + x, 0), a.at[i]))
+                self.loads.append(net.local(at(ref, y * 2 + i, 1), b.at[i]))
+
+        def second(self):
+            for load in self.loads:
+                load.wait()
+            for i in range(2):
+                net.arrived(self.a1.at[i], sibling, self.slot + i)
+                add_into(self.a.at[i], self.a1.at[i])
+            net.send(self.a.at[1 - y], self.a2, by_y, self.slot + 4)
+            for i in range(2):
+                net.arrived(self.b1.at[i], sibling, self.slot + 2 + i)
+                add_into(self.b.at[i], self.b1.at[i])
+            net.send(self.b.at[1 - x], self.b2, by_x, self.slot + 5)
+
+        def third(self):
+            net.arrived(self.a2, sibling, self.slot + 4)
+            add_into(self.a.at[y], self.a2)
+            net.arrived(self.b2, sibling, self.slot + 5)
+            add_into(self.b.at[x], self.b2)
+            return self.a.at[y], self.b.at[x]
+
+    def deep(ref, quarter, half):
+        return ref.at[:, quarter, half]
+
+    he = Sum(he_ref, deep, he_a, he_a1, he_a2, he_b, he_b1, he_b2)
+    hp = Sum(hp_ref, deep, hp_a, hp_a1, hp_a2, hp_b, hp_b1, hp_b2)
+    low = Sum(
+        low_ref, lambda ref, quarter, half: ref.at[quarter, half],
+        low_a, low_a1, low_a2, low_b, low_b1, low_b2,
+    )
+
+    class Line:
+        def __init__(self, ref, inward, total, right, left):
+            self.inward, self.total, self.right, self.left = inward, total, right, left
+            self.slot = net.slots(10)
+            self.loads = []
+            for i in range(4):
+                net.send(ref.at[i, 1 - c], inward.at[i], sibling, self.slot + i)
+                self.loads.append(net.local(ref.at[i, c], total.at[i]))
+
+        def push(self, block, step, side, when):
+            into = self.right if side > 0 else self.left
+            slot = self.slot + 4 + (step - 1) + (0 if side > 0 else 3)
+            net.send(self.total.at[block], into.at[step - 1], (rep, me + 2 * side), slot, when)
+
+        def begin(self):
+            for i in range(4):
+                self.loads[i].wait()
+                net.arrived(self.inward.at[i], sibling, self.slot + i)
+                add_into(self.total.at[i], self.inward.at[i])
+            for step in (3, 2, 1):
+                self.push(step, step, 1, z == 0)
+                self.push(3 - step, step, -1, z == 3)
+
+        def step_on(self, step):
+            for side, into, first in ((1, self.right, 4), (-1, self.left, 7)):
+                block = z + side * (step - 1)
+                here = (z >= 1) & (block <= 3) if side > 0 else (z <= 2) & (block >= 0)
+
+                @pl.when(here)
+                def _():
+                    net.arrived(into.at[step - 1], sibling, self.slot + first + step - 1)
+                    add_into(self.total.at[block], into.at[step - 1])
+
+                if step > 1:
+                    self.push(block, step - 1, side, here)
+
+    out = Line(part_ref, o_in, o_sum, o_right, o_left)
+    back = Line(dn_ref, d_in, d_sum, d_right, d_left)
+
+    small = net.slots(7)
+    for k in range(1, 8):
+        t = lax.rem(me + k, 8)
+        net.send(vec_ref.at[t], vec_in.at[me], (rep, t), small + k - 1)
+    vec_load = net.local(vec_ref.at[me], vec_in.at[me])
+    own_load = net.local(own_ref, vec_mix.at[pl.ds(56, 16)])
+
+    out.begin()
+    back.begin()
+    he.second()
+    hp.second()
+    for k in range(1, 8):
+        net.arrived(vec_in.at[lax.rem(me + 8 - k, 8)], sibling, small + k - 1)
+    vec_load.wait()
+    own_load.wait()
+    total = vec_in[0, 0:8]
+    for s in range(1, 8):
+        total += vec_in[s, 0:8]
+    vec_mix[0:8] = total
+    for s in range(8):
+        vec_mix[8 + 6 * s : 14 + 6 * s] = vec_in[s, 8:14]
+    wide = net.slots(4)
+    net.send(vec_mix, vec_all.at[rep], by_x, wide + 1)
+    net.send(vec_mix, vec_all.at[rep], by_y, wide + 2)
+    net.send(vec_mix, vec_all.at[rep], across, wide + 3)
+    vec_copy = net.local(vec_mix, vec_all.at[rep])
+    out.step_on(3)
+    back.step_on(3)
+    low.second()
+
+    class Turn:
+        def __init__(self, source, half, place):
+            self.half, self.place = half, place
+            self.slot = net.slots(21)
+            self.copies = []
+            for k in range(1, 8):
+                t = lax.rem(me + k, 8)
+                for j, (src, dst) in enumerate(place(source, t, me)):
+                    net.send(src, dst, (rep, t), self.slot + (k - 1) * 3 + j)
+            for src, dst in place(source, me, me):
+                self.copies.append(net.local(src, dst))
+
+        def wait(self):
+            for k in range(1, 8):
+                s = lax.rem(me + 8 - k, 8)
+                for j, (_, dst) in enumerate(self.place(None, me, s)):
+                    net.arrived(dst, sibling, self.slot + (k - 1) * 3 + j)
+            for copy in self.copies:
+                copy.wait()
+
+    def place_exp(half):
+        return lambda source, t, s: [(
+            None if source is None else source.at[t],
+            exp_out.at[rep, half, :, rows_at(s * units, units)],
+        )]
+
+    def place_proj(half):
+        return lambda source, t, s: [
+            (
+                None if source is None else source.at[t, :, pl.ds(j * head, head)],
+                proj_out.at[rep, half, :, rows_at(j * width + s * head, head)],
+            )
+            for j in range(3)
+        ]
+
+    he_done = he.third()
+    he_turns = [Turn(he_done[h], h, place_exp(h)) for h in range(2)]
+    hp_done = hp.third()
+    hp_turns = [Turn(hp_done[h], h, place_proj(h)) for h in range(2)]
+    out.step_on(2)
+    back.step_on(2)
+
+    class Spread:
+        def __init__(self, target, sources):
+            self.target, self.slot = target, net.slots(6)
+            for h, source in enumerate(sources):
+                for k, peer in enumerate((by_x, by_y)):
+                    net.send(source, target.at[rep, h], peer, self.slot + h * 3 + k)
+
+        def on(self):
+            for h, (k, got, peer) in enumerate(((1, y_rep, by_x), (0, x_rep, by_y))):
+                net.arrived(self.target.at[got, h], sibling, self.slot + h * 3 + k)
+                net.send(self.target.at[got, h], self.target.at[got, h], peer, self.slot + h * 3 + 2)
+
+        def wait(self):
+            for h, (k, got) in enumerate(((0, x_rep), (1, y_rep))):
+                net.arrived(self.target.at[got, h], sibling, self.slot + h * 3 + k)
+                net.arrived(self.target.at[d_rep, h], sibling, self.slot + h * 3 + 2)
+
+    low_done = low.third()
+    low_copies = [net.local(low_done[h], low_out.at[rep, h]) for h in range(2)]
+    low_spread = Spread(low_out, low_done)
+    out.step_on(1)
+    back.step_on(1)
+    for turn in he_turns:
+        turn.wait()
+    he_spread = Spread(exp_out, [exp_out.at[rep, h] for h in range(2)])
+    for turn in hp_turns:
+        turn.wait()
+    hp_spread = Spread(proj_out, [proj_out.at[rep, h] for h in range(2)])
+    low_spread.on()
+    osum_copy = net.local(o_sum.at[z], osum_out)
+    dsum_copy = net.local(d_sum.at[z], dsum_out)
+    for k, r in ((1, x_rep), (2, y_rep), (3, d_rep)):
+        net.arrived(vec_all.at[r], sibling, wide + k)
+    vec_copy.wait()
+    vec_out[...] = (vec_all[0] + vec_all[1]) + (vec_all[2] + vec_all[3])
+    he_spread.on()
+    hp_spread.on()
+    low_spread.wait()
+    he_spread.wait()
+    hp_spread.wait()
+    for copy in low_copies + [osum_copy, dsum_copy]:
+        copy.wait()
+    net.finish()
+    assert net.sends <= SETTLE_SEMS and net.started <= SETTLE_SEMS and net.locals <= 64, (
+        net.sends, net.started, net.locals)
+
+
+SETTLE_SEMS = 224
+
+
+def settle(low, he, hp, part, dn, vec, own):
+    n = lax.axis_size("shard")
+    low_rows, width = low.shape
+    units, mix = he.shape[1], hp.shape[1]
+    rows, eighth, count = width // n, width // n // 8, part.shape[0] // n
+    low = low.reshape(4, 2, low_rows // 8, width)
+    he = he.reshape(n, 4, 2, eighth, units)
+    hp = hp.reshape(n, 4, 2, eighth, mix)
+    part = part.reshape(4, 2, count, width)
+    dn = dn.reshape(4, 2, count, width)
+    vmem = pltpu.VMEM
+
+    def pieces(*shape):
+        return [vmem((2,) + shape, bf16), vmem((2,) + shape, bf16), vmem(shape, bf16)] * 2
+
+    block = (count, width)
+    line = [vmem((k,) + block, bf16) for k in (4, 4, 3, 3)]
+    anywhere = pl.BlockSpec(memory_space=pl.ANY)
+    result = pl.pallas_call(
+        settle_kernel,
+        out_shape=[
+            jax.ShapeDtypeStruct((4, 2, low_rows // 8, width), bf16),
+            jax.ShapeDtypeStruct((4, 2, eighth, n * units), bf16),
+            jax.ShapeDtypeStruct((4, 2, eighth, n * mix), bf16),
+            jax.ShapeDtypeStruct(block, bf16),
+            jax.ShapeDtypeStruct(block, bf16),
+            jax.ShapeDtypeStruct((72, LANES), f32),
+        ],
+        in_specs=[anywhere] * 7,
+        out_specs=[anywhere] * 5 + [pl.BlockSpec(memory_space=vmem)],
+        scratch_shapes=pieces(low_rows // 8, width)
+        + pieces(n, eighth, units) + pieces(n, eighth, mix) + line + line + [
+            vmem((8, 16, LANES), f32), vmem((72, LANES), f32), vmem((4, 72, LANES), f32),
+            pltpu.SemaphoreType.DMA((SETTLE_SEMS,)),
+            pltpu.SemaphoreType.DMA((SETTLE_SEMS,)),
+            pltpu.SemaphoreType.DMA((64,)),
+        ],
+        compiler_params=pltpu.CompilerParams(
+            collective_id=1, has_side_effects=True, vmem_limit_bytes=VMEM_LIMIT
+        ),
+    )(low, he, hp, part, dn, vec, own)
+    low, exp, proj, osum, dsum, vec = result
+    return (
+        low.reshape(low_rows, width), exp.reshape(rows, n * units), proj.reshape(rows, n * mix),
+        osum, dsum, vec,
+    )
 
 
 def sharded_heads(
@@ -574,55 +1016,12 @@
 ):
     count, width = tokens.shape
     n = lax.axis_size("shard")
-    rep = lax.axis_index("rep")
     me = lax.axis_index("shard")
-    y, x, z, c = rep // 2, rep % 2, me // 2, me % 2
     head = width // H
     mix = 3 * head
     rows = width // n
-    quarter = rows // 4
     units = expbias.shape[0]
     wide = projbias.shape[0]
-    both = units + mix
-
-    mine = lax.dynamic_slice_in_dim(expander, rep * quarter, quarter, 0).reshape(quarter, n, units)
-    mine_p = lax.dynamic_slice_in_dim(projector, rep * quarter, quarter, 0)
-    mine_p = mine_p.reshape(quarter, 3, n, head).transpose(0, 2, 1, 3).reshape(quarter, n, mix)
-    cols = jnp.concatenate([mine, mine_p], axis=2).transpose(1, 0, 2).reshape(4, 2, quarter, both)
-    far = [by_z(pick(cols, (z + step) % 4, 0), step) for step in (1, 2, 3)]
-    far = jnp.stack(far)
-    kept = pick(far, c, 1)
-    near = jnp.concatenate(
-        [
-            lax.dynamic_slice_in_dim(expander, (2 * z + 1 - c) * units, units, 1),
-            lax.dynamic_slice_in_dim(
-                projector.reshape(rows, 3, width), (2 * z + 1 - c) * head, head, 2
-            ).reshape(rows, mix),
-        ],
-        axis=1,
-    )
-    near = by_core(near)
-    passed = by_core(pick(far, 1 - c, 1))
-    exp_cols = jnp.zeros((4, 2, 2, 2, quarter, units), bf16)
-    proj_cols = jnp.zeros((4, 2, 2, 2, quarter, mix), bf16)
-    own = lax.dynamic_slice_in_dim(expander, me * units, units, 1)
-    own_p = lax.dynamic_slice_in_dim(projector.reshape(rows, 3, width), me * head, head, 2)
-    exp_cols = put(exp_cols, own, z, c)
-    exp_cols = put(exp_cols, near[:, :units], z, 1 - c)
-    proj_cols = put(proj_cols, own_p.reshape(rows, mix), z, c)
-    proj_cols = put(proj_cols, near[:, units:], z, 1 - c)
-
-    def place(py, px, half, value):
-        nonlocal exp_cols, proj_cols
-        core = c if half == 0 else 1 - c
-        for i, step in enumerate((1, 2, 3)):
-            source = (z - step) % 4
-            exp_cols = put(exp_cols, value[i, :, :units], source, core, py, px)
-            proj_cols = put(proj_cols, value[i, :, units:], source, core, py, px)
-
-    plane_gather(kept, passed, y, x, place)
-    exp_cols = exp_cols.reshape(width, units)
-    proj_cols = proj_cols.reshape(width, mix)
 
     vectors = jnp.concatenate(
         [projbias, combbias, contbias, attendgain, attendshift, feedgain, feedshift,
@@ -630,32 +1029,20 @@
     )
     extra = 16
     vectors = jnp.pad(vectors, (0, extra * width - vectors.shape[0])).reshape(extra, width)
-    chain = [jnp.concatenate([tokens, vectors], axis=0)]
-    for _ in range(3):
-        chain.append(by_z(chain[-1], 1))
-    mine = jnp.stack(chain)
-    others = by_core(mine)
-    slots = jnp.stack([mine, others], axis=1).reshape(n, count + extra, width)
-    x_all = slots[:, :count].reshape(n * count, width)
-    vectors = slots[:, count:].reshape(n, extra * width)
-    order = ((z - jnp.arange(4)) % 4)[:, None] * 2 + jnp.stack([c, 1 - c])[None, :]
-    order = order.reshape(-1)
-    ends = vectors[:, wide + 6 * rows : wide + 6 * rows + DOCS].astype(jnp.int32)
-    placed = jnp.zeros((n, wide + 6 * rows), bf16).at[order].set(vectors[:, : wide + 6 * rows])
-    full_projbias = placed[:, :wide].reshape(3, n, head)
-    my_projbias = pick(full_projbias, me, 1).reshape(1, mix).astype(f32)
-    gains = placed[:, wide:].reshape(n, 6, rows).transpose(1, 0, 2).reshape(6, width).astype(f32)
-    norms = gains[2:]
-
     _, _, live = layout(document_ends[0], count)
     upstream = jnp.where(live[:, None], cotangent, jnp.zeros_like(cotangent))
-    upstream, _ = lax.optimization_barrier((upstream, chain[-1]))
-    chain = [upstream]
-    for _ in range(3):
-        chain.append(by_z(chain[-1], 1))
-    mine = jnp.stack(chain)
-    others = by_core(mine)
-    up_all = jnp.stack([mine, others], axis=1).reshape(n * count, width)
+    x_all, vectors, up_all, exp_cols, proj_cols = gather(
+        tokens, vectors, upstream, expander, projector
+    )
+
+    vectors = vectors.reshape(n, extra * width)
+    ends = vectors[:, wide + 6 * rows : wide + 6 * rows + DOCS].astype(jnp.int32)
+    full_projbias = vectors[:, :wide].reshape(3, n, head)
+    my_projbias = lax.dynamic_index_in_dim(full_projbias, me, 1, keepdims=False)
+    my_projbias = my_projbias.reshape(1, mix).astype(f32)
+    gains = vectors[:, wide : wide + 6 * rows].reshape(n, 6, rows).transpose(1, 0, 2)
+    gains = gains.reshape(6, width).astype(f32)
+    norms = gains[2:]
 
     position = jax.vmap(lambda e: layout(e, count)[0])(ends).reshape(-1)
     half = ROT // 2
@@ -670,104 +1057,53 @@
         count, ends, x_all, cosine, signed, norms, my_projbias, expbias.astype(f32)[None],
         proj_cols, exp_cols, combiner, contractor,
     )
-
-    def group_sums(part):
-        part = part.reshape(4, 2, count, width)
-        acc = added(part[:, 0], by_core(part[:, 1]))
-        total = acc[3]
-        for slot in (2, 1, 0):
-            total = added(acc[slot], by_z(total, -1)) if slot else (
-                acc[0].astype(f32) + by_z(total, -1).astype(f32)
-            )
-        return total
-
-    summed = group_sums(part)
-    floated = tokens.astype(f32)
-    block_output = floated + jnp.where(
-        live[:, None], summed + (gains[0] + gains[1]), 0.0
-    )
-    block_output = block_output.astype(bf16)
-
     low = left_trans(ca, up_all).astype(bf16)
-    low = low.reshape(2, 2, 2, (head + units) // 8, width)
-    low_a, low_b = plane_sums(low, y, x)
     out_bias = jnp.sum(up_all, axis=0, dtype=f32)
-
     dh, dm, dn, sums, hidden_bias, mixed_bias = backward_block(
         count, ends, x_all, up_all, cosine, signed, norms, qkv, slope,
         proj_cols, exp_cols, combiner, contractor,
     )
-    high = jnp.concatenate(
-        [left_trans(h2, dh).astype(bf16), left_trans(h1, dm).astype(bf16)], axis=1
-    )
-    high = high.reshape(n, 2, 2, 2, quarter // 2, both).transpose(1, 2, 3, 0, 4, 5)
-    high_a, high_b = plane_sums(high, y, x)
-
-    low_out = jnp.zeros((2, 2, 2, (head + units) // 8, width), f32)
-
-    def place_low(py, px, half, value):
-        nonlocal low_out
-        low_out = put(low_out, value, py, px, half)
-
-    plane_gather(low_a, low_b, y, x, place_low)
-    low_out = low_out.reshape(head + units, width)
-
-    turned = jnp.stack([high_a, high_b], axis=1).reshape(4, 2, quarter, both)
-    far = [pick(turned, z, 0)] + [by_z(pick(turned, (z + step) % 4, 0), step) for step in (1, 2, 3)]
-    far = jnp.stack(far)
-    kept = pick(far, c, 1)
-    passed = by_core(pick(far, 1 - c, 1))
-    exp_rows = jnp.zeros((4, 2, quarter, units), bf16)
-    proj_rows = jnp.zeros((4, 2, quarter, mix), bf16)
-    for i in range(4):
-        source = (z - i) % 4
-        for core, value in ((c, kept[i]), (1 - c, passed[i])):
-            exp_rows = put(exp_rows, value[:, :units], source, core)
-            proj_rows = put(proj_rows, value[:, units:], source, core)
-    exp_rows = exp_rows.reshape(n, quarter, units).transpose(1, 0, 2).reshape(quarter, n * units)
-    proj_rows = (
-        proj_rows.reshape(n, quarter, 3, head).transpose(1, 2, 0, 3).reshape(quarter, 3 * width)
-    )
-    turned = jnp.concatenate([exp_rows, proj_rows], axis=1)
-    exp_out = jnp.zeros((2, 2, 2, quarter // 2, n * units), f32)
-    proj_out = jnp.zeros((2, 2, 2, quarter // 2, 3 * width), f32)
-
-    def place_high(py, px, half, value):
-        nonlocal exp_out, proj_out
-        exp_out = put(exp_out, value[:, : n * units], py, px, half)
-        proj_out = put(proj_out, value[:, n * units :], py, px, half)
-
-    plane_gather(turned[: quarter // 2], turned[quarter // 2 :], y, x, place_high)
-    exp_out = exp_out.reshape(rows, n * units)
-    proj_out = proj_out.reshape(rows, 3 * width)
-
-    d_normed = group_sums(dn)
-    own_normed, own_inverse = normalize(floated)
-    grad = cotangent.astype(f32) + own_inverse * (
+    he = left_trans(h2, dh).astype(bf16)
+    hp = left_trans(h1, dm).astype(bf16)
+
+    vec = jnp.concatenate(
+        [
+            sums.reshape(4, n, rows).transpose(1, 0, 2).reshape(n, 4 * rows // LANES, LANES),
+            jnp.broadcast_to(mixed_bias.reshape(1, mix // LANES, LANES), (n, mix // LANES, LANES)),
+            jnp.zeros((n, 2, LANES), f32),
+        ],
+        axis=1,
+    )
+    own_out = lax.dynamic_slice(out_bias, (me * rows,), (rows,))
+    own = jnp.concatenate([hidden_bias[0], own_out])
+    own = jnp.pad(own, (0, 16 * LANES - own.shape[0])).reshape(16, LANES)
+    low, exp_out, proj_out, osum, dsum, vec = settle(low, he, hp, part, dn, vec, own)
+
+    floated = tokens.astype(f32)
+    block_output = floated + jnp.where(
+        live[:, None], osum.astype(f32) + (gains[0] + gains[1]), 0.0
+    )
+    block_output = block_output.astype(bf16)
+    d_normed = dsum.astype(f32)
+    normed, inverse = normalize(floated)
+    grad = cotangent.astype(f32) + inverse * (
         d_normed
         - jnp.mean(d_normed, axis=1, keepdims=True)
-        - own_normed * jnp.mean(d_normed * own_normed, axis=1, keepdims=True)
+        - normed * jnp.mean(d_normed * normed, axis=1, keepdims=True)
     )
     input_gradient = grad.astype(bf16)
 
-    mixed_full = jnp.zeros((3, n, head), f32)
-    mixed_full = lax.dynamic_update_slice(mixed_full, mixed_bias.reshape(3, 1, head), (0, me, 0))
-    vector = jnp.concatenate(
-        [
-            mixed_full.reshape(n, wide),
-            sums.reshape(4, n, rows).transpose(1, 0, 2).reshape(n, 4 * rows),
-        ],
-        axis=1,
-    )
-    vector = lax.psum_scatter(vector, "shard", scatter_dimension=0, tiled=True)[0]
-    own_out = lax.dynamic_slice(out_bias, (me * rows,), (rows,))
-    vector = lax.psum(jnp.concatenate([vector, own_out, hidden_bias[0]]), "rep")
-    mixed_bias = vector[:wide]
-    s0, s1, s2, s3, out_bias = (vector[wide + i * rows : wide + (i + 1) * rows] for i in range(5))
-    hidden_bias = vector[wide + 5 * rows :]
+    vec = vec.reshape(-1)
+    norm_sums = vec[: 4 * rows].reshape(4, rows)
+    mixed_bias = vec[4 * rows : 4 * rows + n * mix].reshape(n, 3, head).transpose(1, 0, 2)
+    mixed_bias = lax.dynamic_slice(mixed_bias.reshape(-1), (me * wide,), (wide,))
+    rest = vec[4 * rows + n * mix :]
+    hidden_bias, out_bias = rest[:units], rest[units : units + rows]
+    low = low.astype(f32)
     return (
-        block_output, input_gradient, proj_out, mixed_bias, low_out[:head], out_bias,
-        exp_out, hidden_bias, low_out[head:], out_bias, s0, s1, s2, s3,
+        block_output, input_gradient, proj_out.astype(f32), mixed_bias, low[:head], out_bias,
+        exp_out.astype(f32), hidden_bias, low[head:], out_bias,
+        norm_sums[0], norm_sums[1], norm_sums[2], norm_sums[3],
     )
 
 

time: 841 us -> 688 us (0.82)
  Pallas kernels: 95.7 us -> 584 us
  waiting for transfers between devices: 376 us -> 0 us
  local copies, waits for them, and re-layouts: 141 us -> 18.3 us
  starting transfers between devices: 49.8 us -> 0 us
  other arithmetic: 83.9 us -> 38.3 us
  blocking collectives: 39.4 us -> 0 us
    pallas_call x0 -> x2, Pallas kernels: none -> 488 us  [the longest x1 295 us: settle(): pl.pallas_call(settle_kernel, out_shape=[jax.ShapeDtypeStruct((4, 2, low_...]
    ppermute x45 -> x0, waiting for transfers between devices: 376 us -> none  [send(): return lax.ppermute(value, ('rep', 'shard'), links(move))]
    ppermute x45 -> x0, starting transfers between devices: 49.8 us -> none  [send(): return lax.ppermute(value, ('rep', 'shard'), links(move))]
    dynamic_update_slice x73 -> x0, local copies, waits for them, and re-layouts: 37.4 us -> none  [the longest x72 36.7 us: put(): lax.dynamic_update_slice(buffer, value.reshape((1,) * len(index) + buffer...]
    another operation x16 -> x0, other arithmetic: 27.1 us -> none  [the longest x2 11.4 us: sharded_heads(): slots = jnp.stack([mine, others], axis=1).reshape(n, count + extra, width)]
    unnamed x1 -> x0, blocking collectives: 25.8 us -> none
    slice x12 -> x6, local copies, waits for them, and re-layouts: 22 us -> 6.04 us  [the longest x1 3.98 us: sharded_heads(): low[head:]]
    squeeze x20 -> x1, local copies, waits for them, and re-layouts: 15.4 us -> 0.58 us  [sharded_heads(): norm_sums[3]]
  transfers between devices with their start and end apart: 45 -> 0, of which waited for: 22 -> 0; matrix products, arithmetic and copies ran while one was open for 30% -> 0% of each run, Pallas kernels for 12% -> 0%
where the time goes in v3:
time: 688 us; the launch traced here: 680 us
  Pallas kernels  584 us (85%)
  other arithmetic  38.3 us (6%)
  matrix products  38.3 us (6%)
  local copies, waits for them, and re-layouts  18.3 us (3%)
    pallas_call x1, Pallas kernels, settle(): pl.pallas_call(settle_kernel, out_shape=[jax.ShapeDtypeStruct((4, 2, low_...  295 us
    pallas_call x1, Pallas kernels, gather(): pl.pallas_call(gather_kernel, out_shape=[jax.ShapeDtypeStruct(s, bf16) fo...  193 us
    pallas_call x1, Pallas kernels, backward_block(): pl.pallas_call(backward_kernel, grid_spec=pltpu.PrefetchScalarGridSpec(nu...  49.2 us
    pallas_call x1, Pallas kernels, forward_block(): pl.pallas_call(forward_kernel, grid_spec=pltpu.PrefetchScalarGridSpec(num...  46.6 us
    dot_general x3, matrix products, left_trans(): lax.dot_general(left, right, (((0,), (0,)), ((), ())), preferred_element_...  38.3 us

profile of v3, /device:TPU:10, one launch (start us, length us, event | category | flops | bytes accessed | tf_op | source)
XLA Modules:
  0.0 679.7 jit_solution(5294175586465650156)
XLA Ops:
  0.6 1.2 slice.75
  1.9 0.6 iota_compare_fusion.2
  2.5 0.7 convert_bitcast_fusion.2
  3.2 0.1 pad.20.clone
  3.3 0.1 pad.14.clone
  3.4 0.1 pad.17.clone
  3.5 1.4 convert_reduce_fusion.2
  4.9 1.6 fusion.7
  6.6 1.3 broadcast_in_dim.71
  7.8 0.8 dynamic-update-slice
  8.7 0.8 dynamic-update-slice.1
  9.5 0.8 dynamic-update-slice.2
  10.4 0.8 dynamic-update-slice.3
  11.2 0.8 dynamic-update-slice.4
  12.0 0.8 dynamic-update-slice.5
  12.9 0.8 dynamic-update-slice.6
  13.7 0.2 dynamic-update-slice.7
  13.9 0.7 reshape.169.vec_ref
  14.6 2.3 broadcast_select_fusion.up_ref
  16.9 192.8 %shard_map.254 = (bf16[2048,2048]{1,0:T(8,128)(2,1)}, bf16[8,16,2048]{2,1,0:T(8,128)(2,1)}, bf16[2048,2048]{1,0:T(8,128)(2,1)}, bf16[2048,1024]{1,0:T(8,128)(2,1)}, bf16[2048,768]{1,0:T(8,128)(2,1)}) custom-call(bf16[256,2048]{1,0:T(8,128)(2,1)} %tok_ref.1, bf16[16,2048]{1,0:T(8,128)(2,1)} %reshape.169.vec_ref, ...), custom_call_target="tpu_custom_call" | custom-call | tf_op jit(solution)/shard_map/pallas_call | solution.py:716
  209.8 1.3 copy.39
  211.1 0.1 copy.35
  211.2 0.1 select_reduce_fusion
  211.3 4.7 convert_reduce_fusion
  216.0 0.1 dynamic_slice.11
  216.2 0.6 convert.9.pbias_ref
  216.8 0.6 copy.41
  217.4 3.7 fusion.10
  221.1 1.9 maximum_maximum_fusion
  223.1 46.6 %shard_map.255 = (bf16[2048,2048]{1,0:T(8,128)(2,1)}, bf16[2048,2048]{1,0:T(8,128)(2,1)}, bf16[2048,768]{1,0:T(8,128)(2,1)}, bf16[2048,1280]{1,0:T(8,128)(2,1)},...) custom-call(s32[8,4]{1,0:T(8,128)} %copy-done.5, bf16[2048,2048]{1,0:T(8,128)(2,1)} %get-tuple-element.38.x_ref, ...), custom_call_target="tpu_custom_call" | custom-call | flops 25769803776 | bytes 37748736 | tf_op jit(solution)/shard_map/pallas_call | solution.py:452
  269.7 49.2 %shard_map.256 = (bf16[2048,1024]{1,0:T(8,128)(2,1)}, bf16[2048,768]{1,0:T(8,128)(2,1)}, bf16[2048,2048]{1,0:T(8,128)(2,1)}, f32[4,2048]{1,0:T(4,128)}, f32[1,1024]{1,0:T(1,128)}, /*index=5*/f32[1,768]{1,0:T(1,128)}) custom-call(s32[8,4]{1,0:T(8,128)} %copy-done.5, bf16[2048,2048]{1,0:T(8,128)(2,1)} %get-tuple-element.38.x_ref, ...), custom_call_target="tpu_custom_call" | custom-call | flops 25769803776 | bytes 33554432 | tf_op jit(solution)/shard_map/pallas_call | solution.py:474
  318.9 17.0 %convolution_convert_fusion = bf16[1280,2048]{1,0:T(8,128)(2,1)} fusion(bf16[2048,1280]{1,0:T(8,128)(2,1)} %get-tuple-element.41, bf16[2048,2048]{1,0:T(8,128)(2,1)} %get-tuple-element.42.up_ref), kind=kOutput, calls=%fused_computation.1 | convolution fusion | flops 10740039680 | bytes 18874368 | tf_op jit(solution)/shard_map/dot_general | solution.py:69
  335.9 10.5 %convolution_convert_fusion.1 = bf16[2048,1024]{1,0:T(8,128)(2,1)} fusion(bf16[2048,2048]{1,0:T(8,128)(2,1)S(1)} %copy-done.9, bf16[2048,1024]{1,0:T(8,128)(2,1)S(1)} %copy-done.11), kind=kOutput, calls=%fused_computation.4 | convolution fusion | flops 8592031744 | bytes 16777216 | tf_op jit(solution)/shard_map/dot_general | solution.py:69
  346.5 0.6 fusion.12.own_ref
  347.1 0.7 maximum_maximum_fusion.2.vec_ref
  347.8 10.8 %convolution_convert_fusion.2 = bf16[2048,768]{1,0:T(8,128)(2,1)} fusion(bf16[2048,2048]{1,0:T(8,128)(2,1)} %get-tuple-element.47, bf16[2048,768]{1,0:T(8,128)(2,1)S(1)} %copy-done.10), kind=kOutput, calls=%fused_computation.5 | convolution fusion | flops 6444023808 | bytes 14680064 | tf_op jit(solution)/shard_map/dot_general | solution.py:69
  358.6 295.0 %shard_map.257 = (bf16[4,2,160,2048]{3,2,1,0:T(8,128)(2,1)}, bf16[4,2,32,8192]{3,2,1,0:T(8,128)(2,1)}, bf16[4,2,32,6144]{3,2,1,0:T(8,128)(2,1)}, bf16[256,2048]{...) custom-call(bf16[4,2,160,2048]{3,2,1,0:T(8,128)(2,1)} %bitcast.69, ...), custom_call_target="tpu_custom_call" | custom-call | tf_op jit(solution)/shard_map/pallas_call | solution.py:983
  653.6 1.9 convert_reduce_fusion.1
  655.6 3.9 fusion.6
  659.5 0.6 slice_bitcast_fusion.1
  660.1 0.6 slice_bitcast_fusion.2
  660.7 0.7 dynamic_slice.12
  661.4 5.6 bitcast_convert_fusion.2
  667.0 4.7 bitcast_convert_fusion.1
  671.7 1.7 bitcast_convert_fusion
  673.4 1.5 slice.100
  674.9 4.0 slice.101
  678.9 0.6 copy.55
  (57 shorter events, 0.3 us)
Async XLA Ops:
  211.1 4.9 copy-start.5
  318.9 17.0 %copy-start.9 = (bf16[2048,2048]{1,0:T(8,128)(2,1)S(1)}, bf16[2048,2048]{1,0:T(8,128)(2,1)}, u32[]{:S(2)}) copy-start(bf16[2048,2048]{1,0:T(8,128)(2,1)} %get-tuple-element.43) | copy-start | bytes 25165828
  318.9 17.0 %copy-start.11 = (bf16[2048,1024]{1,0:T(8,128)(2,1)S(1)}, bf16[2048,1024]{1,0:T(8,128)(2,1)}, u32[]{:S(2)}) copy-start(bf16[2048,1024]{1,0:T(8,128)(2,1)} %get-tuple-element.46) | copy-start | bytes 12582916
  335.9 10.6 %copy-start.8 = (f32[1,768]{1,0:T(1,128)S(1)}, f32[1,768]{1,0:T(1,128)}, u32[]{:S(2)}) copy-start(f32[1,768]{1,0:T(1,128)} %get-tuple-element.52) | copy-start | bytes 9220
  335.9 10.6 %copy-start.7 = (f32[1,1024]{1,0:T(1,128)S(1)}, f32[1,1024]{1,0:T(1,128)}, u32[]{:S(2)}) copy-start(f32[1,1024]{1,0:T(1,128)} %get-tuple-element.53) | copy-start | bytes 12292
  335.9 11.2 %copy-start.3 = (f32[4,2048]{1,0:T(4,128)S(1)}, f32[4,2048]{1,0:T(4,128)}, u32[]{:S(2)}) copy-start(f32[4,2048]{1,0:T(4,128)} %get-tuple-element.51) | copy-start | bytes 98308
  335.9 11.9 %copy-start.10 = (bf16[2048,768]{1,0:T(8,128)(2,1)S(1)}, bf16[2048,768]{1,0:T(8,128)(2,1)}, u32[]{:S(2)}) copy-start(bf16[2048,768]{1,0:T(8,128)(2,1)} %get-tuple-element.48) | copy-start | bytes 9437188
  358.6 295.0 %copy-start = (bf16[256,2048]{1,0:T(8,128)(2,1)S(1)}, bf16[256,2048]{1,0:T(8,128)(2,1)}, u32[]{:S(2)}) copy-start(bf16[256,2048]{1,0:T(8,128)(2,1)} %tok_ref.1) | copy-start | bytes 3145732
  358.6 297.0 %copy-start.2 = (bf16[256,2048]{1,0:T(8,128)(2,1)S(1)}, bf16[256,2048]{1,0:T(8,128)(2,1)}, u32[]{:S(2)}) copy-start(bf16[256,2048]{1,0:T(8,128)(2,1)} %param.29) | copy-start | bytes 3145732
  653.6 5.9 copy-start.4
  660.7 18.2 %copy-start.6 = (f32[256]{0:T(256)}, f32[256]{0:T(256)S(1)}, u32[]{:S(2)}) copy-start(f32[256]{0:T(256)S(1)} %get-tuple-element.97) | copy-start | bytes 3076
  661.4 5.6 copy-start.1
  661.4 10.3 %slice-start = ((s8[5242880]{0:T(1024)(128)(4,1)}), s8[4194304]{0:T(1024)(128)(4,1)S(1)}, s32[]{:S(2)}) async-start(s8[5242880]{0:T(1024)(128)(4,1)} %bitcast.67), calls=%async_computation | async-start | bytes 8388608
  667.0 4.7 slice-start.1

commit v4 on v3

--- a/solution.py
+++ b/solution.py
@@ -314,16 +314,18 @@
     return jnp.concatenate([front * cosine - turn(front, signed), grads[:, LANES:]], axis=1)
 
 
-def block_allowed(ends_ref, block, count):
-    row = lax.broadcasted_iota(jnp.int32, (count, 1), 0)
-    column = lax.broadcasted_iota(jnp.int32, (1, count), 1)
-    row_doc = jnp.zeros((count, 1), jnp.int32)
-    column_doc = jnp.zeros((1, count), jnp.int32)
+def block_layout(ends, count):
+    row = lax.broadcasted_iota(jnp.int32, (count, 1), 0).astype(f32)
+    column = lax.broadcasted_iota(jnp.int32, (1, count), 1).astype(f32)
+    row_doc = jnp.zeros((count, 1), f32)
+    column_doc = jnp.zeros((1, count), f32)
+    begin = jnp.zeros((count, 1), f32)
     for i in range(DOCS):
-        end = ends_ref[block, i]
-        row_doc += (row >= end).astype(jnp.int32)
-        column_doc += (column >= end).astype(jnp.int32)
-    return (row_doc == column_doc) & (column <= row)
+        end = ends[:, i : i + 1]
+        row_doc += jnp.where(row >= end, 1.0, 0.0)
+        column_doc += jnp.where(column >= end, 1.0, 0.0)
+        begin = jnp.maximum(begin, jnp.where(row >= end, end, 0.0))
+    return (row_doc == column_doc) & (column <= row), row - begin
 
 
 def dot(left, right):
@@ -337,33 +339,32 @@
     return raised / jnp.sum(raised, axis=1, keepdims=True)
 
 
-def forward_kernel(
-    ends_ref, x_ref, cos_ref, sin_ref, norms_ref, pbias_ref, ebias_ref,
-    proj_ref, exp_ref, comb_ref, cont_ref,
-    h1_ref, h2_ref, qkv_ref, ca_ref, slope_ref, part_ref,
+def forward_block(
+    x_ref, ends, angles_ref, norms_ref, pbias_ref, ebias_ref, proj_ref, exp_ref, comb_ref,
+    cont_ref, h1_ref, h2_ref, qkv_ref, ca_ref, slope_ref, part_ref,
 ):
-    block = pl.program_id(0)
     count, width = x_ref.shape
     head = comb_ref.shape[0]
     units = exp_ref.shape[1]
+    allowed, place = block_layout(ends, count)
+    angles = place * angles_ref[0:1, :]
+    cosine, signed = jnp.cos(angles), jnp.sin(angles) * angles_ref[1:2, :]
     normed, _ = normalize(x_ref[...].astype(f32))
-    first = (normed * norms_ref[0:1, :] + norms_ref[1:2, :]).astype(bf16)
-    h1_ref[...] = first
-    second = (normed * norms_ref[2:3, :] + norms_ref[3:4, :]).astype(bf16)
-    h2_ref[...] = second
-    cosine, signed = cos_ref[...], sin_ref[...]
-    mixed = dot(first, proj_ref[...]) + pbias_ref[...]
+    h1_ref[...] = (normed * norms_ref[0:1, :] + norms_ref[1:2, :]).astype(bf16)
+    h2_ref[...] = (normed * norms_ref[2:3, :] + norms_ref[3:4, :]).astype(bf16)
+    mixed = dot(h1_ref[...], proj_ref[...]) + pbias_ref[...]
     q = rotated(mixed[:, :head], cosine, signed).astype(bf16)
     k = rotated(mixed[:, head : 2 * head], cosine, signed).astype(bf16)
     v = mixed[:, 2 * head :].astype(bf16)
     qkv_ref[:, :head] = q
     qkv_ref[:, head : 2 * head] = k
     qkv_ref[:, 2 * head :] = v
-    probs = softmax(q, k, block_allowed(ends_ref, block, count)).astype(bf16)
+    probs = softmax(q, k, allowed).astype(bf16)
     ca_ref[:, :head] = dot(probs, v).astype(bf16)
     tile = min(256, units)
     for start in range(0, units, tile):
-        hidden = dot(second, exp_ref[:, start : start + tile]) + ebias_ref[:, start : start + tile]
+        hidden = dot(h2_ref[...], exp_ref[:, start : start + tile])
+        hidden += ebias_ref[:, start : start + tile]
         below = 0.5 + 0.5 * lax.erf(hidden * math.sqrt(0.5))
         ca_ref[:, head + start : head + start + tile] = (hidden * below).astype(bf16)
         density = jnp.exp(hidden * hidden * -0.5) * (1.0 / math.sqrt(2.0 * math.pi))
@@ -375,42 +376,35 @@
         part_ref[:, cut] = part.astype(bf16)
 
 
-def backward_kernel(
-    ends_ref, x_ref, up_ref, cos_ref, sin_ref, norms_ref, qkv_ref, slope_ref,
-    proj_ref, exp_ref, comb_ref, cont_ref,
-    dh_ref, dm_ref, dn_ref, sums_ref, hbias_ref, mbias_ref,
+def backward_block(
+    x_ref, up_ref, ends, angles_ref, norms_ref, qkv_ref, slope_ref, proj_ref, exp_ref, comb_ref,
+    cont_ref, dh_ref, dm_ref, dn_ref, sums_ref, hbias_ref, mbias_ref, obias_ref,
 ):
-    block = pl.program_id(0)
     count, width = x_ref.shape
     head = comb_ref.shape[0]
     units = exp_ref.shape[1]
-    up = up_ref[...]
-
-    @pl.when(block == 0)
-    def _():
-        sums_ref[...] = jnp.zeros_like(sums_ref)
-        hbias_ref[...] = jnp.zeros_like(hbias_ref)
-        mbias_ref[...] = jnp.zeros_like(mbias_ref)
-
-    d_context = right_trans(up, comb_ref[...]).astype(bf16)
+    allowed, place = block_layout(ends, count)
+    angles = place * angles_ref[0:1, :]
+    cosine, signed = jnp.cos(angles), jnp.sin(angles) * angles_ref[1:2, :]
+    d_context = right_trans(up_ref[...], comb_ref[...]).astype(bf16)
     q, k, v = qkv_ref[:, :head], qkv_ref[:, head : 2 * head], qkv_ref[:, 2 * head :]
-    probs = softmax(q, k, block_allowed(ends_ref, block, count))
+    probs = softmax(q, k, allowed)
     d_probs = right_trans(d_context, v)
     d_v = left_trans(probs.astype(bf16), d_context)
     d_s = probs * (d_probs - jnp.sum(d_probs * probs, axis=1, keepdims=True))
     d_s = d_s.astype(bf16)
     factor = 1.0 / math.sqrt(head)
-    cosine, signed = cos_ref[...], sin_ref[...]
-    d_q = unrotated(dot(d_s, k) * factor, cosine, signed).astype(bf16)
+    dm_ref[:, :head] = unrotated(dot(d_s, k) * factor, cosine, signed).astype(bf16)
     d_k = unrotated(left_trans(d_s, q) * factor, cosine, signed).astype(bf16)
-    dm_ref[:, :head] = d_q
     dm_ref[:, head : 2 * head] = d_k
     dm_ref[:, 2 * head :] = d_v.astype(bf16)
     mbias_ref[...] += jnp.sum(dm_ref[...].astype(f32), axis=0, keepdims=True)
+    obias_ref[...] += jnp.sum(up_ref[...].astype(f32), axis=0, keepdims=True)
     tile = min(256, units)
     for start in range(0, units, tile):
         cut = slice(start, start + tile)
-        d_hidden = (right_trans(up, cont_ref[cut, :]) * slope_ref[:, cut].astype(f32)).astype(bf16)
+        d_active = right_trans(up_ref[...], cont_ref[cut, :])
+        d_hidden = (d_active * slope_ref[:, cut].astype(f32)).astype(bf16)
         dh_ref[:, cut] = d_hidden
         hbias_ref[:, cut] += jnp.sum(d_hidden.astype(f32), axis=0, keepdims=True)
     x = x_ref[...].astype(f32)
@@ -432,66 +426,17 @@
         sums_ref[3:4, cut] += jnp.sum(d_second, axis=0, keepdims=True)
 
 
-def rows_spec(count, columns):
-    return pl.BlockSpec((count, columns), lambda i, *_: (i, 0))
-
-
-def whole_spec(array):
-    return pl.BlockSpec(array.shape, lambda i, *_: (0, 0), pipeline_mode=pl.Buffered(1))
-
-
-def acc_spec(rows, columns):
-    return pl.BlockSpec((rows, columns), lambda i, *_: (0, 0))
-
-
-def forward_block(count, ends, x, cosine, signed, norms, pbias, ebias, proj, exp, comb, cont):
-    slots, width = x.shape
-    units, mix, head = exp.shape[1], proj.shape[1], comb.shape[0]
-    flops = 2 * slots * width * (mix + 2 * units + head)
-    wide = [width, width, mix, head + units, units, width]
-    return pl.pallas_call(
-        forward_kernel,
-        grid_spec=pltpu.PrefetchScalarGridSpec(
-            num_scalar_prefetch=1,
-            grid=(slots // count,),
-            in_specs=[
-                rows_spec(count, width), rows_spec(count, LANES), rows_spec(count, LANES),
-            ] + [whole_spec(a) for a in (norms, pbias, ebias, proj, exp, comb, cont)],
-            out_specs=[rows_spec(count, w) for w in wide],
-        ),
-        out_shape=[jax.ShapeDtypeStruct((slots, w), bf16) for w in wide],
-        compiler_params=pltpu.CompilerParams(vmem_limit_bytes=VMEM_LIMIT),
-        cost_estimate=pl.CostEstimate(
-            flops=flops, bytes_accessed=2 * slots * sum(wide), transcendentals=0
-        ),
-    )(ends, x, cosine, signed, norms, pbias, ebias, proj, exp, comb, cont)
-
-
-def backward_block(count, ends, x, up, cosine, signed, norms, qkv, slope, proj, exp, comb, cont):
-    slots, width = x.shape
-    units, mix, head = exp.shape[1], proj.shape[1], comb.shape[0]
-    flops = 2 * slots * width * (mix + 2 * units + head)
-    return pl.pallas_call(
-        backward_kernel,
-        grid_spec=pltpu.PrefetchScalarGridSpec(
-            num_scalar_prefetch=1,
-            grid=(slots // count,),
-            in_specs=[
-                rows_spec(count, width), rows_spec(count, width),
-                rows_spec(count, LANES), rows_spec(count, LANES), whole_spec(norms),
-                rows_spec(count, mix), rows_spec(count, units),
-            ] + [whole_spec(a) for a in (proj, exp, comb, cont)],
-            out_specs=[rows_spec(count, w) for w in (units, mix, width)]
-            + [acc_spec(4, width), acc_spec(1, units), acc_spec(1, mix)],
-        ),
-        out_shape=[jax.ShapeDtypeStruct((slots, w), bf16) for w in (units, mix, width)]
-        + [jax.ShapeDtypeStruct(s, f32) for s in ((4, width), (1, units), (1, mix))],
-        compiler_params=pltpu.CompilerParams(vmem_limit_bytes=VMEM_LIMIT),
-        cost_estimate=pl.CostEstimate(
-            flops=flops, bytes_accessed=2 * slots * (3 * width + 2 * units), transcendentals=0
-        ),
-    )(ends, x, up, cosine, signed, norms, qkv, slope, proj, exp, comb, cont)
+def accumulate(total, left, right):
+    tile = min(256, left.shape[1])
+
+    @pl.loop(0, left.shape[1] // tile)
+    def _(i):
+        at = pl.ds(pl.multiple_of(i * tile, tile), tile)
+        total[at, :] += left_trans(left[:, at], right[...])
+
+
 MESH = pl.DeviceIdType.MESH
+GATHER_SEMS = 96
 
 
 def position_of():
@@ -553,30 +498,137 @@
                 pl.when(when)(lambda copy=copy: copy.wait_send())
 
 
-def gather_kernel(
-    tok_ref, vec_ref, up_ref, exp_ref, proj_ref,
-    x_out, vec_out, up_out, exp_out, proj_out, send_sem, recv_sem, local_sem,
+class Chain:
+    def __init__(self, source, out, count, where, sems):
+        self.source, self.out, self.count = source, out, count
+        self.rep, self.me, self.z, self.c = where
+        self.side_send, self.side_recv, self.core_send, self.core_recv, self.local_sem = sems
+        self.sibling = self.me + 1 - 2 * self.c
+
+    def block(self, shard):
+        return self.out.at[rows_at(shard * self.count, self.count)]
+
+    def side(self, side, step):
+        block = self.block(self.me - side * 2 * step)
+        peer = (self.rep, self.me + side * 2)
+        index = (0 if side > 0 else 4) + step
+        return pltpu.make_async_remote_copy(
+            src_ref=block, dst_ref=block, send_sem=self.side_send.at[index],
+            recv_sem=self.side_recv.at[index], device_id=peer, device_id_type=MESH,
+        )
+
+    def cross(self, side, step):
+        block = self.block(self.me - side * 2 * step)
+        index = (0 if side > 0 else 4) + step
+        return pltpu.make_async_remote_copy(
+            src_ref=block, dst_ref=block, send_sem=self.core_send.at[index],
+            recv_sem=self.core_recv.at[index], device_id=(self.rep, self.sibling),
+            device_id_type=MESH,
+        )
+
+    def taken(self, side, step):
+        block = self.block(self.sibling - side * 2 * step)
+        index = (0 if side > 0 else 4) + step
+        return pltpu.make_async_remote_copy(
+            src_ref=block, dst_ref=block, send_sem=self.core_send.at[index],
+            recv_sem=self.core_recv.at[index], device_id=(self.rep, self.sibling),
+            device_id_type=MESH,
+        )
+
+    def here(self, side, step):
+        return self.z >= step if side > 0 else self.z + step <= 3
+
+    def on(self, side):
+        return self.z < 3 if side > 0 else self.z > 0
+
+    def first(self, side):
+        mine = self.block(self.me)
+        index = 0 if side > 0 else 4
+        return pltpu.make_async_remote_copy(
+            src_ref=self.source, dst_ref=mine, send_sem=self.side_send.at[index],
+            recv_sem=self.side_recv.at[index], device_id=(self.rep, self.me + side * 2),
+            device_id_type=MESH,
+        )
+
+    def first_cross(self):
+        mine = self.block(self.me)
+        return pltpu.make_async_remote_copy(
+            src_ref=self.source, dst_ref=mine, send_sem=self.core_send.at[0],
+            recv_sem=self.core_recv.at[0], device_id=(self.rep, self.sibling),
+            device_id_type=MESH,
+        )
+
+    def begin(self):
+        for side in (1, -1):
+            pl.when(self.on(side))(lambda: self.first(side).start())
+        self.first_cross().start()
+        pltpu.make_async_copy(self.source, self.block(self.me), self.local_sem).start()
+
+    def wait_own(self):
+        pltpu.make_async_copy(self.source, self.block(self.me), self.local_sem).wait()
+        self.taken(1, 0).wait_recv()
+
+    def step(self, step):
+        for side in (1, -1):
+            here = self.here(side, step)
+
+            @pl.when(here)
+            def _():
+                block = self.block(self.me - side * 2 * step)
+                index = (0 if side > 0 else 4) + step - 1
+                pltpu.make_async_remote_copy(
+                    src_ref=block, dst_ref=block, send_sem=self.side_send.at[index],
+                    recv_sem=self.side_recv.at[index], device_id=(self.rep, self.sibling),
+                    device_id_type=MESH,
+                ).wait_recv()
+                self.cross(side, step).start()
+
+            pl.when(here & self.on(side) & (step < 3))(lambda: self.side(side, step).start())
+
+    def take(self, step):
+        for side in (1, -1):
+            pl.when(self.here(side, step))(lambda: self.taken(side, step).wait_recv())
+
+    def finish(self):
+        self.first_cross().wait_send()
+        for side in (1, -1):
+            pl.when(self.on(side))(lambda: self.first(side).wait_send())
+            for step in (1, 2, 3):
+                here = self.here(side, step)
+                pl.when(here)(lambda: self.cross(side, step).wait_send())
+                if step < 3:
+                    pl.when(here & self.on(side))(lambda: self.side(side, step).wait_send())
+
+
+def block_kernel(
+    tok_ref, vec_ref, up_ref, expander_ref, projector_ref, comb_hbm, cont_hbm, ebias_ref,
+    angles_ref,
+    x_out, up_out, low_out, he_out, hp_out, part_out, dn_out, vec_out, own_out, norms_ref,
+    exp_ref, proj_ref, comb_ref, cont_ref, low_sum, he_sum, hp_sum,
+    xs, us, h1s, h2s, ca, slope, qkv, dh, dm, parts, dns,
+    vecs, bias_all, ends_all, pbias, sums, hbias, mbias, obias,
+    send_sem, recv_sem, local_sem, load_sem, store_sem,
+    xs_send, xs_recv, xc_send, xc_recv, us_send, us_recv, uc_send, uc_recv, own_sem,
 ):
     rep, me, y, x, z, c = position_of()
     count, width = tok_ref.shape
-    rows, quarter = exp_ref.shape[0], exp_ref.shape[0] // 4
-    units, mix = exp_out.shape[1], proj_out.shape[1]
+    rows, quarter = expander_ref.shape[0], expander_ref.shape[0] // 4
+    units, mix = exp_ref.shape[1], proj_ref.shape[1]
     head = mix // 3
     sibling = (rep, me + 1 - 2 * c)
     by_x, by_y = (rep + 1 - 2 * x, me), (rep + 2 - 4 * y, me)
     ring = [(rep, lax.rem(me + k, 8)) for k in range(1, 8)]
     meet(ring + [by_x, by_y])
     net = Net(send_sem, recv_sem, local_sem)
-    waits = []
 
     def weight_copies(go, first, size, source_rows, t):
         source = rows_at(source_rows, size)
         target = rows_at(first, size)
-        go(exp_ref.at[source, rows_at(t * units, units)], exp_out.at[target, :])
+        go(expander_ref.at[source, rows_at(t * units, units)], exp_ref.at[target, :])
         for j in range(3):
             go(
-                proj_ref.at[source, rows_at(j * width + t * head, head)],
-                proj_out.at[target, pl.ds(j * head, head)],
+                projector_ref.at[source, rows_at(j * width + t * head, head)],
+                proj_ref.at[target, pl.ds(j * head, head)],
             )
 
     remote = net.slots(24)
@@ -592,6 +644,17 @@
                 part[0] += 1
 
             weight_copies(go, me * rows + rep * quarter, quarter, rep * quarter, tz * 2 + core)
+    small = net.slots(7)
+    for k, peer in enumerate(ring):
+        net.send(vec_ref, vecs.at[me], peer, small + k)
+    where = (rep, me, z, c)
+    tokens = Chain(
+        tok_ref, x_out, count, where, (xs_send, xs_recv, xc_send, xc_recv, own_sem.at[0])
+    )
+    cotangents = Chain(
+        up_ref, up_out, count, where, (us_send, us_recv, uc_send, uc_recv, own_sem.at[1])
+    )
+    tokens.begin()
     near = net.slots(4)
     part = [0]
 
@@ -602,38 +665,18 @@
     weight_copies(go_near, me * rows, rows, 0, sibling[1])
     copies = []
     weight_copies(lambda s, d: copies.append(net.local(s, d)), me * rows, rows, 0, me)
-
-    mine = rows_at(me * count, count)
-    small = net.slots(7)
-    for k, peer in enumerate(ring):
-        net.send(vec_ref, vec_out.at[me], peer, small + k)
-    copies.append(net.local(vec_ref, vec_out.at[me]))
-
-    def begin(source, out):
-        left, right, across = net.slots(3), net.slots(3), net.slots(7)
-        copies.append(net.local(source, out.at[mine]))
-        net.send(source, out.at[mine], (rep, me + 2), left, z < 3)
-        net.send(source, out.at[mine], (rep, me - 2), right, z > 0)
-        net.send(source, out.at[mine], sibling, across)
-        return out, left, right, across
-
-    def step_on(state, step):
-        out, left, right, across = state
-        for side, first, here, on in ((-1, left, z >= step, z < 3), (1, right, z + step <= 3, z > 0)):
-            block = out.at[rows_at((me + side * 2 * step) * count, count)]
-            pl.when(here)(lambda: net.arrived(block, sibling, first + step - 1))
-            if step < 3:
-                net.send(block, block, (rep, me - side * 2), first + step, here & on)
-            slot = across + step * 2 - (1 if side < 0 else 0)
-            net.send(block, block, sibling, slot, here)
-
-            def take(side=side, step=step, slot=slot, here=here):
-                block = out.at[rows_at((sibling[1] + side * 2 * step) * count, count)]
-                pl.when(here)(lambda: net.arrived(block, sibling, slot))
-
-            waits.append(take)
-
-    tokens = begin(tok_ref, x_out)
+    copies.append(net.local(vec_ref, vecs.at[me]))
+    copies.append(net.local(comb_hbm, comb_ref))
+    copies.append(net.local(cont_hbm, cont_ref))
+    cotangents.begin()
+    for ref in (low_sum, he_sum, hp_sum, sums, hbias, mbias, obias):
+        if ref.shape[0] <= 8:
+            ref[...] = jnp.zeros_like(ref)
+        else:
+
+            @pl.loop(0, ref.shape[0] // 64)
+            def _(i):
+                ref[rows_at(i * 64, 64), :] = jnp.zeros((64, ref.shape[1]), f32)
 
     def shard_rows(step, core):
         return (lax.rem(z + 4 - step, 4) * 2 + core) * rows
@@ -644,17 +687,16 @@
             base = shard_rows(step, core)
             at = rows_at(base + rep * quarter, quarter)
             slot = remote + ((step - 1) * 2 + core) * 4
-            net.arrived(exp_out.at[at, :], sibling, slot)
+            net.arrived(exp_ref.at[at, :], sibling, slot)
             for j in range(3):
-                net.arrived(proj_out.at[at, pl.ds(j * head, head)], sibling, slot + 1 + j)
+                net.arrived(proj_ref.at[at, pl.ds(j * head, head)], sibling, slot + 1 + j)
             peer = by_x if core == 0 else by_y
             hop = first_hop + ((step - 1) * 2 + core) * 2
-            net.send(exp_out.at[at, :], exp_out.at[at, :], peer, hop)
-            net.send(proj_out.at[at, :], proj_out.at[at, :], peer, hop + 1)
-    step_on(tokens, 1)
-    cotangents = begin(up_ref, up_out)
+            net.send(exp_ref.at[at, :], exp_ref.at[at, :], peer, hop)
+            net.send(proj_ref.at[at, :], proj_ref.at[at, :], peer, hop + 1)
+    tokens.step(1)
     second_hop = net.slots(18)
-    ends = []
+    gone = []
     for step in (1, 2, 3):
         for core in (0, 1):
             base = shard_rows(step, core)
@@ -663,70 +705,198 @@
                 other = rows_at(base + (rep + 1 - 2 * x) * quarter, quarter)
             else:
                 other = rows_at(base + (rep + 2 - 4 * y) * quarter, quarter)
-            net.arrived(exp_out.at[other, :], sibling, hop)
-            net.arrived(proj_out.at[other, :], sibling, hop + 1)
+            net.arrived(exp_ref.at[other, :], sibling, hop)
+            net.arrived(proj_ref.at[other, :], sibling, hop + 1)
             hop = second_hop + (step - 1) * 6
             if core == 0:
                 pieces = [(rows_at(base + y * 2 * quarter, 2 * quarter), by_y, hop)]
-                gone = [(rows_at(base + (1 - y) * 2 * quarter, 2 * quarter), hop)]
+                gone += [(rows_at(base + (1 - y) * 2 * quarter, 2 * quarter), hop)]
             else:
                 here = rows_at(base + rep * quarter, quarter)
                 pieces = [(here, by_x, hop + 2), (other, by_x, hop + 4)]
-                gone = [
+                gone += [
                     (rows_at(base + (rep + 1 - 2 * x) * quarter, quarter), hop + 2),
                     (rows_at(base + (3 - rep) * quarter, quarter), hop + 4),
                 ]
             for at, peer, slot in pieces:
-                net.send(exp_out.at[at, :], exp_out.at[at, :], peer, slot)
-                net.send(proj_out.at[at, :], proj_out.at[at, :], peer, slot + 1)
-            ends += gone
-    step_on(tokens, 2)
-    step_on(tokens, 3)
-    for step in (1, 2, 3):
-        step_on(cotangents, step)
-    for at, slot in ends:
-        net.arrived(exp_out.at[at, :], sibling, slot)
-        net.arrived(proj_out.at[at, :], sibling, slot + 1)
-    at = rows_at(sibling[1] * rows, rows)
-    net.arrived(exp_out.at[at, :], sibling, near)
-    for j in range(3):
-        net.arrived(proj_out.at[at, pl.ds(j * head, head)], sibling, near + 1 + j)
+                net.send(exp_ref.at[at, :], exp_ref.at[at, :], peer, slot)
+                net.send(proj_ref.at[at, :], proj_ref.at[at, :], peer, slot + 1)
+
     for k in range(1, 8):
-        net.arrived(vec_out.at[lax.rem(me + 8 - k, 8)], sibling, small + k - 1)
-    for out, _, _, across in (tokens, cotangents):
-        net.arrived(out.at[rows_at(sibling[1] * count, count)], sibling, across)
-    for take in waits:
-        take()
+        net.arrived(vecs.at[lax.rem(me + 8 - k, 8)], sibling, small + k - 1)
     for copy in copies:
         copy.wait()
+    for s in range(8):
+        values = vecs[s].astype(f32)
+        for j in range(3):
+            bias_all[3 * s + j] = values[6 + j : 7 + j, :]
+        ends_all[s] = values[9:10, :LANES]
+        norms_ref[:, s * rows : s * rows + rows] = values[:8, :]
+    for j in range(3):
+        pbias[:, j * head : j * head + head] = bias_all[8 * j + me]
+
+    at = rows_at(sibling[1] * rows, rows)
+    net.arrived(exp_ref.at[at, :], sibling, near)
+    for j in range(3):
+        net.arrived(proj_ref.at[at, pl.ds(j * head, head)], sibling, near + 1 + j)
+    for at, slot in gone:
+        net.arrived(exp_ref.at[at, :], sibling, slot)
+        net.arrived(proj_ref.at[at, :], sibling, slot + 1)
+    tokens.wait_own()
+    cotangents.wait_own()
+
+    @pl.loop(0, 4)
+    def _(slot):
+        second = jnp.where(z == 0, 2, jnp.where(z == 1, 0, 1))
+        last = jnp.where(z < 2, 3, 0)
+        after = jnp.where(z < 3, z + 1, 2)
+        chip = jnp.where(
+            slot == 0, z, jnp.where(slot == 1, after, jnp.where(slot == 2, second, last))
+        )
+
+        def loads(source, into, sems):
+            return [
+                pltpu.make_async_copy(
+                    source.at[rows_at((chip * 2 + b) * count, count)], into[b],
+                    load_sem.at[sems + b],
+                )
+                for b in range(2)
+            ]
+
+        def stores(source, into, sems):
+            return [
+                pltpu.make_async_copy(source.at[b], into.at[chip, b], store_sem.at[sems + b])
+                for b in range(2)
+            ]
+
+        def ends_of(b):
+            return ends_all[chip * 2 + b]
+
+        pl.when(slot > 0)(lambda: tokens.take(slot))
+        x_loads = loads(x_out, [xs.at[b] for b in range(2)], 0)
+        for load in x_loads:
+            load.start()
+        for load in x_loads:
+            load.wait()
+
+        @pl.loop(0, 2)
+        def _(b):
+            at = rows_at(b * count, count)
+            forward_block(
+                xs.at[b], ends_of(b), angles_ref, norms_ref, pbias, ebias_ref, proj_ref, exp_ref,
+                comb_ref, cont_ref, h1s.at[at], h2s.at[at], qkv.at[at], ca.at[at], slope.at[at],
+                parts.at[b],
+            )
+
+        for store in stores(parts, part_out, 0):
+            store.start()
+        pl.when(slot == 2)(lambda: tokens.step(3))
+        pl.when(slot > 0)(lambda: cotangents.take(slot))
+        up_loads = loads(up_out, [us.at[rows_at(b * count, count)] for b in range(2)], 2)
+        for load in up_loads:
+            load.start()
+        for load in up_loads:
+            load.wait()
+
+        @pl.loop(0, 2)
+        def _(b):
+            at = rows_at(b * count, count)
+            backward_block(
+                xs.at[b], us.at[at], ends_of(b), angles_ref, norms_ref, qkv.at[at], slope.at[at],
+                proj_ref, exp_ref, comb_ref, cont_ref, dh.at[at], dm.at[at], dns.at[b], sums,
+                hbias, mbias, obias,
+            )
+
+        for store in stores(dns, dn_out, 2):
+            store.start()
+        accumulate(low_sum, ca, us)
+        accumulate(he_sum, h2s, dh)
+        accumulate(hp_sum, h1s, dm)
+        for store in stores(parts, part_out, 0) + stores(dns, dn_out, 2):
+            store.wait()
+        pl.when(slot < 3)(lambda: cotangents.step(slot + 1))
+        pl.when(slot == 0)(lambda: tokens.step(2))
+
+    for total, out, stage in (
+        (low_sum, low_out, h1s), (he_sum, he_out, dh), (hp_sum, hp_out, dm)
+    ):
+        step = count
+
+        @pl.loop(0, total.shape[0] // step)
+        def _(i):
+            at = rows_at(lax.rem(i, 2) * step, step)
+            move = pltpu.make_async_copy(
+                stage.at[at], out.at[rows_at(i * step, step)], store_sem.at[lax.rem(i, 2)]
+            )
+            pl.when(i >= 2)(lambda: move.wait())
+            stage[at, :] = total[rows_at(i * step, step), :].astype(bf16)
+            move.start()
+
+        for i in range(2):
+            pltpu.make_async_copy(
+                stage.at[rows_at(i * step, step)], out.at[rows_at(i * step, step)], store_sem.at[i]
+            ).wait()
+    vec_out[...] = jnp.zeros_like(vec_out)
+    own_out[...] = jnp.zeros_like(own_out)
+    per = rows // LANES
+    for t in range(8):
+        for j in range(4):
+            for i in range(per):
+                at = t * rows + i * LANES
+                vec_out[t, j * per + i : j * per + i + 1, :] = sums[j : j + 1, at : at + LANES]
+        for i in range(mix // LANES):
+            at = 4 * per + i
+            vec_out[t, at : at + 1, :] = mbias[:, i * LANES : (i + 1) * LANES]
+    for i in range(units // LANES):
+        own_out[i : i + 1, :] = hbias[:, i * LANES : (i + 1) * LANES]
+    for i in range(per):
+        own_out[units // LANES + i : units // LANES + i + 1, :] = obias[
+            :, rows_at(me * rows + i * LANES, LANES)
+        ]
+    tokens.finish()
+    cotangents.finish()
     net.finish()
-    assert net.sends <= GATHER_SEMS and net.started <= GATHER_SEMS and net.locals <= 16
-
-
-GATHER_SEMS = 128
-
-
-def gather(tokens, vectors, upstream, expander, projector):
+    assert net.sends <= GATHER_SEMS and net.started <= GATHER_SEMS and net.locals <= 8
+
+
+def block_passes(tokens, vectors, upstream, expander, projector, combiner, contractor, ebias, angles):
     count, width = tokens.shape
     n = lax.axis_size("shard")
-    units, mix = expander.shape[1] // n, projector.shape[1] // n
+    units, mix, head = expander.shape[1] // n, projector.shape[1] // n, combiner.shape[0]
+    low = head + units
+    vmem, dma = pltpu.VMEM, pltpu.SemaphoreType.DMA
     shapes = [
-        (n * count, width), (n,) + vectors.shape, (n * count, width), (width, units), (width, mix)
+        (n * count, width), (n * count, width), (low, width), (width, units), (width, mix),
+        (n // 2, 2, count, width), (n // 2, 2, count, width),
     ]
+    two = 2 * count
     return pl.pallas_call(
-        gather_kernel,
-        out_shape=[jax.ShapeDtypeStruct(s, bf16) for s in shapes],
-        in_specs=[pl.BlockSpec(memory_space=pl.ANY)] * 5,
-        out_specs=[pl.BlockSpec(memory_space=pl.ANY)] * 5,
+        block_kernel,
+        out_shape=[jax.ShapeDtypeStruct(s, bf16) for s in shapes] + [
+            jax.ShapeDtypeStruct((n, 16, LANES), f32),
+            jax.ShapeDtypeStruct((16, LANES), f32),
+            jax.ShapeDtypeStruct((8, width), f32),
+        ],
+        in_specs=[pl.BlockSpec(memory_space=pl.ANY)] * 7 + [pl.BlockSpec(memory_space=vmem)] * 2,
+        out_specs=[pl.BlockSpec(memory_space=pl.ANY)] * 7 + [pl.BlockSpec(memory_space=vmem)] * 3,
         scratch_shapes=[
-            pltpu.SemaphoreType.DMA((GATHER_SEMS,)),
-            pltpu.SemaphoreType.DMA((GATHER_SEMS,)),
-            pltpu.SemaphoreType.DMA((16,)),
-        ],
+            vmem((width, units), bf16), vmem((width, mix), bf16), vmem((head, width), bf16),
+            vmem((units, width), bf16), vmem((low, width), f32), vmem((width, units), f32),
+            vmem((width, mix), f32),
+            vmem((2, count, width), bf16), vmem((two, width), bf16),
+            vmem((two, width), bf16), vmem((two, width), bf16), vmem((two, low), bf16),
+            vmem((two, units), bf16), vmem((two, mix), bf16), vmem((two, units), bf16),
+            vmem((two, mix), bf16), vmem((2, count, width), bf16), vmem((2, count, width), bf16),
+            vmem((n,) + vectors.shape, bf16), vmem((3 * n, 1, vectors.shape[1]), f32),
+            vmem((n, 1, LANES), f32),
+            vmem((1, mix), f32), vmem((4, width), f32), vmem((1, units), f32),
+            vmem((1, mix), f32), vmem((1, width), f32),
+            dma((GATHER_SEMS,)), dma((GATHER_SEMS,)), dma((8,)), dma((4,)), dma((4,)),
+        ] + [dma((8,))] * 8 + [dma((2,))],
         compiler_params=pltpu.CompilerParams(
             collective_id=0, has_side_effects=True, vmem_limit_bytes=VMEM_LIMIT
         ),
-    )(tokens, vectors, upstream, expander, projector)
+    )(tokens, vectors, upstream, expander, projector, combiner, contractor, ebias, angles)
 
 
 def add_into(target, other):
@@ -763,14 +933,22 @@
 
     class Sum:
         def __init__(self, ref, at, a, a1, a2, b, b1, b2):
+            self.ref, self.at = ref, at
             self.a, self.a1, self.a2, self.b, self.b1, self.b2 = a, a1, a2, b, b1, b2
+            self.slot = net.slots(6)
+
+        def load(self):
             self.loads = []
-            self.slot = net.slots(6)
             for i in range(2):
-                net.send(at(ref, i * 2 + 1 - x, 0), a1.at[i], by_x, self.slot + i)
-                net.send(at(ref, (1 - y) * 2 + i, 1), b1.at[i], by_y, self.slot + 2 + i)
-                self.loads.append(net.local(at(ref, i * 2 + x, 0), a.at[i]))
-                self.loads.append(net.local(at(ref, y * 2 + i, 1), b.at[i]))
+                self.loads.append(net.local(self.at(self.ref, i * 2 + x, 0), self.a.at[i]))
+                self.loads.append(net.local(self.at(self.ref, y * 2 + i, 1), self.b.at[i]))
+
+        def first(self):
+            for i in range(2):
+                source = self.at(self.ref, i * 2 + 1 - x, 0)
+                net.send(source, self.a1.at[i], by_x, self.slot + i)
+                source = self.at(self.ref, (1 - y) * 2 + i, 1)
+                net.send(source, self.b1.at[i], by_y, self.slot + 2 + i)
 
         def second(self):
             for load in self.loads:
@@ -801,6 +979,11 @@
         low_a, low_a1, low_a2, low_b, low_b1, low_b2,
     )
 
+    he.first()
+    hp.first()
+    he.load()
+    hp.load()
+
     class Line:
         def __init__(self, ref, inward, total, right, left):
             self.inward, self.total, self.right, self.left = inward, total, right, left
@@ -815,11 +998,13 @@
             slot = self.slot + 4 + (step - 1) + (0 if side > 0 else 3)
             net.send(self.total.at[block], into.at[step - 1], (rep, me + 2 * side), slot, when)
 
-        def begin(self):
+        def join(self):
             for i in range(4):
                 self.loads[i].wait()
                 net.arrived(self.inward.at[i], sibling, self.slot + i)
                 add_into(self.total.at[i], self.inward.at[i])
+
+        def begin(self):
             for step in (3, 2, 1):
                 self.push(step, step, 1, z == 0)
                 self.push(3 - step, step, -1, z == 3)
@@ -846,11 +1031,59 @@
         net.send(vec_ref.at[t], vec_in.at[me], (rep, t), small + k - 1)
     vec_load = net.local(vec_ref.at[me], vec_in.at[me])
     own_load = net.local(own_ref, vec_mix.at[pl.ds(56, 16)])
-
+    low.load()
+
+    out.join()
     out.begin()
+    he.second()
+    out.step_on(3)
+    back.join()
+    hp.second()
+    low.first()
+    out.step_on(2)
+
+    class Turn:
+        def __init__(self, source, half, place):
+            self.half, self.place = half, place
+            self.slot = net.slots(21)
+            self.copies = []
+            for k in range(1, 8):
+                t = lax.rem(me + k, 8)
+                for j, (src, dst) in enumerate(place(source, t, me)):
+                    net.send(src, dst, (rep, t), self.slot + (k - 1) * 3 + j)
+            for src, dst in place(source, me, me):
+                self.copies.append(net.local(src, dst))
+
+        def wait(self):
+            for k in range(1, 8):
+                s = lax.rem(me + 8 - k, 8)
+                for j, (_, dst) in enumerate(self.place(None, me, s)):
+                    net.arrived(dst, sibling, self.slot + (k - 1) * 3 + j)
+            for copy in self.copies:
+                copy.wait()
+
+    def place_exp(half):
+        return lambda source, t, s: [(
+            None if source is None else source.at[t],
+            exp_out.at[rep, half, :, rows_at(s * units, units)],
+        )]
+
+    def place_proj(half):
+        return lambda source, t, s: [
+            (
+                None if source is None else source.at[t, :, pl.ds(j * head, head)],
+                proj_out.at[rep, half, :, rows_at(j * width + s * head, head)],
+            )
+            for j in range(3)
+        ]
+
+    he_done = he.third()
+    he_turns = [Turn(he_done[h], h, place_exp(h)) for h in range(2)]
+    hp_done = hp.third()
+    hp_turns = [Turn(hp_done[h], h, place_proj(h)) for h in range(2)]
+    out.step_on(1)
     back.begin()
-    he.second()
-    hp.second()
+    low.second()
     for k in range(1, 8):
         net.arrived(vec_in.at[lax.rem(me + 8 - k, 8)], sibling, small + k - 1)
     vec_load.wait()
@@ -866,51 +1099,6 @@
     net.send(vec_mix, vec_all.at[rep], by_y, wide + 2)
     net.send(vec_mix, vec_all.at[rep], across, wide + 3)
     vec_copy = net.local(vec_mix, vec_all.at[rep])
-    out.step_on(3)
-    back.step_on(3)
-    low.second()
-
-    class Turn:
-        def __init__(self, source, half, place):
-            self.half, self.place = half, place
-            self.slot = net.slots(21)
-            self.copies = []
-            for k in range(1, 8):
-                t = lax.rem(me + k, 8)
-                for j, (src, dst) in enumerate(place(source, t, me)):
-                    net.send(src, dst, (rep, t), self.slot + (k - 1) * 3 + j)
-            for src, dst in place(source, me, me):
-                self.copies.append(net.local(src, dst))
-
-        def wait(self):
-            for k in range(1, 8):
-                s = lax.rem(me + 8 - k, 8)
-                for j, (_, dst) in enumerate(self.place(None, me, s)):
-                    net.arrived(dst, sibling, self.slot + (k - 1) * 3 + j)
-            for copy in self.copies:
-                copy.wait()
-
-    def place_exp(half):
-        return lambda source, t, s: [(
-            None if source is None else source.at[t],
-            exp_out.at[rep, half, :, rows_at(s * units, units)],
-        )]
-
-    def place_proj(half):
-        return lambda source, t, s: [
-            (
-                None if source is None else source.at[t, :, pl.ds(j * head, head)],
-                proj_out.at[rep, half, :, rows_at(j * width + s * head, head)],
-            )
-            for j in range(3)
-        ]
-
-    he_done = he.third()
-    he_turns = [Turn(he_done[h], h, place_exp(h)) for h in range(2)]
-    hp_done = hp.third()
-    hp_turns = [Turn(hp_done[h], h, place_proj(h)) for h in range(2)]
-    out.step_on(2)
-    back.step_on(2)
 
     class Spread:
         def __init__(self, target, sources):
@@ -932,23 +1120,24 @@
     low_done = low.third()
     low_copies = [net.local(low_done[h], low_out.at[rep, h]) for h in range(2)]
     low_spread = Spread(low_out, low_done)
-    out.step_on(1)
-    back.step_on(1)
     for turn in he_turns:
         turn.wait()
     he_spread = Spread(exp_out, [exp_out.at[rep, h] for h in range(2)])
     for turn in hp_turns:
         turn.wait()
     hp_spread = Spread(proj_out, [proj_out.at[rep, h] for h in range(2)])
+    back.step_on(3)
     low_spread.on()
-    osum_copy = net.local(o_sum.at[z], osum_out)
-    dsum_copy = net.local(d_sum.at[z], dsum_out)
+    back.step_on(2)
+    he_spread.on()
+    hp_spread.on()
     for k, r in ((1, x_rep), (2, y_rep), (3, d_rep)):
         net.arrived(vec_all.at[r], sibling, wide + k)
     vec_copy.wait()
     vec_out[...] = (vec_all[0] + vec_all[1]) + (vec_all[2] + vec_all[3])
-    he_spread.on()
-    hp_spread.on()
+    back.step_on(1)
+    osum_copy = net.local(o_sum.at[z], osum_out)
+    dsum_copy = net.local(d_sum.at[z], dsum_out)
     low_spread.wait()
     he_spread.wait()
     hp_spread.wait()
@@ -966,12 +1155,10 @@
     n = lax.axis_size("shard")
     low_rows, width = low.shape
     units, mix = he.shape[1], hp.shape[1]
-    rows, eighth, count = width // n, width // n // 8, part.shape[0] // n
+    rows, eighth, count = width // n, width // n // 8, part.shape[2]
     low = low.reshape(4, 2, low_rows // 8, width)
     he = he.reshape(n, 4, 2, eighth, units)
     hp = hp.reshape(n, 4, 2, eighth, mix)
-    part = part.reshape(4, 2, count, width)
-    dn = dn.reshape(4, 2, count, width)
     vmem = pltpu.VMEM
 
     def pieces(*shape):
@@ -1024,64 +1211,28 @@
     wide = projbias.shape[0]
 
     vectors = jnp.concatenate(
-        [projbias, combbias, contbias, attendgain, attendshift, feedgain, feedshift,
+        [attendgain, attendshift, feedgain, feedshift, combbias, contbias, projbias,
          document_ends[0].astype(bf16)]
     )
-    extra = 16
-    vectors = jnp.pad(vectors, (0, extra * width - vectors.shape[0])).reshape(extra, width)
+    vectors = jnp.pad(vectors, (0, 16 * rows - vectors.shape[0])).reshape(16, rows)
     _, _, live = layout(document_ends[0], count)
     upstream = jnp.where(live[:, None], cotangent, jnp.zeros_like(cotangent))
-    x_all, vectors, up_all, exp_cols, proj_cols = gather(
-        tokens, vectors, upstream, expander, projector
-    )
-
-    vectors = vectors.reshape(n, extra * width)
-    ends = vectors[:, wide + 6 * rows : wide + 6 * rows + DOCS].astype(jnp.int32)
-    full_projbias = vectors[:, :wide].reshape(3, n, head)
-    my_projbias = lax.dynamic_index_in_dim(full_projbias, me, 1, keepdims=False)
-    my_projbias = my_projbias.reshape(1, mix).astype(f32)
-    gains = vectors[:, wide : wide + 6 * rows].reshape(n, 6, rows).transpose(1, 0, 2)
-    gains = gains.reshape(6, width).astype(f32)
-    norms = gains[2:]
-
-    position = jax.vmap(lambda e: layout(e, count)[0])(ends).reshape(-1)
     half = ROT // 2
     freqs = jnp.exp(-jnp.arange(half, dtype=f32) * (2.0 / ROT) * math.log(10000.0))
-    angles = position[:, None] * freqs[None, :]
-    sine, cosine = jnp.sin(angles), jnp.cos(angles)
-    still = jnp.ones((n * count, LANES - ROT), f32)
-    cosine = jnp.concatenate([cosine, cosine, still], axis=1)
-    signed = jnp.concatenate([-sine, sine, 0.0 * still], axis=1)
-
-    h1, h2, qkv, ca, slope, part = forward_block(
-        count, ends, x_all, cosine, signed, norms, my_projbias, expbias.astype(f32)[None],
-        proj_cols, exp_cols, combiner, contractor,
-    )
-    low = left_trans(ca, up_all).astype(bf16)
-    out_bias = jnp.sum(up_all, axis=0, dtype=f32)
-    dh, dm, dn, sums, hidden_bias, mixed_bias = backward_block(
-        count, ends, x_all, up_all, cosine, signed, norms, qkv, slope,
-        proj_cols, exp_cols, combiner, contractor,
-    )
-    he = left_trans(h2, dh).astype(bf16)
-    hp = left_trans(h1, dm).astype(bf16)
-
-    vec = jnp.concatenate(
-        [
-            sums.reshape(4, n, rows).transpose(1, 0, 2).reshape(n, 4 * rows // LANES, LANES),
-            jnp.broadcast_to(mixed_bias.reshape(1, mix // LANES, LANES), (n, mix // LANES, LANES)),
-            jnp.zeros((n, 2, LANES), f32),
-        ],
-        axis=1,
-    )
-    own_out = lax.dynamic_slice(out_bias, (me * rows,), (rows,))
-    own = jnp.concatenate([hidden_bias[0], own_out])
-    own = jnp.pad(own, (0, 16 * LANES - own.shape[0])).reshape(16, LANES)
+    still = jnp.zeros((LANES - ROT,), f32)
+    ones = jnp.ones((half,), f32)
+    angles = jnp.stack(
+        [jnp.concatenate([freqs, freqs, still]), jnp.concatenate([-ones, ones, still])]
+    )
+    _, _, low, he, hp, part, dn, vec, own, norms = block_passes(
+        tokens, vectors, upstream, expander, projector, combiner, contractor,
+        expbias.astype(f32)[None], angles,
+    )
     low, exp_out, proj_out, osum, dsum, vec = settle(low, he, hp, part, dn, vec, own)
 
     floated = tokens.astype(f32)
     block_output = floated + jnp.where(
-        live[:, None], osum.astype(f32) + (gains[0] + gains[1]), 0.0
+        live[:, None], osum.astype(f32) + (norms[4] + norms[5]), 0.0
     )
     block_output = block_output.astype(bf16)
     d_normed = dsum.astype(f32)
@@ -1099,10 +1250,9 @@
     mixed_bias = lax.dynamic_slice(mixed_bias.reshape(-1), (me * wide,), (wide,))
     rest = vec[4 * rows + n * mix :]
     hidden_bias, out_bias = rest[:units], rest[units : units + rows]
-    low = low.astype(f32)
     return (
-        block_output, input_gradient, proj_out.astype(f32), mixed_bias, low[:head], out_bias,
-        exp_out.astype(f32), hidden_bias, low[head:], out_bias,
+        block_output, input_gradient, proj_out.astype(f32), mixed_bias, low[:head].astype(f32), out_bias,
+        exp_out.astype(f32), hidden_bias, low[head:].astype(f32), out_bias,
         norm_sums[0], norm_sums[1], norm_sums[2], norm_sums[3],
     )
 

time: 688 us -> 512 us (0.74)
  Pallas kernels: 584 us -> 473 us
  matrix products: 38.3 us -> 0 us
  local copies, waits for them, and re-layouts: 18.3 us -> 6.65 us
  other arithmetic: 38.3 us -> 26.8 us
    pallas_call x1, Pallas kernels: 295 us -> 214 us  [settle(): pl.pallas_call(settle_kernel, out_shape=[jax.ShapeDtypeStruct((4, 2, low_...]
    dot_general x3 -> x0, matrix products: 38.3 us -> none  [left_trans(): lax.dot_general(left, right, (((0,), (0,)), ((), ())), preferred_element_...]
    pallas_call x3 -> x1, Pallas kernels: 289 us -> 259 us  [block_passes(): pl.pallas_call(block_kernel, out_shape=[jax.ShapeDtypeStruct(s, bf16) for...]
    convert_element_type x4 -> x2, other arithmetic: 2.35 us -> 9.59 us  [the longest x1 6.8 us: sharded_heads(): low[head:].astype(f32)]
where the time goes in v4:
time: 512 us; the launch traced here: 507 us
  Pallas kernels  473 us (92%)
  other arithmetic  26.8 us (5%)
  local copies, waits for them, and re-layouts  6.65 us (1%)
    pallas_call x1, Pallas kernels, block_passes(): pl.pallas_call(block_kernel, out_shape=[jax.ShapeDtypeStruct(s, bf16) for...  259 us
    pallas_call x1, Pallas kernels, settle(): pl.pallas_call(settle_kernel, out_shape=[jax.ShapeDtypeStruct((4, 2, low_...  214 us

profile of v4, /device:TPU:10, one launch (start us, length us, event | category | flops | bytes accessed | tf_op | source)
XLA Modules:
  0.0 507.5 jit_solution(17789957043772766969)
XLA Ops:
  0.6 0.0 copy-start.16
  0.7 0.0 copy-start.17
  0.7 0.0 copy-start.10
  0.7 0.0 copy-start.11
  0.7 0.0 copy-start.12
  0.7 0.0 copy-start.13
  0.7 0.0 copy-start.14
  0.7 0.0 copy-start.15
  0.7 0.0 copy-start.9
  0.7 0.0 copy-start.8
  0.8 1.3 slice.58
  2.0 0.6 iota_compare_fusion
  2.7 2.3 broadcast_select_fusion.up_ref
  5.0 0.0 copy-done.10
  5.0 0.2 dynamic-update-slice
  5.2 0.0 copy-done.11
  5.2 0.2 dynamic-update-slice.1
  5.4 0.2 dynamic-update-slice.2
  5.6 0.0 copy-done.13
  5.7 0.2 dynamic-update-slice.3
  5.9 0.2 dynamic-update-slice.4
  6.1 0.2 dynamic-update-slice.5
  6.3 0.2 dynamic-update-slice.6
  6.5 0.2 dynamic-update-slice.7
  6.8 0.6 reshape.99.vec_ref
  7.4 0.6 broadcast_in_dim.42
  8.0 0.1 maximum_bitcast_fusion
  8.1 0.6 pad_maximum_fusion.angles_ref
  8.6 258.7 %shard_map.254 = (bf16[2048,2048]{1,0:T(8,128)(2,1)}, bf16[2048,2048]{1,0:T(8,128)(2,1)}, bf16[1280,2048]{1,0:T(8,128)(2,1)}, bf16[2048,1024]{1,0:T(8,128)(2,1)}...) custom-call(bf16[256,2048]{1,0:T(8,128)(2,1)} %tok_ref.1, ...), custom_call_target="tpu_custom_call" | custom-call | tf_op jit(solution)/shard_map/pallas_call | solution.py:873
  267.3 0.0 copy-start
  267.4 214.4 %shard_map.255 = (bf16[4,2,160,2048]{3,2,1,0:T(8,128)(2,1)}, bf16[4,2,32,8192]{3,2,1,0:T(8,128)(2,1)}, bf16[4,2,32,6144]{3,2,1,0:T(8,128)(2,1)}, bf16[256,2048]{...) custom-call(bf16[4,2,160,2048]{3,2,1,0:T(8,128)(2,1)} %bitcast.36, ...), custom_call_target="tpu_custom_call" | custom-call | tf_op jit(solution)/shard_map/pallas_call | solution.py:1170
  481.8 0.0 copy-start.3
  481.8 0.0 copy-done
  481.8 0.0 copy-start.2
  481.8 0.2 convert_reduce_fusion.1
  482.1 0.4 fusion.7
  482.5 0.5 copy-done.3
  483.0 0.7 convert_reduce_fusion
  483.7 0.9 slice_add_fusion
  484.7 2.4 fusion.6
  487.2 0.7 dynamic_slice.3
  487.8 0.6 slice_bitcast_fusion.1
  488.4 0.6 slice_bitcast_fusion
  489.0 6.8 %slice_convert_fusion = f32[1024,2048]{1,0:T(8,128)} fusion(bf16[1280,2048]{1,0:T(8,128)(2,1)} %bitcast.34), kind=kLoop, calls=%fused_computation | loop fusion | flops 2097152 | bytes 12582912 | tf_op jit(solution)/shard_map/convert_element_type | solution.py:1255
  495.8 2.8 slice_convert_fusion.1
  498.6 4.7 bitcast_convert_fusion
  503.3 3.7 bitcast_convert_fusion.1
  506.9 0.6 copy.42
  (30 shorter events, 0.1 us)
Async XLA Ops:
  0.6 7.4 %copy-start.16 = (f32[1,128]{1,0:T(1,128)S(1)}, f32[1,128]{1,0:T(1,128)}, u32[]{:S(2)}) copy-start(f32[1,128]{1,0:T(1,128)} %constant.7.clone.1) | copy-start | bytes 1540
  0.7 5.9 %copy-start.17 = (s32[1,4]{1,0:T(1,128)S(1)}, s32[1,4]{1,0:T(1,128)}, u32[]{:S(2)}) copy-start(s32[1,4]{1,0:T(1,128)} %param.16) | copy-start | bytes 52
  0.7 4.4 copy-start.10
  0.7 4.5 copy-start.11
  0.7 4.7 copy-start.12
  0.7 4.9 copy-start.13
  0.7 5.2 %copy-start.14 = (bf16[256]{0:T(256)(128)(2,1)S(1)}, bf16[256]{0:T(256)(128)(2,1)}, u32[]{:S(2)}) copy-start(bf16[256]{0:T(256)(128)(2,1)} %param.20) | copy-start | bytes 1540
  0.7 5.4 %copy-start.15 = (bf16[256]{0:T(256)(128)(2,1)S(1)}, bf16[256]{0:T(256)(128)(2,1)}, u32[]{:S(2)}) copy-start(bf16[256]{0:T(256)(128)(2,1)} %param.24) | copy-start | bytes 1540
  0.7 5.6 %copy-start.9 = (bf16[768]{0:T(1024)(128)(2,1)S(1)}, bf16[768]{0:T(1024)(128)(2,1)}, u32[]{:S(2)}) copy-start(bf16[768]{0:T(1024)(128)(2,1)} %param.18) | copy-start | bytes 4612
  0.7 6.6 %copy-start.8 = (bf16[1024]{0:T(1024)(128)(2,1)S(1)}, bf16[1024]{0:T(1024)(128)(2,1)}, u32[]{:S(2)}) copy-start(bf16[1024]{0:T(1024)(128)(2,1)} %param.22) | copy-start | bytes 6148
  267.3 214.5 %copy-start = (bf16[256,2048]{1,0:T(8,128)(2,1)S(1)}, bf16[256,2048]{1,0:T(8,128)(2,1)}, u32[]{:S(2)}) copy-start(bf16[256,2048]{1,0:T(8,128)(2,1)} %tok_ref.1) | copy-start | bytes 3145732
  481.8 1.2 copy-start.3
  481.8 2.9 copy-start.2
  481.8 2.8 copy-start.5
  484.7 2.4 copy-start.6
  488.4 18.5 %copy-start.7 = (f32[256]{0:T(256)}, f32[256]{0:T(256)S(1)}, u32[]{:S(2)}) copy-start(f32[256]{0:T(256)S(1)} %get-tuple-element.76) | copy-start | bytes 3076
  489.0 9.6 %copy-start.1 = (bf16[4,2,32,8192]{3,2,1,0:T(8,128)(2,1)S(1)}, bf16[4,2,32,8192]{3,2,1,0:T(8,128)(2,1)}, u32[]{:S(2)}) copy-start(bf16[4,2,32,8192]{3,2,1,0:T(8,128)(2,1)} %get-tuple-element.41) | copy-start | bytes 12582916
  498.6 4.7 copy-start.4

commit v5 on v4

--- a/solution.py
+++ b/solution.py
@@ -12,7 +12,7 @@
 ROT = 64
 DOCS = 4
 LANES = 128
-VMEM_LIMIT = 60 * 1024 * 1024
+VMEM_LIMIT = 62 * 1024 * 1024
 
 epsilon = 1e-05
 masked_value = -1e30
@@ -339,28 +339,49 @@
     return raised / jnp.sum(raised, axis=1, keepdims=True)
 
 
-def forward_block(
-    x_ref, ends, angles_ref, norms_ref, pbias_ref, ebias_ref, proj_ref, exp_ref, comb_ref,
-    cont_ref, h1_ref, h2_ref, qkv_ref, ca_ref, slope_ref, part_ref,
+def norm_parts(x_ref, at):
+    x = x_ref[at, :].astype(f32)
+    centre = jnp.mean(x, axis=1, keepdims=True)
+    centred = x - centre
+    inverse = lax.rsqrt(jnp.mean(centred * centred, axis=1, keepdims=True) + epsilon)
+    return centred, centre, inverse
+
+
+def tables(ends, count, angles_ref):
+    allowed, place = block_layout(ends, count)
+    angles = place * angles_ref[0:1, :]
+    return allowed, jnp.cos(angles), jnp.sin(angles) * angles_ref[1:2, :]
+
+
+def forward_pass(
+    x_ref, ends, count, angles_ref, norms_ref, pbias_ref, ebias_ref, proj_ref, exp_ref, comb_ref,
+    cont_ref, h1_ref, h2_ref, qkv_ref, ca_ref, slope_ref, stats_ref, part_ref,
 ):
-    count, width = x_ref.shape
+    slots, width = x_ref.shape
     head = comb_ref.shape[0]
     units = exp_ref.shape[1]
-    allowed, place = block_layout(ends, count)
-    angles = place * angles_ref[0:1, :]
-    cosine, signed = jnp.cos(angles), jnp.sin(angles) * angles_ref[1:2, :]
-    normed, _ = normalize(x_ref[...].astype(f32))
-    h1_ref[...] = (normed * norms_ref[0:1, :] + norms_ref[1:2, :]).astype(bf16)
-    h2_ref[...] = (normed * norms_ref[2:3, :] + norms_ref[3:4, :]).astype(bf16)
-    mixed = dot(h1_ref[...], proj_ref[...]) + pbias_ref[...]
-    q = rotated(mixed[:, :head], cosine, signed).astype(bf16)
-    k = rotated(mixed[:, head : 2 * head], cosine, signed).astype(bf16)
-    v = mixed[:, 2 * head :].astype(bf16)
-    qkv_ref[:, :head] = q
-    qkv_ref[:, head : 2 * head] = k
-    qkv_ref[:, 2 * head :] = v
-    probs = softmax(q, k, allowed).astype(bf16)
-    ca_ref[:, :head] = dot(probs, v).astype(bf16)
+    step = min(64, count)
+
+    @pl.loop(0, slots // step)
+    def _(i):
+        at = rows_at(i * step, step)
+        centred, centre, inverse = norm_parts(x_ref, at)
+        normed = centred * inverse
+        h1_ref[at, :] = (normed * norms_ref[0:1, :] + norms_ref[1:2, :]).astype(bf16)
+        h2_ref[at, :] = (normed * norms_ref[2:3, :] + norms_ref[3:4, :]).astype(bf16)
+        stats_ref[at, 0:1] = centre
+        stats_ref[at, 1:2] = inverse
+
+    for j in range(3):
+        cut = slice(j * head, j * head + head)
+        mixed = dot(h1_ref[...], proj_ref[:, cut]) + pbias_ref[:, cut]
+        for b in range(slots // count):
+            at = slice(b * count, b * count + count)
+            value = mixed[at]
+            if j < 2:
+                _, cosine, signed = tables(ends[b], count, angles_ref)
+                value = rotated(value, cosine, signed)
+            qkv_ref[at, cut] = value.astype(bf16)
     tile = min(256, units)
     for start in range(0, units, tile):
         hidden = dot(h2_ref[...], exp_ref[:, start : start + tile])
@@ -369,6 +390,11 @@
         ca_ref[:, head + start : head + start + tile] = (hidden * below).astype(bf16)
         density = jnp.exp(hidden * hidden * -0.5) * (1.0 / math.sqrt(2.0 * math.pi))
         slope_ref[:, start : start + tile] = (below + hidden * density).astype(bf16)
+    for b in range(slots // count):
+        at = slice(b * count, b * count + count)
+        allowed, _ = block_layout(ends[b], count)
+        probs = softmax(qkv_ref[at, :head], qkv_ref[at, head : 2 * head], allowed).astype(bf16)
+        ca_ref[at, :head] = dot(probs, qkv_ref[at, 2 * head :]).astype(bf16)
     tile = min(512, width)
     for start in range(0, width, tile):
         cut = slice(start, start + tile)
@@ -376,44 +402,45 @@
         part_ref[:, cut] = part.astype(bf16)
 
 
-def backward_block(
-    x_ref, up_ref, ends, angles_ref, norms_ref, qkv_ref, slope_ref, proj_ref, exp_ref, comb_ref,
-    cont_ref, dh_ref, dm_ref, dn_ref, sums_ref, hbias_ref, mbias_ref, obias_ref,
+def backward_pass(
+    x_ref, up_ref, ends, count, angles_ref, norms_ref, qkv_ref, slope_ref, stats_ref, proj_ref,
+    exp_ref, comb_ref, cont_ref, dh_ref, dm_ref, dn_ref, sums_ref, hbias_ref, mbias_ref, obias_ref,
 ):
-    count, width = x_ref.shape
+    slots, width = x_ref.shape
     head = comb_ref.shape[0]
     units = exp_ref.shape[1]
-    allowed, place = block_layout(ends, count)
-    angles = place * angles_ref[0:1, :]
-    cosine, signed = jnp.cos(angles), jnp.sin(angles) * angles_ref[1:2, :]
+    tile = min(256, units)
     d_context = right_trans(up_ref[...], comb_ref[...]).astype(bf16)
-    q, k, v = qkv_ref[:, :head], qkv_ref[:, head : 2 * head], qkv_ref[:, 2 * head :]
-    probs = softmax(q, k, allowed)
-    d_probs = right_trans(d_context, v)
-    d_v = left_trans(probs.astype(bf16), d_context)
-    d_s = probs * (d_probs - jnp.sum(d_probs * probs, axis=1, keepdims=True))
-    d_s = d_s.astype(bf16)
-    factor = 1.0 / math.sqrt(head)
-    dm_ref[:, :head] = unrotated(dot(d_s, k) * factor, cosine, signed).astype(bf16)
-    d_k = unrotated(left_trans(d_s, q) * factor, cosine, signed).astype(bf16)
-    dm_ref[:, head : 2 * head] = d_k
-    dm_ref[:, 2 * head :] = d_v.astype(bf16)
-    mbias_ref[...] += jnp.sum(dm_ref[...].astype(f32), axis=0, keepdims=True)
-    obias_ref[...] += jnp.sum(up_ref[...].astype(f32), axis=0, keepdims=True)
-    tile = min(256, units)
     for start in range(0, units, tile):
         cut = slice(start, start + tile)
         d_active = right_trans(up_ref[...], cont_ref[cut, :])
         d_hidden = (d_active * slope_ref[:, cut].astype(f32)).astype(bf16)
         dh_ref[:, cut] = d_hidden
         hbias_ref[:, cut] += jnp.sum(d_hidden.astype(f32), axis=0, keepdims=True)
-    x = x_ref[...].astype(f32)
-    centre = jnp.mean(x, axis=1, keepdims=True)
-    spread = jnp.mean((x - centre) * (x - centre), axis=1, keepdims=True)
-    inverse = lax.rsqrt(spread + epsilon)
+    factor = 1.0 / math.sqrt(head)
+    for b in range(slots // count):
+        at = slice(b * count, b * count + count)
+        allowed, cosine, signed = tables(ends[b], count, angles_ref)
+        q, k = qkv_ref[at, :head], qkv_ref[at, head : 2 * head]
+        v = qkv_ref[at, 2 * head :]
+        d_ctx = d_context[at]
+        probs = softmax(q, k, allowed)
+        d_probs = right_trans(d_ctx, v)
+        d_v = left_trans(probs.astype(bf16), d_ctx)
+        d_s = probs * (d_probs - jnp.sum(d_probs * probs, axis=1, keepdims=True))
+        d_s = d_s.astype(bf16)
+        dm_ref[at, :head] = unrotated(dot(d_s, k) * factor, cosine, signed).astype(bf16)
+        d_k = unrotated(left_trans(d_s, q) * factor, cosine, signed).astype(bf16)
+        dm_ref[at, head : 2 * head] = d_k
+        dm_ref[at, 2 * head :] = d_v.astype(bf16)
+    mbias_ref[...] += jnp.sum(dm_ref[...].astype(f32), axis=0, keepdims=True)
+    obias_ref[...] += jnp.sum(up_ref[...].astype(f32), axis=0, keepdims=True)
+    centre, inverse = stats_ref[:, 0:1], stats_ref[:, 1:2]
     tile = min(256, width)
-    for start in range(0, width, tile):
-        cut = slice(start, start + tile)
+
+    @pl.loop(0, width // tile, unroll=2)
+    def _(i):
+        cut = rows_at(i * tile, tile)
         normed = (x_ref[:, cut].astype(f32) - centre) * inverse
         d_first = right_trans(dm_ref[...], proj_ref[cut, :])
         d_second = right_trans(dh_ref[...], exp_ref[cut, :])
@@ -426,13 +453,15 @@
         sums_ref[3:4, cut] += jnp.sum(d_second, axis=0, keepdims=True)
 
 
-def accumulate(total, left, right):
-    tile = min(256, left.shape[1])
-
-    @pl.loop(0, left.shape[1] // tile)
+def accumulate(total, left, right, tall):
+    wide = min(256, right.shape[1])
+
+    @pl.loop(0, left.shape[1] // tall)
     def _(i):
-        at = pl.ds(pl.multiple_of(i * tile, tile), tile)
-        total[at, :] += left_trans(left[:, at], right[...])
+        at = pl.ds(pl.multiple_of(i * tall, LANES), tall)
+        for start in range(0, right.shape[1], wide):
+            cut = slice(start, start + wide)
+            total[at, cut] += left_trans(left[:, at], right[:, cut])
 
 
 MESH = pl.DeviceIdType.MESH
@@ -502,7 +531,7 @@
     def __init__(self, source, out, count, where, sems):
         self.source, self.out, self.count = source, out, count
         self.rep, self.me, self.z, self.c = where
-        self.side_send, self.side_recv, self.core_send, self.core_recv, self.local_sem = sems
+        self.side_send, self.side_recv, self.core_send, self.core_recv = sems
         self.sibling = self.me + 1 - 2 * self.c
 
     def block(self, shard):
@@ -562,10 +591,7 @@
         for side in (1, -1):
             pl.when(self.on(side))(lambda: self.first(side).start())
         self.first_cross().start()
-        pltpu.make_async_copy(self.source, self.block(self.me), self.local_sem).start()
-
     def wait_own(self):
-        pltpu.make_async_copy(self.source, self.block(self.me), self.local_sem).wait()
         self.taken(1, 0).wait_recv()
 
     def step(self, step):
@@ -605,10 +631,10 @@
     angles_ref,
     x_out, up_out, low_out, he_out, hp_out, part_out, dn_out, vec_out, own_out, norms_ref,
     exp_ref, proj_ref, comb_ref, cont_ref, low_sum, he_sum, hp_sum,
-    xs, us, h1s, h2s, ca, slope, qkv, dh, dm, parts, dns,
+    xs, us, h1s, h2s, ca, slope, qkv, dh, dm, parts, dns, stats,
     vecs, bias_all, ends_all, pbias, sums, hbias, mbias, obias,
     send_sem, recv_sem, local_sem, load_sem, store_sem,
-    xs_send, xs_recv, xc_send, xc_recv, us_send, us_recv, uc_send, uc_recv, own_sem,
+    xs_send, xs_recv, xc_send, xc_recv, us_send, us_recv, uc_send, uc_recv,
 ):
     rep, me, y, x, z, c = position_of()
     count, width = tok_ref.shape
@@ -649,10 +675,10 @@
         net.send(vec_ref, vecs.at[me], peer, small + k)
     where = (rep, me, z, c)
     tokens = Chain(
-        tok_ref, x_out, count, where, (xs_send, xs_recv, xc_send, xc_recv, own_sem.at[0])
+        tok_ref, x_out, count, where, (xs_send, xs_recv, xc_send, xc_recv)
     )
     cotangents = Chain(
-        up_ref, up_out, count, where, (us_send, us_recv, uc_send, uc_recv, own_sem.at[1])
+        up_ref, up_out, count, where, (us_send, us_recv, uc_send, uc_recv)
     )
     tokens.begin()
     near = net.slots(4)
@@ -744,78 +770,103 @@
         net.arrived(proj_ref.at[at, :], sibling, slot + 1)
     tokens.wait_own()
     cotangents.wait_own()
-
-    @pl.loop(0, 4)
-    def _(slot):
+    cotangents.step(1)
+
+    def chip_of(slot):
         second = jnp.where(z == 0, 2, jnp.where(z == 1, 0, 1))
         last = jnp.where(z < 2, 3, 0)
         after = jnp.where(z < 3, z + 1, 2)
-        chip = jnp.where(
+        return jnp.where(
             slot == 0, z, jnp.where(slot == 1, after, jnp.where(slot == 2, second, last))
         )
 
-        def loads(source, into, sems):
+    class Loads:
+        def __init__(self, own, source, into, first):
+            self.own, self.source, self.into, self.first = own, source, into, first
+
+        def start_own(self):
+            theirs = self.source.at[rows_at(sibling[1] * count, count)]
+            for source, b in ((self.own, c), (theirs, 1 - c)):
+                pltpu.make_async_copy(
+                    source, self.into.at[rows_at(b * count, count)], load_sem.at[self.first + b]
+                ).start()
+
+        def copies(self, slot):
             return [
                 pltpu.make_async_copy(
-                    source.at[rows_at((chip * 2 + b) * count, count)], into[b],
-                    load_sem.at[sems + b],
+                    self.source.at[rows_at((chip_of(slot) * 2 + b) * count, count)],
+                    self.into.at[rows_at(b * count, count)], load_sem.at[self.first + b],
                 )
                 for b in range(2)
             ]
 
-        def stores(source, into, sems):
+        def start(self, slot):
+            for copy in self.copies(slot):
+                copy.start()
+
+        def wait(self, slot):
+            for copy in self.copies(slot):
+                copy.wait()
+
+    x_loads, up_loads = Loads(tok_ref, x_out, xs, 0), Loads(up_ref, up_out, us, 2)
+    x_loads.start_own()
+    up_loads.start_own()
+
+    @pl.loop(0, 4)
+    def _(slot):
+        chip = chip_of(slot)
+        ends = [ends_all[chip * 2 + b] for b in range(2)]
+
+        def stores(source, into, first):
             return [
-                pltpu.make_async_copy(source.at[b], into.at[chip, b], store_sem.at[sems + b])
+                pltpu.make_async_copy(
+                    source.at[rows_at(b * count, count)], into.at[chip, b],
+                    store_sem.at[first + b],
+                )
                 for b in range(2)
             ]
 
-        def ends_of(b):
-            return ends_all[chip * 2 + b]
-
-        pl.when(slot > 0)(lambda: tokens.take(slot))
-        x_loads = loads(x_out, [xs.at[b] for b in range(2)], 0)
-        for load in x_loads:
-            load.start()
-        for load in x_loads:
-            load.wait()
-
-        @pl.loop(0, 2)
-        def _(b):
-            at = rows_at(b * count, count)
-            forward_block(
-                xs.at[b], ends_of(b), angles_ref, norms_ref, pbias, ebias_ref, proj_ref, exp_ref,
-                comb_ref, cont_ref, h1s.at[at], h2s.at[at], qkv.at[at], ca.at[at], slope.at[at],
-                parts.at[b],
-            )
-
+        x_loads.wait(slot)
+        forward_pass(
+            xs, ends, count, angles_ref, norms_ref, pbias, ebias_ref, proj_ref, exp_ref, comb_ref,
+            cont_ref, h1s, h2s, qkv, ca, slope, stats, parts,
+        )
         for store in stores(parts, part_out, 0):
             store.start()
         pl.when(slot == 2)(lambda: tokens.step(3))
-        pl.when(slot > 0)(lambda: cotangents.take(slot))
-        up_loads = loads(up_out, [us.at[rows_at(b * count, count)] for b in range(2)], 2)
-        for load in up_loads:
-            load.start()
-        for load in up_loads:
-            load.wait()
-
-        @pl.loop(0, 2)
-        def _(b):
-            at = rows_at(b * count, count)
-            backward_block(
-                xs.at[b], us.at[at], ends_of(b), angles_ref, norms_ref, qkv.at[at], slope.at[at],
-                proj_ref, exp_ref, comb_ref, cont_ref, dh.at[at], dm.at[at], dns.at[b], sums,
-                hbias, mbias, obias,
-            )
-
+
+        @pl.when(slot == 3)
+        def _():
+            cotangents.take(slot)
+            up_loads.start(slot)
+
+        up_loads.wait(slot)
+        backward_pass(
+            xs, us, ends, count, angles_ref, norms_ref, qkv, slope, stats, proj_ref, exp_ref,
+            comb_ref, cont_ref, dh, dm, dns, sums, hbias, mbias, obias,
+        )
         for store in stores(dns, dn_out, 2):
             store.start()
-        accumulate(low_sum, ca, us)
-        accumulate(he_sum, h2s, dh)
-        accumulate(hp_sum, h1s, dm)
+        pl.when(slot == 0)(lambda: tokens.step(2))
+        pl.when(slot == 1)(lambda: cotangents.step(2))
+
+        @pl.when(slot < 3)
+        def _():
+            tokens.take(slot + 1)
+            x_loads.start(slot + 1)
+
+        accumulate(low_sum, ca, us, ca.shape[1])
+
+        @pl.when(slot < 2)
+        def _():
+            cotangents.take(slot + 1)
+            up_loads.start(slot + 1)
+
+        accumulate(he_sum, h2s, dh, width // 2)
+        accumulate(hp_sum, h1s, dm, width // 2)
         for store in stores(parts, part_out, 0) + stores(dns, dn_out, 2):
             store.wait()
-        pl.when(slot < 3)(lambda: cotangents.step(slot + 1))
-        pl.when(slot == 0)(lambda: tokens.step(2))
+        pl.when(slot == 2)(lambda: cotangents.step(3))
 
     for total, out, stage in (
         (low_sum, low_out, h1s), (he_sum, he_out, dh), (hp_sum, hp_out, dm)
@@ -883,16 +934,17 @@
             vmem((width, units), bf16), vmem((width, mix), bf16), vmem((head, width), bf16),
             vmem((units, width), bf16), vmem((low, width), f32), vmem((width, units), f32),
             vmem((width, mix), f32),
-            vmem((2, count, width), bf16), vmem((two, width), bf16),
+            vmem((two, width), bf16), vmem((two, width), bf16),
             vmem((two, width), bf16), vmem((two, width), bf16), vmem((two, low), bf16),
             vmem((two, units), bf16), vmem((two, mix), bf16), vmem((two, units), bf16),
-            vmem((two, mix), bf16), vmem((2, count, width), bf16), vmem((2, count, width), bf16),
+            vmem((two, mix), bf16), vmem((two, width), bf16), vmem((two, width), bf16),
+            vmem((two, LANES), f32),
             vmem((n,) + vectors.shape, bf16), vmem((3 * n, 1, vectors.shape[1]), f32),
             vmem((n, 1, LANES), f32),
             vmem((1, mix), f32), vmem((4, width), f32), vmem((1, units), f32),
             vmem((1, mix), f32), vmem((1, width), f32),
             dma((GATHER_SEMS,)), dma((GATHER_SEMS,)), dma((8,)), dma((4,)), dma((4,)),
-        ] + [dma((8,))] * 8 + [dma((2,))],
+        ] + [dma((8,))] * 8,
         compiler_params=pltpu.CompilerParams(
             collective_id=0, has_side_effects=True, vmem_limit_bytes=VMEM_LIMIT
         ),

time: 512 us -> 488 us (0.953)
  Pallas kernels: 473 us -> 449 us
    pallas_call x1, Pallas kernels: 259 us -> 235 us  [block_passes(): pl.pallas_call(block_kernel, out_shape=[jax.ShapeDtypeStruct(s, bf16) for...]
where the time goes in v5:
time: 488 us; the launch traced here: 484 us
  Pallas kernels  449 us (92%)
  other arithmetic  26.8 us (5%)
  local copies, waits for them, and re-layouts  6.65 us (1%)
    pallas_call x1, Pallas kernels, block_passes(): pl.pallas_call(block_kernel, out_shape=[jax.ShapeDtypeStruct(s, bf16) for...  235 us
    pallas_call x1, Pallas kernels, settle(): pl.pallas_call(settle_kernel, out_shape=[jax.ShapeDtypeStruct((4, 2, low_...  214 us

profile of v5, /device:TPU:10, one launch (start us, length us, event | category | flops | bytes accessed | tf_op | source)
XLA Modules:
  0.0 483.8 jit_solution(18164983899010444147)
XLA Ops:
  0.6 0.0 copy-start.16
  0.7 0.0 copy-start.17
  0.7 0.0 copy-start.10
  0.7 0.0 copy-start.11
  0.7 0.0 copy-start.12
  0.7 0.0 copy-start.13
  0.7 0.0 copy-start.14
  0.7 0.0 copy-start.15
  0.7 0.0 copy-start.9
  0.7 0.0 copy-start.8
  0.8 1.3 slice.58
  2.0 0.6 iota_compare_fusion
  2.7 2.3 broadcast_select_fusion.up_ref
  5.0 0.0 copy-done.10
  5.0 0.2 dynamic-update-slice
  5.2 0.0 copy-done.11
  5.2 0.2 dynamic-update-slice.1
  5.4 0.0 copy-done.12
  5.4 0.2 dynamic-update-slice.2
  5.6 0.0 copy-done.13
  5.7 0.2 dynamic-update-slice.3
  5.9 0.0 copy-done.14
  5.9 0.2 dynamic-update-slice.4
  6.1 0.2 dynamic-update-slice.5
  6.3 0.2 dynamic-update-slice.6
  6.5 0.2 dynamic-update-slice.7
  6.8 0.6 reshape.99.vec_ref
  7.4 0.6 broadcast_in_dim.42
  8.0 0.1 maximum_bitcast_fusion
  8.1 0.6 pad_maximum_fusion.angles_ref
  8.6 235.0 %shard_map.254 = (bf16[2048,2048]{1,0:T(8,128)(2,1)}, bf16[2048,2048]{1,0:T(8,128)(2,1)}, bf16[1280,2048]{1,0:T(8,128)(2,1)}, bf16[2048,1024]{1,0:T(8,128)(2,1)}...) custom-call(bf16[256,2048]{1,0:T(8,128)(2,1)} %tok_ref.1, ...), custom_call_target="tpu_custom_call" | custom-call | tf_op jit(solution)/shard_map/pallas_call | solution.py:924
  243.6 0.0 copy-start
  243.6 214.4 %shard_map.255 = (bf16[4,2,160,2048]{3,2,1,0:T(8,128)(2,1)}, bf16[4,2,32,8192]{3,2,1,0:T(8,128)(2,1)}, bf16[4,2,32,6144]{3,2,1,0:T(8,128)(2,1)}, bf16[256,2048]{...) custom-call(bf16[4,2,160,2048]{3,2,1,0:T(8,128)(2,1)} %bitcast.36, ...), custom_call_target="tpu_custom_call" | custom-call | tf_op jit(solution)/shard_map/pallas_call | solution.py:1222
  458.1 0.0 copy-start.2
  458.1 0.2 convert_reduce_fusion.1
  458.4 0.4 fusion.7
  458.8 0.5 copy-done.3
  459.3 0.7 convert_reduce_fusion
  460.0 0.9 slice_add_fusion
  461.0 2.4 fusion.6
  463.5 0.7 dynamic_slice.3
  464.1 0.6 slice_bitcast_fusion.1
  464.7 0.6 slice_bitcast_fusion
  465.3 6.8 %slice_convert_fusion = f32[1024,2048]{1,0:T(8,128)} fusion(bf16[1280,2048]{1,0:T(8,128)(2,1)} %bitcast.34), kind=kLoop, calls=%fused_computation | loop fusion | flops 2097152 | bytes 12582912 | tf_op jit(solution)/shard_map/convert_element_type | solution.py:1307
  472.1 2.8 slice_convert_fusion.1
  474.9 4.7 bitcast_convert_fusion
  479.6 3.7 bitcast_convert_fusion.1
  483.2 0.6 copy.42
  (30 shorter events, 0.1 us)
Async XLA Ops:
  0.6 7.4 %copy-start.16 = (f32[1,128]{1,0:T(1,128)S(1)}, f32[1,128]{1,0:T(1,128)}, u32[]{:S(2)}) copy-start(f32[1,128]{1,0:T(1,128)} %constant.7.clone.1) | copy-start | bytes 1540
  0.7 5.9 %copy-start.17 = (s32[1,4]{1,0:T(1,128)S(1)}, s32[1,4]{1,0:T(1,128)}, u32[]{:S(2)}) copy-start(s32[1,4]{1,0:T(1,128)} %param.16) | copy-start | bytes 52
  0.7 4.4 copy-start.10
  0.7 4.5 copy-start.11
  0.7 4.7 copy-start.12
  0.7 4.9 %copy-start.13 = (bf16[256]{0:T(256)(128)(2,1)S(1)}, bf16[256]{0:T(256)(128)(2,1)}, u32[]{:S(2)}) copy-start(bf16[256]{0:T(256)(128)(2,1)} %param.28) | copy-start | bytes 1540
  0.7 5.2 %copy-start.14 = (bf16[256]{0:T(256)(128)(2,1)S(1)}, bf16[256]{0:T(256)(128)(2,1)}, u32[]{:S(2)}) copy-start(bf16[256]{0:T(256)(128)(2,1)} %param.20) | copy-start | bytes 1540
  0.7 5.4 %copy-start.15 = (bf16[256]{0:T(256)(128)(2,1)S(1)}, bf16[256]{0:T(256)(128)(2,1)}, u32[]{:S(2)}) copy-start(bf16[256]{0:T(256)(128)(2,1)} %param.24) | copy-start | bytes 1540
  0.7 5.6 %copy-start.9 = (bf16[768]{0:T(1024)(128)(2,1)S(1)}, bf16[768]{0:T(1024)(128)(2,1)}, u32[]{:S(2)}) copy-start(bf16[768]{0:T(1024)(128)(2,1)} %param.18) | copy-start | bytes 4612
  0.7 6.6 %copy-start.8 = (bf16[1024]{0:T(1024)(128)(2,1)S(1)}, bf16[1024]{0:T(1024)(128)(2,1)}, u32[]{:S(2)}) copy-start(bf16[1024]{0:T(1024)(128)(2,1)} %param.22) | copy-start | bytes 6148
  243.6 214.5 %copy-start = (bf16[256,2048]{1,0:T(8,128)(2,1)S(1)}, bf16[256,2048]{1,0:T(8,128)(2,1)}, u32[]{:S(2)}) copy-start(bf16[256,2048]{1,0:T(8,128)(2,1)} %tok_ref.1) | copy-start | bytes 3145732
  458.1 1.2 copy-start.3
  458.1 2.9 copy-start.2
  458.1 2.8 copy-start.5
  461.0 2.4 copy-start.6
  464.7 18.5 %copy-start.7 = (f32[256]{0:T(256)}, f32[256]{0:T(256)S(1)}, u32[]{:S(2)}) copy-start(f32[256]{0:T(256)S(1)} %get-tuple-element.76) | copy-start | bytes 3076
  465.3 9.6 %copy-start.1 = (bf16[4,2,32,8192]{3,2,1,0:T(8,128)(2,1)S(1)}, bf16[4,2,32,8192]{3,2,1,0:T(8,128)(2,1)}, u32[]{:S(2)}) copy-start(bf16[4,2,32,8192]{3,2,1,0:T(8,128)(2,1)} %get-tuple-element.41) | copy-start | bytes 12582916
  474.9 4.7 copy-start.4

commit v6 on v5

--- a/solution.py
+++ b/solution.py
@@ -465,7 +465,6 @@
 
 
 MESH = pl.DeviceIdType.MESH
-GATHER_SEMS = 96
 
 
 def position_of():
@@ -494,17 +493,21 @@
         self.started += count
         return first
 
-    def send(self, src, dst, peer, slot, when=None):
+    def send(self, ends, slot, when=None):
         index = self.sends
         self.sends += 1
-        copy = pltpu.make_async_remote_copy(
-            src_ref=src, dst_ref=dst, send_sem=self.send_sem.at[index],
-            recv_sem=self.recv_sem.at[slot], device_id=peer, device_id_type=MESH,
-        )
+
+        def copy():
+            src, dst, peer = ends()
+            return pltpu.make_async_remote_copy(
+                src_ref=src, dst_ref=dst, send_sem=self.send_sem.at[index],
+                recv_sem=self.recv_sem.at[slot], device_id=peer, device_id_type=MESH,
+            )
+
         if when is None:
-            copy.start()
+            copy().start()
         else:
-            pl.when(when)(lambda: copy.start())
+            pl.when(when)(lambda: copy().start())
         self.sent.append((copy, when))
 
     def arrived(self, dst, peer, slot):
@@ -519,12 +522,12 @@
         copy.start()
         return copy
 
-    def finish(self):
-        for copy, when in self.sent:
+    def left(self, sent):
+        for copy, when in sent:
             if when is None:
-                copy.wait_send()
+                copy().wait_send()
             else:
-                pl.when(when)(lambda copy=copy: copy.wait_send())
+                pl.when(when)(lambda copy=copy: copy().wait_send())
 
 
 class Chain:
@@ -626,14 +629,29 @@
                     pl.when(here & self.on(side))(lambda: self.side(side, step).wait_send())
 
 
+def add_into(target, other):
+    rows = target.shape[-2]
+    step = min(32, rows)
+
+    @pl.loop(0, rows // step)
+    def _(i):
+        at = (Ellipsis, pl.ds(pl.multiple_of(i * step, step), step), slice(None))
+        lead = (slice(None),) * (len(target.shape) - 2)
+        at = lead + at[1:]
+        target[at] = (target[at].astype(f32) + other[at].astype(f32)).astype(target.dtype)
+
+
 def block_kernel(
     tok_ref, vec_ref, up_ref, expander_ref, projector_ref, comb_hbm, cont_hbm, ebias_ref,
     angles_ref,
-    x_out, up_out, low_out, he_out, hp_out, part_out, dn_out, vec_out, own_out, norms_ref,
+    low_out, exp_out, proj_out, osum_out, dsum_out, vec_out, norms_ref,
+    x_out, up_out, part_own, dn_own, o_in, d_in, o_land, d_land, low_land, he_land, hp_land,
+    h_save, qkv_save, slope_save, stats_save,
     exp_ref, proj_ref, comb_ref, cont_ref, low_sum, he_sum, hp_sum,
-    xs, us, h1s, h2s, ca, slope, qkv, dh, dm, parts, dns, stats,
+    xs, us, hs, pd, ca, slope, qkv, dh, dm, spare, stats,
     vecs, bias_all, ends_all, pbias, sums, hbias, mbias, obias,
-    send_sem, recv_sem, local_sem, load_sem, store_sem,
+    vec_msg, vec_in, vec_mix, vec_all,
+    send_sem, recv_sem, local_sem, load_sem, store_sem, cross_send, cross_recv,
     xs_send, xs_recv, xc_send, xc_recv, us_send, us_recv, uc_send, uc_recv,
 ):
     rep, me, y, x, z, c = position_of()
@@ -642,9 +660,13 @@
     units, mix = exp_ref.shape[1], proj_ref.shape[1]
     head = mix // 3
     sibling = (rep, me + 1 - 2 * c)
-    by_x, by_y = (rep + 1 - 2 * x, me), (rep + 2 - 4 * y, me)
+    x_rep, y_rep, d_rep = rep + 1 - 2 * x, rep + 2 - 4 * y, 3 - rep
+    by_x, by_y, across = (x_rep, me), (y_rep, me), (d_rep, me)
     ring = [(rep, lax.rem(me + k, 8)) for k in range(1, 8)]
-    meet(ring + [by_x, by_y])
+    meet(ring + [by_x, by_y, across])
+    slots = hs.shape[0] // 2
+    h1s, h2s = hs.at[pl.ds(0, slots)], hs.at[pl.ds(slots, slots)]
+    parts, dns = pd.at[pl.ds(0, slots)], pd.at[pl.ds(slots, slots)]
     net = Net(send_sem, recv_sem, local_sem)
 
     def weight_copies(go, first, size, source_rows, t):
@@ -657,22 +679,27 @@
                 proj_ref.at[target, pl.ds(j * head, head)],
             )
 
-    remote = net.slots(24)
-    for step in (1, 2, 3):
-        tz = lax.rem(z + step, 4)
+    remote = net.slots(32)
+    chips = []
+    for i in range(3):
+        down, up = 3 - i, i
+        chips.append(jnp.where(
+            z < 2, jnp.where(down <= z, down - 1, down), jnp.where(up >= z, up + 1, up)
+        ))
+    for chip in chips:
         for core in (0, 1):
             part = [0]
 
             def go(src, dst):
                 net.send(
-                    src, dst, (rep, tz * 2 + core), remote + ((step - 1) * 2 + c) * 4 + part[0]
+                    lambda: (src, dst, (rep, chip * 2 + core)), remote + me * 4 + part[0]
                 )
                 part[0] += 1
 
-            weight_copies(go, me * rows + rep * quarter, quarter, rep * quarter, tz * 2 + core)
+            weight_copies(go, me * rows + rep * quarter, quarter, rep * quarter, chip * 2 + core)
     small = net.slots(7)
     for k, peer in enumerate(ring):
-        net.send(vec_ref, vecs.at[me], peer, small + k)
+        net.send(lambda peer=peer: (vec_ref, vecs.at[me], peer), small + k)
     where = (rep, me, z, c)
     tokens = Chain(
         tok_ref, x_out, count, where, (xs_send, xs_recv, xc_send, xc_recv)
@@ -685,7 +712,7 @@
     part = [0]
 
     def go_near(src, dst):
-        net.send(src, dst, sibling, near + part[0])
+        net.send(lambda: (src, dst, sibling), near + part[0])
         part[0] += 1
 
     weight_copies(go_near, me * rows, rows, 0, sibling[1])
@@ -705,48 +732,50 @@
                 ref[rows_at(i * 64, 64), :] = jnp.zeros((64, ref.shape[1]), f32)
 
     def shard_rows(step, core):
-        return (lax.rem(z + 4 - step, 4) * 2 + core) * rows
-
-    first_hop = net.slots(12)
-    for step in (1, 2, 3):
+        return (chips[step - 1] * 2 + core) * rows
+
+    first_hop, second_hop = net.slots(12), net.slots(18)
+    gone = []
+
+    def pass_on(ref_at, peer, slot):
+        for ref, more in ((exp_ref, 0), (proj_ref, 1)):
+            net.send(lambda ref=ref: (ref.at[ref_at, :], ref.at[ref_at, :], peer), slot + more)
+
+    def landed(step):
         for core in (0, 1):
-            base = shard_rows(step, core)
-            at = rows_at(base + rep * quarter, quarter)
-            slot = remote + ((step - 1) * 2 + core) * 4
+            at = rows_at(shard_rows(step, core) + rep * quarter, quarter)
+            slot = remote + (chips[step - 1] * 2 + core) * 4
             net.arrived(exp_ref.at[at, :], sibling, slot)
             for j in range(3):
                 net.arrived(proj_ref.at[at, pl.ds(j * head, head)], sibling, slot + 1 + j)
             peer = by_x if core == 0 else by_y
-            hop = first_hop + ((step - 1) * 2 + core) * 2
-            net.send(exp_ref.at[at, :], exp_ref.at[at, :], peer, hop)
-            net.send(proj_ref.at[at, :], proj_ref.at[at, :], peer, hop + 1)
-    tokens.step(1)
-    second_hop = net.slots(18)
-    gone = []
-    for step in (1, 2, 3):
+            pass_on(at, peer, first_hop + ((step - 1) * 2 + core) * 2)
+
+    def crossed(step):
         for core in (0, 1):
             base = shard_rows(step, core)
             hop = first_hop + ((step - 1) * 2 + core) * 2
-            if core == 0:
-                other = rows_at(base + (rep + 1 - 2 * x) * quarter, quarter)
-            else:
-                other = rows_at(base + (rep + 2 - 4 * y) * quarter, quarter)
+            other = rows_at(base + (x_rep if core == 0 else y_rep) * quarter, quarter)
             net.arrived(exp_ref.at[other, :], sibling, hop)
             net.arrived(proj_ref.at[other, :], sibling, hop + 1)
             hop = second_hop + (step - 1) * 6
             if core == 0:
-                pieces = [(rows_at(base + y * 2 * quarter, 2 * quarter), by_y, hop)]
-                gone += [(rows_at(base + (1 - y) * 2 * quarter, 2 * quarter), hop)]
+                pass_on(rows_at(base + y * 2 * quarter, 2 * quarter), by_y, hop)
+                gone.append((rows_at(base + (1 - y) * 2 * quarter, 2 * quarter), hop))
             else:
-                here = rows_at(base + rep * quarter, quarter)
-                pieces = [(here, by_x, hop + 2), (other, by_x, hop + 4)]
-                gone += [
-                    (rows_at(base + (rep + 1 - 2 * x) * quarter, quarter), hop + 2),
-                    (rows_at(base + (3 - rep) * quarter, quarter), hop + 4),
-                ]
-            for at, peer, slot in pieces:
-                net.send(exp_ref.at[at, :], exp_ref.at[at, :], peer, slot)
-                net.send(proj_ref.at[at, :], proj_ref.at[at, :], peer, slot + 1)
+                pass_on(rows_at(base + rep * quarter, quarter), by_x, hop + 2)
+                pass_on(other, by_x, hop + 4)
+                gone.append((rows_at(base + x_rep * quarter, quarter), hop + 2))
+                gone.append((rows_at(base + d_rep * quarter, quarter), hop + 4))
+
+    landed(1)
+    landed(2)
+    crossed(1)
+    landed(3)
+    crossed(2)
+    crossed(3)
+    tokens.step(1)
+    opening, net.sent = net.sent, []
 
     for k in range(1, 8):
         net.arrived(vecs.at[lax.rem(me + 8 - k, 8)], sibling, small + k - 1)
@@ -812,287 +841,296 @@
     x_loads.start_own()
     up_loads.start_own()
 
-    @pl.loop(0, 4)
-    def _(slot):
-        chip = chip_of(slot)
-        ends = [ends_all[chip * 2 + b] for b in range(2)]
-
-        def stores(source, into, first):
-            return [
-                pltpu.make_async_copy(
-                    source.at[rows_at(b * count, count)], into.at[chip, b],
-                    store_sem.at[first + b],
+    def stores(source, own, theirs, first, chip):
+        mine = pltpu.make_async_copy(
+            source.at[rows_at(c * count, count)], own.at[chip], store_sem.at[first]
+        )
+        other = pltpu.make_async_remote_copy(
+            src_ref=source.at[rows_at((1 - c) * count, count)], dst_ref=theirs.at[chip],
+            send_sem=cross_send.at[first], recv_sem=cross_recv.at[first * 4 + chip],
+            device_id=sibling, device_id_type=MESH,
+        )
+        return mine, other
+
+    def store(source, own, theirs, first, chip):
+        mine, other = stores(source, own, theirs, first, chip)
+        mine.start()
+        other.start()
+
+    def stored(source, own, theirs, first, chip):
+        mine, other = stores(source, own, theirs, first, chip)
+        mine.wait()
+        other.wait_send()
+
+    def saves():
+        pairs = [(hs, h_save), (qkv, qkv_save), (slope, slope_save), (stats, stats_save)]
+        return [(pair, store_sem.at[2 + i]) for i, pair in enumerate(pairs)]
+
+    class Piece:
+        def __init__(self, total, land, start, step, stage, tmp):
+            self.total, self.land, self.start, self.step = total, land, start, step
+            self.stage, self.tmp = stage, tmp
+            self.size = land.shape[1]
+            self.slot = net.slots(6)
+
+        def each(self, quarter, half, work):
+            @pl.loop(0, self.size // self.step)
+            def _(i):
+                work(
+                    rows_at(self.start(quarter, half, i), self.step),
+                    rows_at(i * self.step, self.step),
                 )
-                for b in range(2)
-            ]
-
-        x_loads.wait(slot)
-        forward_pass(
-            xs, ends, count, angles_ref, norms_ref, pbias, ebias_ref, proj_ref, exp_ref, comb_ref,
-            cont_ref, h1s, h2s, qkv, ca, slope, stats, parts,
-        )
-        for store in stores(parts, part_out, 0):
-            store.start()
-        pl.when(slot == 2)(lambda: tokens.step(3))
-
-        @pl.when(slot == 3)
+
+        def lower(self, quarter, half, target):
+            def work(at, to):
+                target[to, :] = self.total[at, :].astype(bf16)
+
+            self.each(quarter, half, work)
+
+        def add(self, quarter, half, source):
+            def work(at, to):
+                self.total[at, :] += source[to, :].astype(f32)
+
+            self.each(quarter, half, work)
+
+        def room(self, first):
+            return self.tmp.at[pl.ds(first, self.size)]
+
+        def first(self):
+            before = len(net.sent)
+            for i in range(2):
+                for half, quarter, peer in (
+                    (0, i * 2 + 1 - x, by_x), (1, (1 - y) * 2 + i, by_y)
+                ):
+                    place = half * 2 + i
+                    self.lower(quarter, half, self.stage[place])
+                    net.send(
+                        lambda place=place, peer=peer: (
+                            self.stage[place], self.land.at[place], peer
+                        ),
+                        self.slot + place,
+                    )
+            self.sent, net.sent = net.sent[before:], net.sent[:before]
+
+        def fetch(self, place):
+            net.arrived(self.land.at[place], sibling, self.slot + place)
+            return net.local(self.land.at[place], self.room(place * self.size))
+
+        def second(self):
+            loads = [self.fetch(place) for place in range(4)]
+            for half, other, peer in ((0, 1 - y, by_y), (1, 1 - x, by_x)):
+                for i in range(2):
+                    loads[half * 2 + i].wait()
+                    quarter = i * 2 + x if half == 0 else y * 2 + i
+                    self.add(quarter, half, self.room((half * 2 + i) * self.size))
+                quarter = other * 2 + x if half == 0 else y * 2 + other
+                stage = self.later(half)
+                self.lower(quarter, half, stage)
+                net.send(
+                    lambda stage=stage, half=half, peer=peer: (
+                        stage, self.land.at[4 + half], peer
+                    ),
+                    self.slot + 4 + half,
+                )
+
+        def later(self, half):
+            first = 6 + half if self.tmp.shape[0] >= 8 * self.size else half
+            return self.room(first * self.size)
+
+        def third(self):
+            loads = [self.fetch(4 + half) for half in range(2)]
+            for half in range(2):
+                loads[half].wait()
+                self.add(rep, half, self.room((4 + half) * self.size))
+                self.lower(rep, half, self.room((2 + half) * self.size))
+            return [self.room((2 + half) * self.size) for half in range(2)]
+
+    def low_start(quarter, half, i):
+        return quarter * (low_sum.shape[0] // 4) + half * (low_sum.shape[0] // 8) + i * 32
+
+    def high_start(quarter, half, i):
+        return i * rows + quarter * (rows // 4) + half * (rows // 8)
+
+    low_size, high_size = low_land.shape[1], he_land.shape[1]
+
+    def halves(ref):
+        return [ref.at[pl.ds(i * high_size, high_size)] for i in range(2)]
+
+    low_stage = [parts.at[pl.ds(i * low_size, low_size)] for i in range(3)] + [spare]
+    low = Piece(low_sum, low_land, low_start, 32, low_stage, cont_ref)
+    he = Piece(he_sum, he_land, high_start, rows // 8, halves(dh) + halves(slope), exp_ref)
+    hp = Piece(hp_sum, hp_land, high_start, rows // 8, halves(dm) + halves(qkv), proj_ref)
+
+    @pl.loop(0, 5)
+    def _(turn_index):
+        slot = jnp.minimum(turn_index, 3)
+
+        @pl.when(turn_index < 4)
         def _():
-            cotangents.take(slot)
-            up_loads.start(slot)
-
-        up_loads.wait(slot)
-        backward_pass(
-            xs, us, ends, count, angles_ref, norms_ref, qkv, slope, stats, proj_ref, exp_ref,
-            comb_ref, cont_ref, dh, dm, dns, sums, hbias, mbias, obias,
-        )
-        for store in stores(dns, dn_out, 2):
-            store.start()
-        pl.when(slot == 0)(lambda: tokens.step(2))
-        pl.when(slot == 1)(lambda: cotangents.step(2))
-
-        @pl.when(slot < 3)
+            chip = chip_of(slot)
+            ends = [ends_all[chip * 2 + b] for b in range(2)]
+            x_loads.wait(slot)
+            forward_pass(
+                xs, ends, count, angles_ref, norms_ref, pbias, ebias_ref, proj_ref, exp_ref,
+                comb_ref, cont_ref, h1s, h2s, qkv, ca, slope, stats, parts,
+            )
+            store(parts, part_own, o_in, 0, chip)
+            pl.when(slot == 2)(lambda: tokens.step(3))
+
+            @pl.when(slot == 3)
+            def _():
+                cotangents.step(3)
+                cotangents.take(3)
+                up_loads.start(3)
+
+            up_loads.wait(slot)
+            accumulate(low_sum, ca, us, ca.shape[1])
+            stored(parts, part_own, o_in, 0, chip)
+
+        @pl.when(turn_index == 2)
         def _():
-            tokens.take(slot + 1)
-            x_loads.start(slot + 1)
-
-        accumulate(low_sum, ca, us, ca.shape[1])
-
-        @pl.when(slot < 2)
+            for (here, there), sem in saves():
+                pltpu.make_async_copy(here, there, sem).start()
+            tokens.take(3)
+            x_loads.start(3)
+            for (here, there), sem in saves():
+                pltpu.make_async_copy(here, there, sem).wait()
+
+        pl.when(turn_index == 3)(lambda: low.first())
+
+        @pl.when(turn_index == 4)
         def _():
-            cotangents.take(slot + 1)
-            up_loads.start(slot + 1)
-
-        accumulate(he_sum, h2s, dh, width // 2)
-        accumulate(hp_sum, h1s, dm, width // 2)
-        for store in stores(parts, part_out, 0) + stores(dns, dn_out, 2):
-            store.wait()
-        pl.when(slot == 2)(lambda: cotangents.step(3))
-
-    for total, out, stage in (
-        (low_sum, low_out, h1s), (he_sum, he_out, dh), (hp_sum, hp_out, dm)
-    ):
-        step = count
-
-        @pl.loop(0, total.shape[0] // step)
-        def _(i):
-            at = rows_at(lax.rem(i, 2) * step, step)
-            move = pltpu.make_async_copy(
-                stage.at[at], out.at[rows_at(i * step, step)], store_sem.at[lax.rem(i, 2)]
+            for (here, there), sem in saves():
+                pltpu.make_async_copy(there, here, sem).start()
+            x_loads.start(2)
+            up_loads.start(2)
+            for (here, there), sem in saves():
+                pltpu.make_async_copy(there, here, sem).wait()
+            x_loads.wait(2)
+            up_loads.wait(2)
+
+        @pl.when(turn_index != 2)
+        def _():
+            slot = jnp.where(turn_index == 4, 2, turn_index)
+            chip = chip_of(slot)
+            ends = [ends_all[chip * 2 + b] for b in range(2)]
+            backward_pass(
+                xs, us, ends, count, angles_ref, norms_ref, qkv, slope, stats, proj_ref, exp_ref,
+                comb_ref, cont_ref, dh, dm, dns, sums, hbias, mbias, obias,
             )
-            pl.when(i >= 2)(lambda: move.wait())
-            stage[at, :] = total[rows_at(i * step, step), :].astype(bf16)
-            move.start()
-
-        for i in range(2):
-            pltpu.make_async_copy(
-                stage.at[rows_at(i * step, step)], out.at[rows_at(i * step, step)], store_sem.at[i]
-            ).wait()
-    vec_out[...] = jnp.zeros_like(vec_out)
-    own_out[...] = jnp.zeros_like(own_out)
+            store(dns, dn_own, d_in, 1, chip)
+            pl.when(slot == 0)(lambda: tokens.step(2))
+            pl.when(slot == 1)(lambda: cotangents.step(2))
+
+            @pl.when(turn_index < 2)
+            def _():
+                tokens.take(slot + 1)
+                x_loads.start(slot + 1)
+                cotangents.take(slot + 1)
+                up_loads.start(slot + 1)
+
+            accumulate(he_sum, h2s, dh, width // 2)
+            accumulate(hp_sum, h1s, dm, width // 2)
+            stored(dns, dn_own, d_in, 1, chip)
+
+    he.first()
+    low.second()
+    hp.first()
+    net.left(opening)
+
+    class Line:
+        def __init__(self, own, inward, land, total, first):
+            self.own, self.inward, self.land, self.total = own, inward, land, total
+            self.first = first
+            self.slot = net.slots(6)
+
+        def block(self, index):
+            return self.total.at[rows_at(index * count, count)]
+
+        def join(self):
+            room = [xs.at[pl.ds(i * count, count)] for i in range(2)]
+            room += [us.at[pl.ds(i * count, count)] for i in range(2)]
+            loads = []
+            for i in range(4):
+                loads.append(net.local(self.own.at[i], self.block(i)))
+                pltpu.make_async_remote_copy(
+                    src_ref=self.inward.at[i], dst_ref=self.inward.at[i],
+                    send_sem=cross_send.at[self.first],
+                    recv_sem=cross_recv.at[self.first * 4 + i],
+                    device_id=sibling, device_id_type=MESH,
+                ).wait_recv()
+                loads.append(net.local(self.inward.at[i], room[i]))
+            for i in range(4):
+                loads[2 * i].wait()
+                loads[2 * i + 1].wait()
+                add_into(self.block(i), room[i])
+
+        def push(self, block, step, side, when):
+            place = (step - 1) + (0 if side > 0 else 3)
+            net.send(
+                lambda: (self.block(block), self.land.at[place], (rep, me + 2 * side)),
+                self.slot + place, when,
+            )
+
+        def begin(self, steps):
+            for step in steps:
+                self.push(step, step, 1, z == 0)
+                self.push(3 - step, step, -1, z == 3)
+
+        def step_on(self, step):
+            for side in (1, -1):
+                place = (step - 1) + (0 if side > 0 else 3)
+                block = z + side * (step - 1)
+                here = (z >= 1) & (block <= 3) if side > 0 else (z <= 2) & (block >= 0)
+                index = net.locals
+                net.locals += 1
+
+                @pl.when(here)
+                def _():
+                    net.arrived(self.land.at[place], sibling, self.slot + place)
+                    load = pltpu.make_async_copy(
+                        self.land.at[place], comb_ref, local_sem.at[index]
+                    )
+                    load.start()
+                    load.wait()
+                    add_into(self.block(block), comb_ref)
+
+                if step > 1:
+                    self.push(block, step - 1, side, here)
+
+    out = Line(part_own, o_in, o_land, hs, 0)
+    back = Line(dn_own, d_in, d_land, pd, 1)
+    out.join()
+    out.begin((3, 2, 1))
+
+    vec_msg[...] = jnp.zeros_like(vec_msg)
+    vec_mix[...] = jnp.zeros_like(vec_mix)
     per = rows // LANES
     for t in range(8):
         for j in range(4):
             for i in range(per):
                 at = t * rows + i * LANES
-                vec_out[t, j * per + i : j * per + i + 1, :] = sums[j : j + 1, at : at + LANES]
+                vec_msg[t, j * per + i : j * per + i + 1, :] = sums[j : j + 1, at : at + LANES]
         for i in range(mix // LANES):
             at = 4 * per + i
-            vec_out[t, at : at + 1, :] = mbias[:, i * LANES : (i + 1) * LANES]
+            vec_msg[t, at : at + 1, :] = mbias[:, i * LANES : (i + 1) * LANES]
     for i in range(units // LANES):
-        own_out[i : i + 1, :] = hbias[:, i * LANES : (i + 1) * LANES]
+        vec_mix[56 + i : 57 + i, :] = hbias[:, i * LANES : (i + 1) * LANES]
     for i in range(per):
-        own_out[units // LANES + i : units // LANES + i + 1, :] = obias[
-            :, rows_at(me * rows + i * LANES, LANES)
-        ]
-    tokens.finish()
-    cotangents.finish()
-    net.finish()
-    assert net.sends <= GATHER_SEMS and net.started <= GATHER_SEMS and net.locals <= 8
-
-
-def block_passes(tokens, vectors, upstream, expander, projector, combiner, contractor, ebias, angles):
-    count, width = tokens.shape
-    n = lax.axis_size("shard")
-    units, mix, head = expander.shape[1] // n, projector.shape[1] // n, combiner.shape[0]
-    low = head + units
-    vmem, dma = pltpu.VMEM, pltpu.SemaphoreType.DMA
-    shapes = [
-        (n * count, width), (n * count, width), (low, width), (width, units), (width, mix),
-        (n // 2, 2, count, width), (n // 2, 2, count, width),
-    ]
-    two = 2 * count
-    return pl.pallas_call(
-        block_kernel,
-        out_shape=[jax.ShapeDtypeStruct(s, bf16) for s in shapes] + [
-            jax.ShapeDtypeStruct((n, 16, LANES), f32),
-            jax.ShapeDtypeStruct((16, LANES), f32),
-            jax.ShapeDtypeStruct((8, width), f32),
-        ],
-        in_specs=[pl.BlockSpec(memory_space=pl.ANY)] * 7 + [pl.BlockSpec(memory_space=vmem)] * 2,
-        out_specs=[pl.BlockSpec(memory_space=pl.ANY)] * 7 + [pl.BlockSpec(memory_space=vmem)] * 3,
-        scratch_shapes=[
-            vmem((width, units), bf16), vmem((width, mix), bf16), vmem((head, width), bf16),
-            vmem((units, width), bf16), vmem((low, width), f32), vmem((width, units), f32),
-            vmem((width, mix), f32),
-            vmem((two, width), bf16), vmem((two, width), bf16),
-            vmem((two, width), bf16), vmem((two, width), bf16), vmem((two, low), bf16),
-            vmem((two, units), bf16), vmem((two, mix), bf16), vmem((two, units), bf16),
-            vmem((two, mix), bf16), vmem((two, width), bf16), vmem((two, width), bf16),
-            vmem((two, LANES), f32),
-            vmem((n,) + vectors.shape, bf16), vmem((3 * n, 1, vectors.shape[1]), f32),
-            vmem((n, 1, LANES), f32),
-            vmem((1, mix), f32), vmem((4, width), f32), vmem((1, units), f32),
-            vmem((1, mix), f32), vmem((1, width), f32),
-            dma((GATHER_SEMS,)), dma((GATHER_SEMS,)), dma((8,)), dma((4,)), dma((4,)),
-        ] + [dma((8,))] * 8,
-        compiler_params=pltpu.CompilerParams(
-            collective_id=0, has_side_effects=True, vmem_limit_bytes=VMEM_LIMIT
-        ),
-    )(tokens, vectors, upstream, expander, projector, combiner, contractor, ebias, angles)
-
-
-def add_into(target, other):
-    rows = target.shape[-2]
-    step = min(32, rows)
-
-    @pl.loop(0, rows // step)
-    def _(i):
-        at = (Ellipsis, pl.ds(pl.multiple_of(i * step, step), step), slice(None))
-        lead = (slice(None),) * (len(target.shape) - 2)
-        at = lead + at[1:]
-        target[at] = (target[at].astype(f32) + other[at].astype(f32)).astype(target.dtype)
-
-
-def settle_kernel(
-    low_ref, he_ref, hp_ref, part_ref, dn_ref, vec_ref, own_ref,
-    low_out, exp_out, proj_out, osum_out, dsum_out, vec_out,
-    low_a, low_a1, low_a2, low_b, low_b1, low_b2,
-    he_a, he_a1, he_a2, he_b, he_b1, he_b2,
-    hp_a, hp_a1, hp_a2, hp_b, hp_b1, hp_b2,
-    o_in, o_sum, o_right, o_left, d_in, d_sum, d_right, d_left,
-    vec_in, vec_mix, vec_all, send_sem, recv_sem, local_sem,
-):
-    rep, me, y, x, z, c = position_of()
-    width = low_ref.shape[-1]
-    units, mix = he_ref.shape[-1], hp_ref.shape[-1]
-    head = mix // 3
-    sibling = (rep, me + 1 - 2 * c)
-    x_rep, y_rep, d_rep = rep + 1 - 2 * x, rep + 2 - 4 * y, 3 - rep
-    by_x, by_y, across = (x_rep, me), (y_rep, me), (d_rep, me)
-    ring = [(rep, lax.rem(me + k, 8)) for k in range(1, 8)]
-    meet(ring + [by_x, by_y, across])
-    net = Net(send_sem, recv_sem, local_sem)
-
-    class Sum:
-        def __init__(self, ref, at, a, a1, a2, b, b1, b2):
-            self.ref, self.at = ref, at
-            self.a, self.a1, self.a2, self.b, self.b1, self.b2 = a, a1, a2, b, b1, b2
-            self.slot = net.slots(6)
-
-        def load(self):
-            self.loads = []
-            for i in range(2):
-                self.loads.append(net.local(self.at(self.ref, i * 2 + x, 0), self.a.at[i]))
-                self.loads.append(net.local(self.at(self.ref, y * 2 + i, 1), self.b.at[i]))
-
-        def first(self):
-            for i in range(2):
-                source = self.at(self.ref, i * 2 + 1 - x, 0)
-                net.send(source, self.a1.at[i], by_x, self.slot + i)
-                source = self.at(self.ref, (1 - y) * 2 + i, 1)
-                net.send(source, self.b1.at[i], by_y, self.slot + 2 + i)
-
-        def second(self):
-            for load in self.loads:
-                load.wait()
-            for i in range(2):
-                net.arrived(self.a1.at[i], sibling, self.slot + i)
-                add_into(self.a.at[i], self.a1.at[i])
-            net.send(self.a.at[1 - y], self.a2, by_y, self.slot + 4)
-            for i in range(2):
-                net.arrived(self.b1.at[i], sibling, self.slot + 2 + i)
-                add_into(self.b.at[i], self.b1.at[i])
-            net.send(self.b.at[1 - x], self.b2, by_x, self.slot + 5)
-
-        def third(self):
-            net.arrived(self.a2, sibling, self.slot + 4)
-            add_into(self.a.at[y], self.a2)
-            net.arrived(self.b2, sibling, self.slot + 5)
-            add_into(self.b.at[x], self.b2)
-            return self.a.at[y], self.b.at[x]
-
-    def deep(ref, quarter, half):
-        return ref.at[:, quarter, half]
-
-    he = Sum(he_ref, deep, he_a, he_a1, he_a2, he_b, he_b1, he_b2)
-    hp = Sum(hp_ref, deep, hp_a, hp_a1, hp_a2, hp_b, hp_b1, hp_b2)
-    low = Sum(
-        low_ref, lambda ref, quarter, half: ref.at[quarter, half],
-        low_a, low_a1, low_a2, low_b, low_b1, low_b2,
-    )
-
-    he.first()
-    hp.first()
-    he.load()
-    hp.load()
-
-    class Line:
-        def __init__(self, ref, inward, total, right, left):
-            self.inward, self.total, self.right, self.left = inward, total, right, left
-            self.slot = net.slots(10)
-            self.loads = []
-            for i in range(4):
-                net.send(ref.at[i, 1 - c], inward.at[i], sibling, self.slot + i)
-                self.loads.append(net.local(ref.at[i, c], total.at[i]))
-
-        def push(self, block, step, side, when):
-            into = self.right if side > 0 else self.left
-            slot = self.slot + 4 + (step - 1) + (0 if side > 0 else 3)
-            net.send(self.total.at[block], into.at[step - 1], (rep, me + 2 * side), slot, when)
-
-        def join(self):
-            for i in range(4):
-                self.loads[i].wait()
-                net.arrived(self.inward.at[i], sibling, self.slot + i)
-                add_into(self.total.at[i], self.inward.at[i])
-
-        def begin(self):
-            for step in (3, 2, 1):
-                self.push(step, step, 1, z == 0)
-                self.push(3 - step, step, -1, z == 3)
-
-        def step_on(self, step):
-            for side, into, first in ((1, self.right, 4), (-1, self.left, 7)):
-                block = z + side * (step - 1)
-                here = (z >= 1) & (block <= 3) if side > 0 else (z <= 2) & (block >= 0)
-
-                @pl.when(here)
-                def _():
-                    net.arrived(into.at[step - 1], sibling, self.slot + first + step - 1)
-                    add_into(self.total.at[block], into.at[step - 1])
-
-                if step > 1:
-                    self.push(block, step - 1, side, here)
-
-    out = Line(part_ref, o_in, o_sum, o_right, o_left)
-    back = Line(dn_ref, d_in, d_sum, d_right, d_left)
-
+        vec_mix[64 + i : 65 + i, :] = obias[:, rows_at(me * rows + i * LANES, LANES)]
     small = net.slots(7)
     for k in range(1, 8):
         t = lax.rem(me + k, 8)
-        net.send(vec_ref.at[t], vec_in.at[me], (rep, t), small + k - 1)
-    vec_load = net.local(vec_ref.at[me], vec_in.at[me])
-    own_load = net.local(own_ref, vec_mix.at[pl.ds(56, 16)])
-    low.load()
-
-    out.join()
-    out.begin()
+        net.send(lambda t=t: (vec_msg.at[t], vec_in.at[me], (rep, t)), small + k - 1)
+    vec_load = net.local(vec_msg.at[me], vec_in.at[me])
+
     he.second()
     out.step_on(3)
+    net.left(low.sent)
     back.join()
     hp.second()
-    low.first()
     out.step_on(2)
+    low_done = low.third()
 
     class Turn:
         def __init__(self, source, half, place):
@@ -1102,7 +1140,10 @@
             for k in range(1, 8):
                 t = lax.rem(me + k, 8)
                 for j, (src, dst) in enumerate(place(source, t, me)):
-                    net.send(src, dst, (rep, t), self.slot + (k - 1) * 3 + j)
+                    net.send(
+                        lambda src=src, dst=dst, t=t: (src, dst, (rep, t)),
+                        self.slot + (k - 1) * 3 + j,
+                    )
             for src, dst in place(source, me, me):
                 self.copies.append(net.local(src, dst))
 
@@ -1114,16 +1155,19 @@
             for copy in self.copies:
                 copy.wait()
 
+    eighth = rows // 8
+
     def place_exp(half):
         return lambda source, t, s: [(
-            None if source is None else source.at[t],
+            None if source is None else source.at[rows_at(t * eighth, eighth)],
             exp_out.at[rep, half, :, rows_at(s * units, units)],
         )]
 
     def place_proj(half):
         return lambda source, t, s: [
             (
-                None if source is None else source.at[t, :, pl.ds(j * head, head)],
+                None if source is None
+                else source.at[rows_at(t * eighth, eighth), pl.ds(j * head, head)],
                 proj_out.at[rep, half, :, rows_at(j * width + s * head, head)],
             )
             for j in range(3)
@@ -1133,13 +1177,40 @@
     he_turns = [Turn(he_done[h], h, place_exp(h)) for h in range(2)]
     hp_done = hp.third()
     hp_turns = [Turn(hp_done[h], h, place_proj(h)) for h in range(2)]
+
+    class Spread:
+        def __init__(self, target, sources):
+            self.target, self.slot = target, net.slots(6)
+            for h, source in enumerate(sources):
+                for k, peer in enumerate((by_x, by_y)):
+                    net.send(
+                        lambda source=source, h=h, peer=peer: (source, target.at[rep, h], peer),
+                        self.slot + h * 3 + k,
+                    )
+
+        def on(self):
+            for h, (k, got, peer) in enumerate(((1, y_rep, by_x), (0, x_rep, by_y))):
+                net.arrived(self.target.at[got, h], sibling, self.slot + h * 3 + k)
+                net.send(
+                    lambda h=h, got=got, peer=peer: (
+                        self.target.at[got, h], self.target.at[got, h], peer
+                    ),
+                    self.slot + h * 3 + 2,
+                )
+
+        def wait(self):
+            for h, (k, got) in enumerate(((0, x_rep), (1, y_rep))):
+                net.arrived(self.target.at[got, h], sibling, self.slot + h * 3 + k)
+                net.arrived(self.target.at[d_rep, h], sibling, self.slot + h * 3 + 2)
+
+    low_copies = [net.local(low_done[h], low_out.at[rep, h]) for h in range(2)]
+    low_spread = Spread(low_out, low_done)
     out.step_on(1)
-    back.begin()
-    low.second()
+    back.begin((3, 2, 1))
+
     for k in range(1, 8):
         net.arrived(vec_in.at[lax.rem(me + 8 - k, 8)], sibling, small + k - 1)
     vec_load.wait()
-    own_load.wait()
     total = vec_in[0, 0:8]
     for s in range(1, 8):
         total += vec_in[s, 0:8]
@@ -1147,39 +1218,18 @@
     for s in range(8):
         vec_mix[8 + 6 * s : 14 + 6 * s] = vec_in[s, 8:14]
     wide = net.slots(4)
-    net.send(vec_mix, vec_all.at[rep], by_x, wide + 1)
-    net.send(vec_mix, vec_all.at[rep], by_y, wide + 2)
-    net.send(vec_mix, vec_all.at[rep], across, wide + 3)
+    for k, peer in ((1, by_x), (2, by_y), (3, across)):
+        net.send(lambda peer=peer: (vec_mix, vec_all.at[rep], peer), wide + k)
     vec_copy = net.local(vec_mix, vec_all.at[rep])
 
-    class Spread:
-        def __init__(self, target, sources):
-            self.target, self.slot = target, net.slots(6)
-            for h, source in enumerate(sources):
-                for k, peer in enumerate((by_x, by_y)):
-                    net.send(source, target.at[rep, h], peer, self.slot + h * 3 + k)
-
-        def on(self):
-            for h, (k, got, peer) in enumerate(((1, y_rep, by_x), (0, x_rep, by_y))):
-                net.arrived(self.target.at[got, h], sibling, self.slot + h * 3 + k)
-                net.send(self.target.at[got, h], self.target.at[got, h], peer, self.slot + h * 3 + 2)
-
-        def wait(self):
-            for h, (k, got) in enumerate(((0, x_rep), (1, y_rep))):
-                net.arrived(self.target.at[got, h], sibling, self.slot + h * 3 + k)
-                net.arrived(self.target.at[d_rep, h], sibling, self.slot + h * 3 + 2)
-
-    low_done = low.third()
-    low_copies = [net.local(low_done[h], low_out.at[rep, h]) for h in range(2)]
-    low_spread = Spread(low_out, low_done)
-    for turn in he_turns:
-        turn.wait()
+    for turn_of in he_turns:
+        turn_of.wait()
     he_spread = Spread(exp_out, [exp_out.at[rep, h] for h in range(2)])
-    for turn in hp_turns:
-        turn.wait()
+    for turn_of in hp_turns:
+        turn_of.wait()
     hp_spread = Spread(proj_out, [proj_out.at[rep, h] for h in range(2)])
+    low_spread.on()
     back.step_on(3)
-    low_spread.on()
     back.step_on(2)
     he_spread.on()
     hp_spread.on()
@@ -1188,64 +1238,77 @@
     vec_copy.wait()
     vec_out[...] = (vec_all[0] + vec_all[1]) + (vec_all[2] + vec_all[3])
     back.step_on(1)
-    osum_copy = net.local(o_sum.at[z], osum_out)
-    dsum_copy = net.local(d_sum.at[z], dsum_out)
+    osum_copy = net.local(out.block(z), osum_out)
+    dsum_copy = net.local(back.block(z), dsum_out)
     low_spread.wait()
     he_spread.wait()
     hp_spread.wait()
     for copy in low_copies + [osum_copy, dsum_copy]:
         copy.wait()
-    net.finish()
-    assert net.sends <= SETTLE_SEMS and net.started <= SETTLE_SEMS and net.locals <= 64, (
+    tokens.finish()
+    cotangents.finish()
+    net.left(net.sent + he.sent + hp.sent)
+    assert net.sends <= SENDS and net.started <= SENDS and net.locals <= LOCALS, (
         net.sends, net.started, net.locals)
 
 
-SETTLE_SEMS = 224
-
-
-def settle(low, he, hp, part, dn, vec, own):
+SENDS = 320
+LOCALS = 80
+
+
+def block_passes(tokens, vectors, upstream, expander, projector, combiner, contractor, ebias, angles):
+    count, width = tokens.shape
     n = lax.axis_size("shard")
-    low_rows, width = low.shape
-    units, mix = he.shape[1], hp.shape[1]
-    rows, eighth, count = width // n, width // n // 8, part.shape[2]
-    low = low.reshape(4, 2, low_rows // 8, width)
-    he = he.reshape(n, 4, 2, eighth, units)
-    hp = hp.reshape(n, 4, 2, eighth, mix)
-    vmem = pltpu.VMEM
-
-    def pieces(*shape):
-        return [vmem((2,) + shape, bf16), vmem((2,) + shape, bf16), vmem(shape, bf16)] * 2
-
-    block = (count, width)
-    line = [vmem((k,) + block, bf16) for k in (4, 4, 3, 3)]
+    units, mix, head = expander.shape[1] // n, projector.shape[1] // n, combiner.shape[0]
+    low, rows, two = head + units, width // n, 2 * count
+    eighth = rows // 8
+    vmem, dma = pltpu.VMEM, pltpu.SemaphoreType.DMA
     anywhere = pl.BlockSpec(memory_space=pl.ANY)
+    block = (n // 2, count, width)
+    results = [
+        (4, 2, low // 8, width), (4, 2, eighth, n * units), (4, 2, eighth, n * mix),
+        (count, width), (count, width),
+    ]
+    passing = [
+        (n * count, width), (n * count, width), block, block, block, block,
+        (6, count, width), (6, count, width),
+        (6, low // 8, width), (6, n * eighth, units), (6, n * eighth, mix),
+        (2 * two, width), (two, mix), (two, units),
+    ]
     result = pl.pallas_call(
-        settle_kernel,
-        out_shape=[
-            jax.ShapeDtypeStruct((4, 2, low_rows // 8, width), bf16),
-            jax.ShapeDtypeStruct((4, 2, eighth, n * units), bf16),
-            jax.ShapeDtypeStruct((4, 2, eighth, n * mix), bf16),
-            jax.ShapeDtypeStruct(block, bf16),
-            jax.ShapeDtypeStruct(block, bf16),
-            jax.ShapeDtypeStruct((72, LANES), f32),
+        block_kernel,
+        out_shape=[jax.ShapeDtypeStruct(s, bf16) for s in results] + [
+            jax.ShapeDtypeStruct((72, LANES), f32), jax.ShapeDtypeStruct((8, width), f32),
+        ] + [jax.ShapeDtypeStruct(s, bf16) for s in passing] + [
+            jax.ShapeDtypeStruct((two, LANES), f32)
         ],
-        in_specs=[anywhere] * 7,
-        out_specs=[anywhere] * 5 + [pl.BlockSpec(memory_space=vmem)],
-        scratch_shapes=pieces(low_rows // 8, width)
-        + pieces(n, eighth, units) + pieces(n, eighth, mix) + line + line + [
-            vmem((8, 16, LANES), f32), vmem((72, LANES), f32), vmem((4, 72, LANES), f32),
-            pltpu.SemaphoreType.DMA((SETTLE_SEMS,)),
-            pltpu.SemaphoreType.DMA((SETTLE_SEMS,)),
-            pltpu.SemaphoreType.DMA((64,)),
-        ],
+        in_specs=[anywhere] * 7 + [pl.BlockSpec(memory_space=vmem)] * 2,
+        out_specs=[anywhere] * 5 + [pl.BlockSpec(memory_space=vmem)] * 2
+        + [anywhere] * (len(passing) + 1),
+        scratch_shapes=[
+            vmem((width, units), bf16), vmem((width, mix), bf16), vmem((head, width), bf16),
+            vmem((units, width), bf16), vmem((low, width), f32), vmem((width, units), f32),
+            vmem((width, mix), f32),
+            vmem((two, width), bf16), vmem((two, width), bf16), vmem((2 * two, width), bf16),
+            vmem((2 * two, width), bf16), vmem((two, low), bf16),
+            vmem((two, units), bf16), vmem((two, mix), bf16), vmem((two, units), bf16),
+            vmem((two, mix), bf16), vmem((low // 8, width), bf16), vmem((two, LANES), f32),
+            vmem((n,) + vectors.shape, bf16), vmem((3 * n, 1, vectors.shape[1]), f32),
+            vmem((n, 1, LANES), f32),
+            vmem((1, mix), f32), vmem((4, width), f32), vmem((1, units), f32),
+            vmem((1, mix), f32), vmem((1, width), f32),
+            vmem((n, 16, LANES), f32), vmem((n, 16, LANES), f32), vmem((72, LANES), f32),
+            vmem((4, 72, LANES), f32),
+            dma((SENDS,)), dma((SENDS,)), dma((LOCALS,)), dma((4,)), dma((6,)), dma((2,)), dma((8,)),
+        ] + [dma((8,))] * 8,
         compiler_params=pltpu.CompilerParams(
-            collective_id=1, has_side_effects=True, vmem_limit_bytes=VMEM_LIMIT
+            collective_id=0, has_side_effects=True, vmem_limit_bytes=VMEM_LIMIT
         ),
-    )(low, he, hp, part, dn, vec, own)
-    low, exp, proj, osum, dsum, vec = result
+    )(tokens, vectors, upstream, expander, projector, combiner, contractor, ebias, angles)
+    low_sum, exp_sum, proj_sum, osum, dsum, vec, norms = result[:7]
     return (
-        low.reshape(low_rows, width), exp.reshape(rows, n * units), proj.reshape(rows, n * mix),
-        osum, dsum, vec,
+        low_sum.reshape(low, width), exp_sum.reshape(rows, n * units),
+        proj_sum.reshape(rows, n * mix), osum, dsum, vec, norms,
     )
 
 
@@ -1276,11 +1339,10 @@
     angles = jnp.stack(
         [jnp.concatenate([freqs, freqs, still]), jnp.concatenate([-ones, ones, still])]
     )
-    _, _, low, he, hp, part, dn, vec, own, norms = block_passes(
+    low, exp_out, proj_out, osum, dsum, vec, norms = block_passes(
         tokens, vectors, upstream, expander, projector, combiner, contractor,
         expbias.astype(f32)[None], angles,
     )
-    low, exp_out, proj_out, osum, dsum, vec = settle(low, he, hp, part, dn, vec, own)
 
     floated = tokens.astype(f32)
     block_output = floated + jnp.where(

time: 488 us -> 461 us (0.945)
  Pallas kernels: 449 us -> 424 us
    pallas_call x1 -> x0, Pallas kernels: 214 us -> none  [settle(): pl.pallas_call(settle_kernel, out_shape=[jax.ShapeDtypeStruct((4, 2, low_...]
    pallas_call x1, Pallas kernels: 235 us -> 424 us  [block_passes(): pl.pallas_call(block_kernel, out_shape=[jax.ShapeDtypeStruct(s, bf16) for...]
where the time goes in v6:
time: 461 us; the launch traced here: 458 us
  Pallas kernels  424 us (92%)
  other arithmetic  26.9 us (6%)
  local copies, waits for them, and re-layouts  6.64 us (1%)
    pallas_call x1, Pallas kernels, block_passes(): pl.pallas_call(block_kernel, out_shape=[jax.ShapeDtypeStruct(s, bf16) for...  424 us

profile of v6, /device:TPU:10, one launch (start us, length us, event | category | flops | bytes accessed | tf_op | source)
XLA Modules:
  0.0 458.2 jit_solution(16857495160380429200)
XLA Ops:
  0.6 0.0 copy-start.16
  0.7 0.0 copy-start.17
  0.7 0.0 copy-start.10
  0.7 0.0 copy-start.11
  0.7 0.0 copy-start.12
  0.7 0.0 copy-start.13
  0.7 0.0 copy-start.14
  0.7 0.0 copy-start.15
  0.7 0.0 copy-start.9
  0.7 0.0 copy-start.8
  0.8 1.3 slice.58
  2.0 0.6 iota_compare_fusion
  2.7 2.3 broadcast_select_fusion.up_ref
  5.0 0.2 dynamic-update-slice
  5.2 0.0 copy-done.11
  5.2 0.2 dynamic-update-slice.1
  5.4 0.2 dynamic-update-slice.2
  5.7 0.2 dynamic-update-slice.3
  5.9 0.0 copy-done.14
  5.9 0.2 dynamic-update-slice.4
  6.1 0.2 dynamic-update-slice.5
  6.3 0.2 dynamic-update-slice.6
  6.5 0.0 copy-done.17
  6.5 0.2 dynamic-update-slice.7
  6.8 0.6 reshape.90.vec_ref
  7.4 0.6 broadcast_in_dim.42
  8.0 0.1 maximum_bitcast_fusion
  8.1 0.6 pad_maximum_fusion.angles_ref
  8.6 423.8 %shard_map.254 = (bf16[4,2,160,2048]{3,2,1,0:T(8,128)(2,1)}, bf16[4,2,32,8192]{3,2,1,0:T(8,128)(2,1)}, bf16[4,2,32,6144]{3,2,1,0:T(8,128)(2,1)}, bf16[256,2048]{...) custom-call(bf16[256,2048]{1,0:T(8,128)(2,1)} %tok_ref.1, ...), custom_call_target="tpu_custom_call" | custom-call | tf_op jit(solution)/shard_map/pallas_call | solution.py:1278
  432.5 0.0 copy-start.2
  432.5 0.0 copy-start.5
  432.5 0.2 convert_reduce_fusion.1
  432.8 0.4 fusion.7
  433.2 0.5 copy-done.3
  433.7 0.7 convert_reduce_fusion
  434.4 0.9 slice_add_fusion
  435.4 2.4 fusion.6
  437.8 0.0 copy-done.6
  437.9 0.7 dynamic_slice.3
  438.5 0.6 slice_bitcast_fusion.1
  439.1 0.6 slice_bitcast_fusion
  439.7 6.8 %slice_convert_fusion = f32[1024,2048]{1,0:T(8,128)} fusion(bf16[1280,2048]{1,0:T(8,128)(2,1)} %bitcast.31), kind=kLoop, calls=%fused_computation | loop fusion | flops 2097152 | bytes 12582912 | tf_op jit(solution)/shard_map/convert_element_type | solution.py:1369
  446.5 2.8 slice_convert_fusion.1
  449.3 0.0 copy-done.1
  449.3 4.7 %bitcast_convert_fusion = f32[256,8192]{1,0:T(8,128)} fusion(bf16[4,2,32,8192]{3,2,1,0:T(8,128)(2,1)S(1)} %copy-done.1), kind=kLoop, calls=%fused_computation.1 | loop fusion | flops 2097152 | bytes 12582912 | tf_op jit(solution)/shard_map/convert_element_type | solution.py:1369
  454.0 3.7 bitcast_convert_fusion.1
  457.6 0.0 copy-done.7
  457.6 0.6 copy.42
  (29 shorter events, 0.1 us)
Async XLA Ops:
  0.6 7.4 %copy-start.16 = (f32[1,128]{1,0:T(1,128)S(1)}, f32[1,128]{1,0:T(1,128)}, u32[]{:S(2)}) copy-start(f32[1,128]{1,0:T(1,128)} %constant.7.clone.1) | copy-start | bytes 1540
  0.7 5.9 %copy-start.17 = (s32[1,4]{1,0:T(1,128)S(1)}, s32[1,4]{1,0:T(1,128)}, u32[]{:S(2)}) copy-start(s32[1,4]{1,0:T(1,128)} %param.16) | copy-start | bytes 52
  0.7 4.4 copy-start.10
  0.7 4.5 copy-start.11
  0.7 4.7 %copy-start.12 = (bf16[256]{0:T(256)(128)(2,1)S(1)}, bf16[256]{0:T(256)(128)(2,1)}, u32[]{:S(2)}) copy-start(bf16[256]{0:T(256)(128)(2,1)} %param.27) | copy-start | bytes 1540
  0.7 4.9 %copy-start.13 = (bf16[256]{0:T(256)(128)(2,1)S(1)}, bf16[256]{0:T(256)(128)(2,1)}, u32[]{:S(2)}) copy-start(bf16[256]{0:T(256)(128)(2,1)} %param.28) | copy-start | bytes 1540
  0.7 5.2 %copy-start.14 = (bf16[256]{0:T(256)(128)(2,1)S(1)}, bf16[256]{0:T(256)(128)(2,1)}, u32[]{:S(2)}) copy-start(bf16[256]{0:T(256)(128)(2,1)} %param.20) | copy-start | bytes 1540
  0.7 5.4 %copy-start.15 = (bf16[256]{0:T(256)(128)(2,1)S(1)}, bf16[256]{0:T(256)(128)(2,1)}, u32[]{:S(2)}) copy-start(bf16[256]{0:T(256)(128)(2,1)} %param.24) | copy-start | bytes 1540
  0.7 5.6 %copy-start.9 = (bf16[768]{0:T(1024)(128)(2,1)S(1)}, bf16[768]{0:T(1024)(128)(2,1)}, u32[]{:S(2)}) copy-start(bf16[768]{0:T(1024)(128)(2,1)} %param.18) | copy-start | bytes 4612
  0.7 6.6 %copy-start.8 = (bf16[1024]{0:T(1024)(128)(2,1)S(1)}, bf16[1024]{0:T(1024)(128)(2,1)}, u32[]{:S(2)}) copy-start(bf16[1024]{0:T(1024)(128)(2,1)} %param.22) | copy-start | bytes 6148
  8.6 423.9 %copy-start = (bf16[256,2048]{1,0:T(8,128)(2,1)S(1)}, bf16[256,2048]{1,0:T(8,128)(2,1)}, u32[]{:S(2)}) copy-start(bf16[256,2048]{1,0:T(8,128)(2,1)} %tok_ref.1) | copy-start | bytes 3145732
  432.5 1.2 copy-start.3
  432.5 2.9 copy-start.2
  432.5 2.8 copy-start.5
  435.4 2.4 copy-start.6
  439.1 18.5 %copy-start.7 = (f32[256]{0:T(256)}, f32[256]{0:T(256)S(1)}, u32[]{:S(2)}) copy-start(f32[256]{0:T(256)S(1)} %get-tuple-element.62) | copy-start | bytes 3076
  439.7 9.6 %copy-start.1 = (bf16[4,2,32,8192]{3,2,1,0:T(8,128)(2,1)S(1)}, bf16[4,2,32,8192]{3,2,1,0:T(8,128)(2,1)}, u32[]{:S(2)}) copy-start(bf16[4,2,32,8192]{3,2,1,0:T(8,128)(2,1)} %get-tuple-element.27) | copy-start | bytes 12582916
  449.3 4.7 %copy-start.4 = (bf16[4,2,32,6144]{3,2,1,0:T(8,128)(2,1)S(1)}, bf16[4,2,32,6144]{3,2,1,0:T(8,128)(2,1)}, u32[]{:S(2)}) copy-start(bf16[4,2,32,6144]{3,2,1,0:T(8,128)(2,1)} %get-tuple-element.24) | copy-start | bytes 9437188

commit v7 on v6

--- a/solution.py
+++ b/solution.py
@@ -644,7 +644,7 @@
 def block_kernel(
     tok_ref, vec_ref, up_ref, expander_ref, projector_ref, comb_hbm, cont_hbm, ebias_ref,
     angles_ref,
-    low_out, exp_out, proj_out, osum_out, dsum_out, vec_out, norms_ref,
+    comb_out, cont_out, exp_out, proj_out, osum_out, dsum_out, vec_out, norms_ref,
     x_out, up_out, part_own, dn_own, o_in, d_in, o_land, d_land, low_land, he_land, hp_land,
     h_save, qkv_save, slope_save, stats_save,
     exp_ref, proj_ref, comb_ref, cont_ref, low_sum, he_sum, hp_sum,
@@ -684,7 +684,7 @@
     for i in range(3):
         down, up = 3 - i, i
         chips.append(jnp.where(
-            z < 2, jnp.where(down <= z, down - 1, down), jnp.where(up >= z, up + 1, up)
+            z < 2, jnp.where(up >= z, up + 1, up), jnp.where(down <= z, down - 1, down)
         ))
     for chip in chips:
         for core in (0, 1):
@@ -866,6 +866,8 @@
         pairs = [(hs, h_save), (qkv, qkv_save), (slope, slope_save), (stats, stats_save)]
         return [(pair, store_sem.at[2 + i]) for i, pair in enumerate(pairs)]
 
+    restores = [pltpu.make_async_copy(there, here, sem) for (here, there), sem in saves()]
+
     class Piece:
         def __init__(self, total, land, start, step, stage, tmp):
             self.total, self.land, self.start, self.step = total, land, start, step
@@ -946,7 +948,9 @@
             return [self.room((2 + half) * self.size) for half in range(2)]
 
     def low_start(quarter, half, i):
-        return quarter * (low_sum.shape[0] // 4) + half * (low_sum.shape[0] // 8) + i * 32
+        first = quarter * (head // 4) + half * (head // 8)
+        rest = head + quarter * (units // 4) + half * (units // 8) + (i - 1) * 32
+        return jnp.where(i == 0, first, rest)
 
     def high_start(quarter, half, i):
         return i * rows + quarter * (rows // 4) + half * (rows // 8)
@@ -1000,12 +1004,9 @@
 
         @pl.when(turn_index == 4)
         def _():
-            for (here, there), sem in saves():
-                pltpu.make_async_copy(there, here, sem).start()
-            x_loads.start(2)
-            up_loads.start(2)
-            for (here, there), sem in saves():
-                pltpu.make_async_copy(there, here, sem).wait()
+            restores[0].start()
+            for restore in restores[1:]:
+                restore.wait()
             x_loads.wait(2)
             up_loads.wait(2)
 
@@ -1029,14 +1030,20 @@
                 cotangents.take(slot + 1)
                 up_loads.start(slot + 1)
 
+            @pl.when(turn_index == 3)
+            def _():
+                for restore in restores[1:]:
+                    restore.start()
+                x_loads.start(2)
+                up_loads.start(2)
+
+            pl.when(turn_index == 4)(lambda: restores[0].wait())
             accumulate(he_sum, h2s, dh, width // 2)
             accumulate(hp_sum, h1s, dm, width // 2)
             stored(dns, dn_own, d_in, 1, chip)
 
+    net.left(opening)
     he.first()
-    low.second()
-    hp.first()
-    net.left(opening)
 
     class Line:
         def __init__(self, own, inward, land, total, first):
@@ -1102,6 +1109,8 @@
     back = Line(dn_own, d_in, d_land, pd, 1)
     out.join()
     out.begin((3, 2, 1))
+    hp.first()
+    low.second()
 
     vec_msg[...] = jnp.zeros_like(vec_msg)
     vec_mix[...] = jnp.zeros_like(vec_mix)
@@ -1132,6 +1141,36 @@
     out.step_on(2)
     low_done = low.third()
 
+    class Spread:
+        def __init__(self, target, sources):
+            self.target, self.slot = target, net.slots(6)
+            for h, source in enumerate(sources):
+                for k, peer in enumerate((by_x, by_y)):
+                    net.send(
+                        lambda source=source, h=h, peer=peer: (source, target.at[rep, h], peer),
+                        self.slot + h * 3 + k,
+                    )
+
+        def on(self):
+            for h, (k, got, peer) in enumerate(((1, y_rep, by_x), (0, x_rep, by_y))):
+                net.arrived(self.target.at[got, h], sibling, self.slot + h * 3 + k)
+                net.send(
+                    lambda h=h, got=got, peer=peer: (
+                        self.target.at[got, h], self.target.at[got, h], peer
+                    ),
+                    self.slot + h * 3 + 2,
+                )
+
+        def wait(self):
+            for h, (k, got) in enumerate(((0, x_rep), (1, y_rep))):
+                net.arrived(self.target.at[got, h], sibling, self.slot + h * 3 + k)
+                net.arrived(self.target.at[d_rep, h], sibling, self.slot + h * 3 + 2)
+
+    low_copies, low_spreads = [], []
+    for target, first in ((cont_out, head // 8), (comb_out, 0)):
+        pieces = [done.at[pl.ds(first, target.shape[2])] for done in low_done]
+        low_copies += [net.local(pieces[h], target.at[rep, h]) for h in range(2)]
+        low_spreads.append(Spread(target, pieces))
     class Turn:
         def __init__(self, source, half, place):
             self.half, self.place = half, place
@@ -1178,33 +1217,6 @@
     hp_done = hp.third()
     hp_turns = [Turn(hp_done[h], h, place_proj(h)) for h in range(2)]
 
-    class Spread:
-        def __init__(self, target, sources):
-            self.target, self.slot = target, net.slots(6)
-            for h, source in enumerate(sources):
-                for k, peer in enumerate((by_x, by_y)):
-                    net.send(
-                        lambda source=source, h=h, peer=peer: (source, target.at[rep, h], peer),
-                        self.slot + h * 3 + k,
-                    )
-
-        def on(self):
-            for h, (k, got, peer) in enumerate(((1, y_rep, by_x), (0, x_rep, by_y))):
-                net.arrived(self.target.at[got, h], sibling, self.slot + h * 3 + k)
-                net.send(
-                    lambda h=h, got=got, peer=peer: (
-                        self.target.at[got, h], self.target.at[got, h], peer
-                    ),
-                    self.slot + h * 3 + 2,
-                )
-
-        def wait(self):
-            for h, (k, got) in enumerate(((0, x_rep), (1, y_rep))):
-                net.arrived(self.target.at[got, h], sibling, self.slot + h * 3 + k)
-                net.arrived(self.target.at[d_rep, h], sibling, self.slot + h * 3 + 2)
-
-    low_copies = [net.local(low_done[h], low_out.at[rep, h]) for h in range(2)]
-    low_spread = Spread(low_out, low_done)
     out.step_on(1)
     back.begin((3, 2, 1))
 
@@ -1228,11 +1240,12 @@
     for turn_of in hp_turns:
         turn_of.wait()
     hp_spread = Spread(proj_out, [proj_out.at[rep, h] for h in range(2)])
-    low_spread.on()
+    for spread in low_spreads:
+        spread.on()
+    he_spread.on()
     back.step_on(3)
+    hp_spread.on()
     back.step_on(2)
-    he_spread.on()
-    hp_spread.on()
     for k, r in ((1, x_rep), (2, y_rep), (3, d_rep)):
         net.arrived(vec_all.at[r], sibling, wide + k)
     vec_copy.wait()
@@ -1240,7 +1253,8 @@
     back.step_on(1)
     osum_copy = net.local(out.block(z), osum_out)
     dsum_copy = net.local(back.block(z), dsum_out)
-    low_spread.wait()
+    for spread in low_spreads:
+        spread.wait()
     he_spread.wait()
     hp_spread.wait()
     for copy in low_copies + [osum_copy, dsum_copy]:
@@ -1266,7 +1280,8 @@
     anywhere = pl.BlockSpec(memory_space=pl.ANY)
     block = (n // 2, count, width)
     results = [
-        (4, 2, low // 8, width), (4, 2, eighth, n * units), (4, 2, eighth, n * mix),
+        (4, 2, head // 8, width), (4, 2, units // 8, width),
+        (4, 2, eighth, n * units), (4, 2, eighth, n * mix),
         (count, width), (count, width),
     ]
     passing = [
@@ -1283,7 +1298,7 @@
             jax.ShapeDtypeStruct((two, LANES), f32)
         ],
         in_specs=[anywhere] * 7 + [pl.BlockSpec(memory_space=vmem)] * 2,
-        out_specs=[anywhere] * 5 + [pl.BlockSpec(memory_space=vmem)] * 2
+        out_specs=[anywhere] * 6 + [pl.BlockSpec(memory_space=vmem)] * 2
         + [anywhere] * (len(passing) + 1),
         scratch_shapes=[
             vmem((width, units), bf16), vmem((width, mix), bf16), vmem((head, width), bf16),
@@ -1305,9 +1320,9 @@
             collective_id=0, has_side_effects=True, vmem_limit_bytes=VMEM_LIMIT
         ),
     )(tokens, vectors, upstream, expander, projector, combiner, contractor, ebias, angles)
-    low_sum, exp_sum, proj_sum, osum, dsum, vec, norms = result[:7]
+    comb_sum, cont_sum, exp_sum, proj_sum, osum, dsum, vec, norms = result[:8]
     return (
-        low_sum.reshape(low, width), exp_sum.reshape(rows, n * units),
+        comb_sum.reshape(head, width), cont_sum.reshape(units, width), exp_sum.reshape(rows, n * units),
         proj_sum.reshape(rows, n * mix), osum, dsum, vec, norms,
     )
 
@@ -1339,7 +1354,7 @@
     angles = jnp.stack(
         [jnp.concatenate([freqs, freqs, still]), jnp.concatenate([-ones, ones, still])]
     )
-    low, exp_out, proj_out, osum, dsum, vec, norms = block_passes(
+    comb_out, cont_out, exp_out, proj_out, osum, dsum, vec, norms = block_passes(
         tokens, vectors, upstream, expander, projector, combiner, contractor,
         expbias.astype(f32)[None], angles,
     )
@@ -1365,8 +1380,8 @@
     rest = vec[4 * rows + n * mix :]
     hidden_bias, out_bias = rest[:units], rest[units : units + rows]
     return (
-        block_output, input_gradient, proj_out.astype(f32), mixed_bias, low[:head].astype(f32), out_bias,
-        exp_out.astype(f32), hidden_bias, low[head:].astype(f32), out_bias,
+        block_output, input_gradient, proj_out.astype(f32), mixed_bias, comb_out.astype(f32), out_bias,
+        exp_out.astype(f32), hidden_bias, cont_out.astype(f32), out_bias,
         norm_sums[0], norm_sums[1], norm_sums[2], norm_sums[3],
     )
 

time: 461 us -> 456 us (0.989)
  Pallas kernels: 424 us -> 419 us
    pallas_call x1, Pallas kernels: 424 us -> 419 us  [block_passes(): pl.pallas_call(block_kernel, out_shape=[jax.ShapeDtypeStruct(s, bf16) for...]
where the time goes in v7:
time: 456 us; the launch traced here: 452 us
  Pallas kernels  419 us (92%)
  other arithmetic  25.7 us (6%)
  local copies, waits for them, and re-layouts  6.65 us (1%)
    pallas_call x1, Pallas kernels, block_passes(): pl.pallas_call(block_kernel, out_shape=[jax.ShapeDtypeStruct(s, bf16) for...  419 us

profile of v7, /device:TPU:10, one launch (start us, length us, event | category | flops | bytes accessed | tf_op | source)
XLA Modules:
  0.0 452.3 jit_solution(2767969074758032434)
XLA Ops:
  0.6 0.0 copy-start.17
  0.7 0.0 copy-start.18
  0.7 0.0 copy-start.11
  0.7 0.0 copy-start.12
  0.7 0.0 copy-start.13
  0.7 0.0 copy-start.14
  0.7 0.0 copy-start.15
  0.7 0.0 copy-start.16
  0.7 0.0 copy-start.10
  0.7 0.0 copy-start.9
  0.8 1.3 slice.52
  2.0 0.6 iota_compare_fusion
  2.7 2.3 broadcast_select_fusion.up_ref
  5.0 0.2 dynamic-update-slice
  5.2 0.2 dynamic-update-slice.1
  5.4 0.2 dynamic-update-slice.2
  5.7 0.2 dynamic-update-slice.3
  5.9 0.2 dynamic-update-slice.4
  6.1 0.2 dynamic-update-slice.5
  6.3 0.0 copy-done.10
  6.3 0.2 dynamic-update-slice.6
  6.5 0.2 dynamic-update-slice.7
  6.8 0.6 reshape.93.vec_ref
  7.4 0.0 copy-done.9
  7.4 0.6 broadcast_in_dim.42
  8.0 0.1 maximum_bitcast_fusion
  8.1 0.0 copy-done.17
  8.1 0.6 pad_maximum_fusion.angles_ref
  8.6 419.1 %shard_map.254 = (bf16[4,2,32,2048]{3,2,1,0:T(8,128)(2,1)}, bf16[4,2,128,2048]{3,2,1,0:T(8,128)(2,1)}, bf16[4,2,32,8192]{3,2,1,0:T(8,128)(2,1)}, bf16[4,2,32,614...) custom-call(bf16[256,2048]{1,0:T(8,128)(2,1)} %tok_ref.1, ...), custom_call_target="tpu_custom_call" | custom-call | tf_op jit(solution)/shard_map/pallas_call | solution.py:1293
  427.7 0.0 copy-start.2
  427.7 0.0 copy-start.6
  427.8 0.2 convert_reduce_fusion.1
  428.0 0.4 fusion.7
  428.4 0.5 copy-done.3
  428.9 0.7 convert_reduce_fusion
  429.6 0.9 slice_add_fusion
  430.6 0.0 copy-done.2
  430.6 0.0 copy-done.6
  430.6 0.0 copy-start.7
  430.6 2.4 fusion.6
  433.1 0.7 dynamic_slice.3
  433.8 0.6 slice_bitcast_fusion.1
  434.3 0.6 slice_bitcast_fusion
  434.9 6.8 %bitcast_convert_fusion = f32[1024,2048]{1,0:T(8,128)} fusion(bf16[4,2,128,2048]{3,2,1,0:T(8,128)(2,1)} %get-tuple-element.29), kind=kLoop, calls=%fused_computation | loop fusion | flops 2097152 | bytes 12582912 | tf_op jit(solution)/shard_map/convert_element_type | solution.py:1384
  441.7 4.7 %bitcast_convert_fusion.1 = f32[256,8192]{1,0:T(8,128)} fusion(bf16[4,2,32,8192]{3,2,1,0:T(8,128)(2,1)S(1)} %copy-done.1), kind=kLoop, calls=%fused_computation.1 | loop fusion | flops 2097152 | bytes 12582912 | tf_op jit(solution)/shard_map/convert_element_type | solution.py:1384
  446.4 3.7 bitcast_convert_fusion.2
  450.1 1.6 bitcast_convert_fusion.3
  451.7 0.6 copy.42
  (31 shorter events, 0.1 us)
Async XLA Ops:
  0.6 7.4 %copy-start.17 = (f32[1,128]{1,0:T(1,128)S(1)}, f32[1,128]{1,0:T(1,128)}, u32[]{:S(2)}) copy-start(f32[1,128]{1,0:T(1,128)} %constant.7.clone.1) | copy-start | bytes 1540
  0.7 5.9 %copy-start.18 = (s32[1,4]{1,0:T(1,128)S(1)}, s32[1,4]{1,0:T(1,128)}, u32[]{:S(2)}) copy-start(s32[1,4]{1,0:T(1,128)} %param.16) | copy-start | bytes 52
  0.7 4.4 copy-start.11
  0.7 4.5 %copy-start.12 = (bf16[256]{0:T(256)(128)(2,1)S(1)}, bf16[256]{0:T(256)(128)(2,1)}, u32[]{:S(2)}) copy-start(bf16[256]{0:T(256)(128)(2,1)} %param.26) | copy-start | bytes 1540
  0.7 4.7 %copy-start.13 = (bf16[256]{0:T(256)(128)(2,1)S(1)}, bf16[256]{0:T(256)(128)(2,1)}, u32[]{:S(2)}) copy-start(bf16[256]{0:T(256)(128)(2,1)} %param.27) | copy-start | bytes 1540
  0.7 4.9 %copy-start.14 = (bf16[256]{0:T(256)(128)(2,1)S(1)}, bf16[256]{0:T(256)(128)(2,1)}, u32[]{:S(2)}) copy-start(bf16[256]{0:T(256)(128)(2,1)} %param.28) | copy-start | bytes 1540
  0.7 5.2 %copy-start.15 = (bf16[256]{0:T(256)(128)(2,1)S(1)}, bf16[256]{0:T(256)(128)(2,1)}, u32[]{:S(2)}) copy-start(bf16[256]{0:T(256)(128)(2,1)} %param.20) | copy-start | bytes 1540
  0.7 5.4 %copy-start.16 = (bf16[256]{0:T(256)(128)(2,1)S(1)}, bf16[256]{0:T(256)(128)(2,1)}, u32[]{:S(2)}) copy-start(bf16[256]{0:T(256)(128)(2,1)} %param.24) | copy-start | bytes 1540
  0.7 5.6 %copy-start.10 = (bf16[768]{0:T(1024)(128)(2,1)S(1)}, bf16[768]{0:T(1024)(128)(2,1)}, u32[]{:S(2)}) copy-start(bf16[768]{0:T(1024)(128)(2,1)} %param.18) | copy-start | bytes 4612
  0.7 6.6 %copy-start.9 = (bf16[1024]{0:T(1024)(128)(2,1)S(1)}, bf16[1024]{0:T(1024)(128)(2,1)}, u32[]{:S(2)}) copy-start(bf16[1024]{0:T(1024)(128)(2,1)} %param.22) | copy-start | bytes 6148
  8.6 419.1 %copy-start = (bf16[256,2048]{1,0:T(8,128)(2,1)S(1)}, bf16[256,2048]{1,0:T(8,128)(2,1)}, u32[]{:S(2)}) copy-start(bf16[256,2048]{1,0:T(8,128)(2,1)} %tok_ref.1) | copy-start | bytes 3145732
  427.7 1.2 copy-start.3
  427.7 2.9 copy-start.2
  427.7 2.8 copy-start.6
  430.6 2.4 copy-start.7
  434.3 17.4 %copy-start.8 = (f32[256]{0:T(256)}, f32[256]{0:T(256)S(1)}, u32[]{:S(2)}) copy-start(f32[256]{0:T(256)S(1)} %get-tuple-element.64) | copy-start | bytes 3076
  434.9 6.8 %copy-start.1 = (bf16[4,2,32,8192]{3,2,1,0:T(8,128)(2,1)S(1)}, bf16[4,2,32,8192]{3,2,1,0:T(8,128)(2,1)}, u32[]{:S(2)}) copy-start(bf16[4,2,32,8192]{3,2,1,0:T(8,128)(2,1)} %get-tuple-element.28) | copy-start | bytes 12582916
  441.7 4.7 %copy-start.4 = (bf16[4,2,32,6144]{3,2,1,0:T(8,128)(2,1)S(1)}, bf16[4,2,32,6144]{3,2,1,0:T(8,128)(2,1)}, u32[]{:S(2)}) copy-start(bf16[4,2,32,6144]{3,2,1,0:T(8,128)(2,1)} %get-tuple-element.25) | copy-start | bytes 9437188
  446.4 3.7 copy-start.5

commit v8 on v7

--- a/solution.py
+++ b/solution.py
@@ -3,6 +3,7 @@
 
 import jax
 import jax.numpy as jnp
+import numpy as np
 from jax import lax
 from jax.experimental import pallas as pl
 from jax.experimental.pallas import tpu as pltpu
@@ -1327,6 +1328,55 @@
     )
 
 
+def finish_kernel(
+    ends_ref, tok_ref, cot_ref, osum_ref, dsum_ref, norms_ref, comb_ref, cont_ref, exp_ref, proj_ref,
+    out_ref, grad_ref, comb_out, cont_out, exp_out, proj_out,
+):
+    for source, target in (
+        (comb_ref, comb_out), (cont_ref, cont_out), (exp_ref, exp_out), (proj_ref, proj_out)
+    ):
+        target[...] = source[...].astype(f32)
+    count = tok_ref.shape[0]
+    row = pl.program_id(0) * count + lax.broadcasted_iota(jnp.int32, (count, 1), 0)
+    live = row < ends_ref[0, DOCS - 1]
+    floated = tok_ref[...].astype(f32)
+    added_up = osum_ref[...].astype(f32) + (norms_ref[4:5, :] + norms_ref[5:6, :])
+    out_ref[...] = (floated + jnp.where(live, added_up, 0.0)).astype(bf16)
+    normed, inverse = normalize(floated)
+    d_normed = dsum_ref[...].astype(f32)
+    grad = cot_ref[...].astype(f32) + inverse * (
+        d_normed
+        - jnp.mean(d_normed, axis=1, keepdims=True)
+        - normed * jnp.mean(d_normed * normed, axis=1, keepdims=True)
+    )
+    grad_ref[...] = grad.astype(bf16)
+
+
+def finish(ends, tokens, cotangent, osum, dsum, norms, sums):
+    steps = 2
+    thin = [tokens, cotangent, osum, dsum]
+
+    def spec(array):
+        return pl.BlockSpec((array.shape[0] // steps, array.shape[1]), lambda i, *_: (i, 0))
+
+    return pl.pallas_call(
+        finish_kernel,
+        grid_spec=pltpu.PrefetchScalarGridSpec(
+            num_scalar_prefetch=1,
+            grid=(steps,),
+            in_specs=[spec(a) for a in thin]
+            + [pl.BlockSpec(norms.shape, lambda i, *_: (0, 0))] + [spec(a) for a in sums],
+            out_specs=[spec(a) for a in [tokens, cotangent] + list(sums)],
+        ),
+        out_shape=[jax.ShapeDtypeStruct(tokens.shape, bf16)] * 2
+        + [jax.ShapeDtypeStruct(a.shape, f32) for a in sums],
+        compiler_params=pltpu.CompilerParams(vmem_limit_bytes=VMEM_LIMIT),
+        cost_estimate=pl.CostEstimate(
+            flops=20 * tokens.size, bytes_accessed=6 * sum(a.size for a in sums), transcendentals=0
+        ),
+    )(ends, *thin, norms, *sums)
+
+
 def sharded_heads(
     tokens, document_ends, projector, projbias, combiner, combbias, expander, expbias,
     contractor, contbias, attendgain, attendshift, feedgain, feedshift, cotangent,
@@ -1340,38 +1390,30 @@
     units = expbias.shape[0]
     wide = projbias.shape[0]
 
-    vectors = jnp.concatenate(
-        [attendgain, attendshift, feedgain, feedshift, combbias, contbias, projbias,
-         document_ends[0].astype(bf16)]
-    )
-    vectors = jnp.pad(vectors, (0, 16 * rows - vectors.shape[0])).reshape(16, rows)
+    parts = [attendgain, attendshift, feedgain, feedshift, combbias, contbias, projbias,
+             document_ends[0].astype(bf16)]
+    vectors, first = jnp.zeros((16 * rows,), bf16), 0
+    for part in parts:
+        last = first + part.shape[0]
+        vectors += jnp.pad(part, (first, 16 * rows - last))
+        first = last
+    vectors = vectors.reshape(16, rows)
     _, _, live = layout(document_ends[0], count)
     upstream = jnp.where(live[:, None], cotangent, jnp.zeros_like(cotangent))
     half = ROT // 2
-    freqs = jnp.exp(-jnp.arange(half, dtype=f32) * (2.0 / ROT) * math.log(10000.0))
-    still = jnp.zeros((LANES - ROT,), f32)
-    ones = jnp.ones((half,), f32)
-    angles = jnp.stack(
-        [jnp.concatenate([freqs, freqs, still]), jnp.concatenate([-ones, ones, still])]
+    freqs = np.exp(-np.arange(half) * (2.0 / ROT) * math.log(10000.0))
+    still, ones = np.zeros(LANES - ROT), np.ones(half)
+    angles = jnp.asarray(
+        np.stack([np.concatenate([freqs, freqs, still]), np.concatenate([-ones, ones, still])]), f32
     )
     comb_out, cont_out, exp_out, proj_out, osum, dsum, vec, norms = block_passes(
         tokens, vectors, upstream, expander, projector, combiner, contractor,
         expbias.astype(f32)[None], angles,
     )
 
-    floated = tokens.astype(f32)
-    block_output = floated + jnp.where(
-        live[:, None], osum.astype(f32) + (norms[4] + norms[5]), 0.0
-    )
-    block_output = block_output.astype(bf16)
-    d_normed = dsum.astype(f32)
-    normed, inverse = normalize(floated)
-    grad = cotangent.astype(f32) + inverse * (
-        d_normed
-        - jnp.mean(d_normed, axis=1, keepdims=True)
-        - normed * jnp.mean(d_normed * normed, axis=1, keepdims=True)
-    )
-    input_gradient = grad.astype(bf16)
+    block_output, input_gradient, comb_out, cont_out, exp_out, proj_out = finish(
+        document_ends, tokens, cotangent, osum, dsum, norms, (comb_out, cont_out, exp_out, proj_out)
+    )
 
     vec = vec.reshape(-1)
     norm_sums = vec[: 4 * rows].reshape(4, rows)
@@ -1380,8 +1422,8 @@
     rest = vec[4 * rows + n * mix :]
     hidden_bias, out_bias = rest[:units], rest[units : units + rows]
     return (
-        block_output, input_gradient, proj_out.astype(f32), mixed_bias, comb_out.astype(f32), out_bias,
-        exp_out.astype(f32), hidden_bias, cont_out.astype(f32), out_bias,
+        block_output, input_gradient, proj_out, mixed_bias, comb_out, out_bias,
+        exp_out, hidden_bias, cont_out, out_bias,
         norm_sums[0], norm_sums[1], norm_sums[2], norm_sums[3],
     )
 

time: 456 us -> 449 us (0.985)
  other arithmetic: 25.7 us -> 5.68 us
  Pallas kernels: 419 us -> 434 us
    convert_element_type x5 -> x0, other arithmetic: 19.2 us -> none  [the longest x1 6.8 us: sharded_heads(): cont_out.astype(f32)]
    pallas_call x0 -> x1, Pallas kernels: none -> 15.2 us  [finish(): pl.pallas_call(finish_kernel, grid_spec=pltpu.PrefetchScalarGridSpec(num_...]
where the time goes in v8:
time: 449 us; the launch traced here: 445 us
  Pallas kernels  434 us (97%)
  other arithmetic  5.68 us (1%)
    pallas_call x1, Pallas kernels, block_passes(): pl.pallas_call(block_kernel, out_shape=[jax.ShapeDtypeStruct(s, bf16) for...  419 us
    pallas_call x1, Pallas kernels, finish(): pl.pallas_call(finish_kernel, grid_spec=pltpu.PrefetchScalarGridSpec(num_...  15.2 us

profile of v8, /device:TPU:10, one launch (start us, length us, event | category | flops | bytes accessed | tf_op | source)
XLA Modules:
  0.0 444.8 jit_solution(4412904615587487889)
XLA Ops:
  0.6 1.2 slice.46
  1.9 0.6 iota_compare_fusion
  2.5 2.3 broadcast_select_fusion.up_ref
  4.9 0.7 convert_bitcast_fusion
  5.5 0.8 pad_add_fusion
  6.3 0.6 reshape.73.vec_ref
  6.9 1.3 broadcast_in_dim.21
  8.2 418.9 %shard_map.263 = (bf16[4,2,32,2048]{3,2,1,0:T(8,128)(2,1)}, bf16[4,2,128,2048]{3,2,1,0:T(8,128)(2,1)}, bf16[4,2,32,8192]{3,2,1,0:T(8,128)(2,1)}, bf16[4,2,32,614...) custom-call(bf16[256,2048]{1,0:T(8,128)(2,1)} %tok_ref.3, ...), custom_call_target="tpu_custom_call" | custom-call | tf_op jit(solution)/shard_map/pallas_call | solution.py:1294
  427.1 0.0 copy-start
  427.1 15.2 %shard_map.264 = (bf16[256,2048]{1,0:T(8,128)(2,1)}, bf16[256,2048]{1,0:T(8,128)(2,1)}, f32[256,2048]{1,0:T(8,128)}, f32[1024,2048]{1,0:T(8,128)}, f32[256,8192]{1,0:T(8,128)}, /*index=5*/f32[256,6144]{1,0:T(8,128)}) custom-call(s32[1,4]{1,0:T(1,128)} %ends_ref.1, bf16[256,2048]{1,0:T(8,128)(2,1)} %tok_ref.3, bf16[256,2048]{1,0:T(8,128)(2,1)} %cot_ref.1, ...), custom_call_target="tpu_custom_call" | custom-call | flops 10485760 | bytes 37748736 | tf_op jit(solution)/shard_map/pallas_call | solution.py:1362
  442.3 0.0 copy-done
  442.4 0.7 dynamic_slice.3
  443.1 0.6 slice_bitcast_fusion.1
  443.7 0.0 copy-start.1
  443.7 0.6 slice_bitcast_fusion
  444.3 0.6 copy.35
  444.8 0.0 copy-done.1
  (4 shorter events, 0.0 us)
Async XLA Ops:
  427.1 15.2 %copy-start = (f32[72,128]{1,0:T(8,128)S(1)}, f32[72,128]{1,0:T(8,128)}, u32[]{:S(2)}) copy-start(f32[72,128]{1,0:T(8,128)} %get-tuple-element.38) | copy-start | bytes 110596
  443.7 1.2 copy-start.1
